TPU v7x, 32 devices: a whole 2x2x4 slice. The times are simulated.
32 devices in a mesh: seq: 8 (over z, y), mp: 4 (over x, core).
Axes of the slice: x: 2, y: 2, z: 4, core: 2. Of those that a mesh axis runs over, the one named last changes fastest.
Arguments:
- hidden: bfloat16 [4, 4096, 8192], P(None, 'seq', 'mp'), may hold values from -1000 to 1000
- norm_gain: bfloat16 [4, 8192], P(None, 'mp'), may hold values from 0.25 to 1.75
- proj_weight: bfloat16 [4, 8192, 1024], P(None, 'mp'), may hold values from -0.0625 to 0.0625
- start_block: bfloat16 [8, 512, 128], replicated, may hold values from -6 to 6
Outputs:
- latents: bfloat16 [4096, 8, 128], P('seq', 'mp')
All inputs are finite; a program needn't handle non-finite values.
Results may differ from a plain program's by a relative error of at most 0.025.
Values may be sent and summed in bfloat16 or wider, within the bound.
No kernel may reach another device: no remote copies, remote signals or barrier semaphores. Data moves between devices by JAX's collectives and lax.ppermute only.
A program may use at most 64 MiB of HBM per device.

v0:
```python
import jax
import jax.numpy as jnp
from jax import lax
from jax.sharding import PartitionSpec as P

D = 8192
HD = 128
ITERS = 2


epsilon = 1e-05
highest_precision = lax.Precision.HIGHEST


def orthonormal_basis(image_block):
    inner_block = jnp.einsum("sar,saq->srq", image_block, image_block, precision=highest_precision)
    lower_factor = jnp.linalg.cholesky(inner_block)
    solved = jax.scipy.linalg.solve_triangular(
        lower_factor, jnp.swapaxes(image_block, 1, 2), lower=True
    )
    return jnp.swapaxes(solved, 1, 2)


def on_device(hidden, norm_gain, proj_weight, start_block):
    layer_count, token_count, width_here = hidden.shape
    mp_count = lax.axis_size("mp")
    count_of_streams = proj_weight.shape[2] // HD
    own_streams = count_of_streams // mp_count
    squares = jnp.sum(jnp.square(hidden.astype(jnp.float32)), axis=2)
    totals = lax.psum(squares, "mp")
    factor = lax.rsqrt(totals / D + epsilon)
    normed = (
        hidden.astype(jnp.float32) * factor[:, :, None] * norm_gain.astype(jnp.float32)[:, None, :]
    ).astype(jnp.bfloat16)
    weight_matrices = proj_weight.reshape(layer_count, width_here, count_of_streams, HD)
    reduced = lax.psum_scatter(
        jnp.einsum(
            "ltw,lwsh->slth", normed, weight_matrices, preferred_element_type=jnp.float32
        ).astype(jnp.bfloat16),
        "mp",
        scatter_dimension=0,
        tiled=True,
    )
    stacked = reduced.transpose(0, 2, 1, 3).reshape(own_streams, token_count, layer_count * HD)
    block_of_basis = lax.dynamic_slice_in_dim(
        start_block, lax.axis_index("mp") * own_streams, own_streams, 0
    ).astype(jnp.float32)
    partial_gram = jnp.einsum("sta,stb->sab", stacked, stacked, preferred_element_type=jnp.float32)
    total_gram_matrix = lax.psum(partial_gram.astype(jnp.bfloat16), "seq").astype(jnp.float32)
    for repeat in range(ITERS):
        block_of_basis = orthonormal_basis(
            jnp.einsum(
                "zcv,zvt->zct", total_gram_matrix, block_of_basis, precision=highest_precision
            )
        )
    basis_half = block_of_basis.astype(jnp.bfloat16)
    return jnp.einsum(
        "sta,sar->tsr", stacked, basis_half, preferred_element_type=jnp.float32
    ).astype(jnp.bfloat16)


def solution(mesh):
    return jax.shard_map(
        on_device,
        mesh=mesh,
        in_specs=(P(None, "seq", "mp"), P(None, "mp"), P(None, "mp", None), P()),
        out_specs=P("seq", "mp", None),
        check_vma=False,
    )
```

profile of v0, /device:TPU:0, one launch (start us, length us, event | category | flops | bytes accessed | tf_op | source)
XLA Modules:
  0.0 308.0 jit_solution(11197083132615537288)
XLA Ops:
  6.5 0.0 copy-start
  6.5 0.0 all-reduce.6.cloned.1.call-start
  6.5 0.8 convert_element_type.32
  7.4 5.1 %fusion = f32[4,512]{1,0:T(4,128)S(1)} fusion(bf16[4,512,2048]{2,1,0:T(8,128)(2,1)} %param.7), kind=kLoop, calls=%fused_computation.2 | loop fusion | flops 12580864 | bytes 8396800 | tf_op jit(solution)/shard_map/reduce_sum | solution.py:29
  12.4 8.5 %psum.14 = f32[4,512]{1,0:T(4,128)S(1)} all-reduce(f32[4,512]{1,0:T(4,128)S(1)} %fusion), channel_id=1, replica_groups=mesh['seq'=8,'mp'=4] {'mp'}, use_global_device_ids=true, to_apply=%region_1.0 | all-reduce | flops 2048 | bytes 16384 | tf_op jit(solution)/shard_map/psum | solution.py:30
  21.0 0.0 copy-start.1
  21.0 16.4 %convert_bitcast_fusion = bf16[8,4,512,128]{3,2,0,1:T(8,128)(2,1)} fusion(bf16[4,512,2048]{2,1,0:T(8,128)(2,1)} %param.7, f32[4,2048]{1,0:T(4,128)S(1)} %convert_element_type.32, f32[4,512]{1,0:T(4,128)S(1)} %add_rsqrt_fusion, bf16[4,2048,1024]{2,1,0:T(8,128)(2,1)} %param.9), kind=kOutput, calls=%fused_computation.11 | convolution fusion | flops 8608808960 | bytes 29401088 | tf_op jit(solution)/shard_map/ltw,lwsh->slth/dot_general | solution.py:37
  37.4 0.0 all-reduce.6.cloned.1.call-update
  37.4 0.2 all-reduce.4.cloned.1.call-start
  37.6 0.0 copy-done.1
  37.6 0.6 dynamic-slice
  38.9 84.5 %all-reduce.6.cloned.1.call-done = bf16[8,4,512,128]{3,2,0,1:T(8,128)(2,1)} async-done(((bf16[8,4,512,128]{3,2,0,1:T(8,128)(2,1)}), bf16[8,4,512,128]{3,2,0,1:T(8,128)(2,1)}) %all-reduce.6.cloned.1.call-update) | async-done | bytes 4194320
  123.4 1.3 constant_dynamic-slice_fusion
  124.7 0.5 copy.35
  125.2 1.8 convolution_convert_fusion
  127.0 0.0 all-reduce.4.cloned.1.call-update
  127.1 78.4 %all-reduce.4.cloned.1.call-done = bf16[2,512,512]{2,1,0:T(8,128)(2,1)} async-done(((bf16[2,512,512]{2,1,0:T(8,128)(2,1)}), bf16[2,512,512]{2,1,0:T(8,128)(2,1)}) %all-reduce.4.cloned.1.call-update) | async-done | bytes 1048592 | tf_op jit(solution)/shard_map/psum | solution.py:49
  205.5 0.0 copy-done
  205.5 1.7 fusion.18
  207.1 1.0 fusion.25
  208.2 0.1 copy.38
  208.3 23.5 %custom-call.8 = f32[2,128,128]{2,1,0:T(8,128)S(1)} custom-call(f32[2,128,128]{2,1,0:T(8,128)S(1)} %fusion.23), custom_call_target="Cholesky" | custom-call | tf_op jit(solution)/shard_map/jit(cholesky)/cholesky | solution.py:17
  231.8 0.1 compare_reduce_fusion.1
  231.9 0.1 select_bitcast_fusion.1
  232.0 19.7 %custom-call.9 = f32[2,1,128,128]{2,3,1,0:T(8,128)S(1)} custom-call(f32[2,1,128,128]{3,2,1,0:T(8,128)S(1)} %select_bitcast_fusion.1), custom_call_target="InvertDiagBlocksLowerTriangular" | custom-call | tf_op jit(solution)/shard_map/jit(_solve_triangular)/vmap()/triangular_solve | solution.py:18
  251.7 0.6 fusion.16
  252.3 2.2 fusion.26
  254.6 1.0 fusion.27
  255.6 0.1 copy.42
  255.7 23.7 %custom-call.10 = f32[2,128,128]{2,1,0:T(8,128)S(1)} custom-call(f32[2,128,128]{2,1,0:T(8,128)S(1)} %fusion.21), custom_call_target="Cholesky" | custom-call | tf_op jit(solution)/shard_map/jit(cholesky)/cholesky | solution.py:17
  279.4 0.1 compare_reduce_fusion
  279.5 0.1 select_bitcast_fusion
  279.6 19.7 %custom-call.11 = f32[2,1,128,128]{2,3,1,0:T(8,128)S(1)} custom-call(f32[2,1,128,128]{3,2,1,0:T(8,128)S(1)} %select_bitcast_fusion), custom_call_target="InvertDiagBlocksLowerTriangular" | custom-call | tf_op jit(solution)/shard_map/jit(_solve_triangular)/vmap()/triangular_solve | solution.py:18
  299.3 0.6 convolution_convert_fusion.2
  300.0 0.3 fusion.14
  300.3 0.9 copy.46
  (7 shorter events, 0.1 us)
Async XLA Ops:
  6.5 198.9 %copy-start = (bf16[8,512,128]{2,1,0:T(8,128)(2,1)S(1)}, bf16[8,512,128]{2,1,0:T(8,128)(2,1)}, u32[]{:S(2)}) copy-start(bf16[8,512,128]{2,1,0:T(8,128)(2,1)} %param.10) | copy-start | bytes 3145732
  6.5 116.9 %all-reduce.6.cloned.1.call-start = ((), (), s32[]{:S(2)}) async-start(), calls=%async_computation.1 | async-start | bytes 8388608
  21.0 16.7 %copy-start.1 = (u32[32]{0:T(128)S(1)}, u32[32]{0:T(128)}, u32[]{:S(2)}) copy-start(u32[32]{0:T(128)} %constant.51) | copy-start | bytes 388
  37.4 168.1 %all-reduce.4.cloned.1.call-start = ((), (), s32[]{:S(2)}) async-start(), calls=%async_computation | async-start | bytes 2097152 | tf_op jit(solution)/shard_map/psum | solution.py:49
Sparse Core Ops, SparseCore 0:
  37.5 85.8 all-reduce.5
  127.3 78.1 all-reduce.3
where the time goes:
time: 308 us
  waiting for transfers between devices  163 us (53%)
  other arithmetic  93 us (30%)
  matrix products  25.7 us (8%)
  between operations  14.2 us (5%)
  blocking collectives  8.49 us (3%)
  local copies, waits for them, and re-layouts  3.48 us (1%)
    unnamed x3, waiting for transfers between devices  84.6 us
    psum x1, waiting for transfers between devices, on_device(): lax.psum(partial_gram.astype(jnp.bfloat16), 'seq').astype(jnp.float32)  78.4 us
    another operation x7, other arithmetic, orthonormal_basis(): lower_factor = jnp.linalg.cholesky(inner_block)  47.5 us
    another operation x5, other arithmetic, orthonormal_basis(): jax.scipy.linalg.solve_triangular(lower_factor, jnp.swapaxes(image_block,...  39.6 us
    dot_general x1, matrix products, on_device(): jnp.einsum('ltw,lwsh->slth', normed, weight_matrices, preferred_element_t...  16.4 us
    psum x1, blocking collectives, on_device(): totals = lax.psum(squares, 'mp')  8.49 us
  transfers between devices with their start and end apart: 2, of which 2 were waited for; matrix products, arithmetic and copies ran while one was open for 0% of the time, Pallas kernels for 0%

commit v1 on v0

v1 whole, which is shorter than its diff:
```python
import functools

import jax
import jax.numpy as jnp
from jax import lax
from jax.experimental import pallas as pl
from jax.experimental.pallas import tpu as pltpu
from jax.sharding import PartitionSpec as P

HD = 128
ITERS = 2
EPSILON = 1e-05
F32 = jnp.float32
BF16 = jnp.bfloat16
HIGHEST = lax.Precision.HIGHEST
MIB = 1 << 20


def halving_order(count):
    bits = count.bit_length() - 1
    return sorted(range(count), key=lambda r: int(format(r, f"0{bits}b")[::-1], 2)) if bits else [0]


def exchange(x, axis, bit):
    size = lax.axis_size(axis)
    return lax.ppermute(x, axis, [(j, j ^ bit) for j in range(size)])


def partial_kernel(first, steps, count, with_squares, m_ref, hid_ref, gain_ref, *refs):
    w_refs, refs = refs[:count], refs[count:]
    keep_ref, send_ref = refs[:2]
    sq_ref = refs[2] if with_squares else None
    acc_ref, sqacc_ref = refs[-2:]
    layer, k = pl.program_id(0), pl.program_id(1)
    gains = gain_ref[...].astype(F32)
    which = lax.broadcasted_iota(jnp.int32, gains.shape, 0)
    gain = jnp.sum(jnp.where(which == first + layer, gains, 0.0), axis=0, keepdims=True)
    rows = hid_ref[0].astype(F32)
    weights = jnp.concatenate([w[0] for w in w_refs], axis=1)
    product = jnp.dot((rows * gain).astype(BF16), weights, preferred_element_type=F32)

    @pl.when(k == 0)
    def _():
        acc_ref[...] = product

    @pl.when(k > 0)
    def _():
        acc_ref[...] += product

    if with_squares:
        square = rows * rows
        part = sum(square[:, i * 128 : (i + 1) * 128] for i in range(square.shape[1] // 128))

        @pl.when(k == 0)
        def _():
            sqacc_ref[...] = part

        @pl.when(k > 0)
        def _():
            sqacc_ref[...] += part

    @pl.when(k == steps - 1)
    def _():
        half = acc_ref.shape[1] // 2
        keep_ref[0] = acc_ref[:, :half].astype(BF16)
        send_ref[0] = acc_ref[:, half:].astype(BF16)
        if with_squares:
            sq_ref[0] = lax.dot_general(
                jnp.ones((8, 128), F32),
                sqacc_ref[...],
                (((1,), (1,)), ((), ())),
                precision=HIGHEST,
                preferred_element_type=F32,
            )


def partial_products(hidden, gains, weights, me, slot, layers, own, with_squares):
    _, tokens, width = hidden.shape
    mp = lax.axis_size("mp")
    order = halving_order(mp)
    block = min(width, 512)
    steps = width // block
    first, count = layers[0], len(layers)
    half = mp // 2 * HD

    def columns(r):
        return lambda layer, k, m: (first + layer, k, own * (m[0] ^ r) + slot)

    outs = [jax.ShapeDtypeStruct((count, tokens, half), BF16)] * 2
    out_specs = [pl.BlockSpec((1, tokens, half), lambda layer, k, m: (layer, 0, 0))] * 2
    if with_squares:
        outs.append(jax.ShapeDtypeStruct((count, 8, tokens), F32))
        out_specs.append(pl.BlockSpec((1, 8, tokens), lambda layer, k, m: (layer, 0, 0)))
    return pl.pallas_call(
        functools.partial(partial_kernel, first, steps, mp, with_squares),
        out_shape=outs,
        grid_spec=pltpu.PrefetchScalarGridSpec(
            num_scalar_prefetch=1,
            grid=(count, steps),
            in_specs=[
                pl.BlockSpec((1, tokens, block), lambda layer, k, m: (first + layer, 0, k)),
                pl.BlockSpec((hidden.shape[0], block), lambda layer, k, m: (0, k)),
            ]
            + [pl.BlockSpec((1, block, HD), columns(r)) for r in order],
            out_specs=out_specs,
            scratch_shapes=[
                pltpu.VMEM((tokens, mp * HD), F32),
                pltpu.VMEM((tokens, 128), F32),
            ],
        ),
        compiler_params=pltpu.CompilerParams(vmem_limit_bytes=24 * MIB),
        cost_estimate=pl.CostEstimate(
            flops=2 * count * tokens * width * mp * HD,
            bytes_accessed=count * width * (tokens + mp * HD) * 2,
            transcendentals=0,
        ),
        name=f"partial_s{slot}_l{first}",
    )(me, hidden, gains, *([weights] * mp))


def gram_kernel(shapes, width, squares_ref, *refs):
    stacked_ref, gram_ref = refs[-2:]
    refs = refs[:-2]
    layers = squares_ref.shape[0]
    factor = lax.rsqrt(squares_ref[...] / width + EPSILON)
    factor = jnp.transpose(factor.reshape(layers * 8, -1))
    at, blocks = 0, []
    for count, parts in shapes:
        for i in range(count):
            total = sum(refs[at + j][i].astype(F32) for j in range(parts))
            layer = len(blocks)
            blocks.append((total * factor[:, 8 * layer : 8 * layer + 1]).astype(BF16))
        at += parts
    stacked = jnp.concatenate(blocks, axis=1)
    stacked_ref[...] = stacked
    column = 0
    for i, block in enumerate(blocks):
        upto = (i + 1) * HD
        gram_ref[:, column : column + upto] = lax.dot_general(
            block, stacked[:, :upto], (((0,), (0,)), ((), ())), preferred_element_type=F32
        ).astype(BF16)
        column += upto


def stacked_and_gram(contributions, squares, width):
    layers, _, tokens = squares.shape
    shapes = [(parts[0].shape[0], len(parts)) for parts in contributions]
    arrays = [a for parts in contributions for a in parts]
    packed = layers * (layers + 1) // 2 * HD
    return pl.pallas_call(
        functools.partial(gram_kernel, shapes, width),
        out_shape=[
            jax.ShapeDtypeStruct((tokens, layers * HD), BF16),
            jax.ShapeDtypeStruct((HD, packed), BF16),
        ],
        grid=(1,),
        in_specs=[pl.BlockSpec(squares.shape, lambda i: (0, 0, 0))]
        + [pl.BlockSpec((a.shape[0], tokens, HD), lambda i: (0, 0, 0)) for a in arrays],
        out_specs=[
            pl.BlockSpec((tokens, layers * HD), lambda i: (0, 0)),
            pl.BlockSpec((HD, packed), lambda i: (0, 0)),
        ],
        compiler_params=pltpu.CompilerParams(vmem_limit_bytes=24 * MIB),
        name="stacked_gram",
    )(squares, *arrays)


def sum_over_seq(x):
    size = lax.axis_size("seq")
    me = lax.axis_index("seq")
    bits = [1 << i for i in range(size.bit_length() - 1)]
    for bit in bits[:-1]:
        half = x.shape[0] // 2
        mine = jnp.where((me & bit) != 0, half, 0)
        got = exchange(lax.dynamic_slice_in_dim(x, half - mine, half, 0).astype(BF16), "seq", bit)
        x = lax.dynamic_slice_in_dim(x, mine, half, 0).astype(F32) + got.astype(F32)
    x = x.astype(BF16)
    x = (x.astype(F32) + exchange(x, "seq", bits[-1]).astype(F32)).astype(BF16)
    for bit in bits[:-1][::-1]:
        got = exchange(x, "seq", bit)
        upper = (me & bit) != 0
        x = jnp.concatenate([jnp.where(upper, got, x), jnp.where(upper, x, got)], axis=0)
    return x


def split3(x):
    high = x.astype(BF16)
    rest = x - high.astype(F32)
    middle = rest.astype(BF16)
    return high, middle, (rest - middle.astype(F32)).astype(BF16)


def rank_update(x):
    h, m, l = split3(x)
    left = jnp.concatenate([h, h, m, h, m, l], axis=0)
    right = jnp.concatenate([h, m, h, l, m, h], axis=0)
    return lax.dot_general(left, right, (((0,), (0,)), ((), ())), preferred_element_type=F32)


def reciprocal(d):
    r = pl.reciprocal(d, approx=True)
    return r * (2.0 - d * r)


def factor_panel(rows, base):
    b, n = rows.shape
    lane = lax.broadcasted_iota(jnp.int32, (b, n), 1)
    row = lax.broadcasted_iota(jnp.int32, (b, n), 0)
    columns = [jnp.broadcast_to(rows[:, base + j : base + j + 1], (b, n)) for j in range(b)]
    pivots = jnp.zeros((b, n), F32)
    for k in range(b):
        pivot = jnp.broadcast_to(columns[k][k : k + 1, :], (b, n))
        pivots = jnp.where(row == k, pivot, pivots)
        here = lane == base + k
        rows = jnp.where(here & (row >= k), jnp.where(row == k, 1.0, 0.0), rows)
        if k < b - 1:
            multiplier = jnp.where(row > k, columns[k] * reciprocal(pivot), 0.0)
            rows = rows - multiplier * jnp.broadcast_to(rows[k : k + 1, :], (b, n))
            for j in range(k + 1, b):
                columns[j] = columns[j] - multiplier * jnp.broadcast_to(columns[j][k : k + 1, :], (b, n))
    rows = jnp.where((lane > base + row) & (lane < base + b), 0.0, rows)
    return rows * lax.rsqrt(pivots)


def inverse_cholesky(matrices, b=16):
    n = matrices[0].shape[0]
    panels = [[] for _ in matrices]
    rests = list(matrices)
    lane = lax.broadcasted_iota(jnp.int32, (n, n), 1)
    row = lax.broadcasted_iota(jnp.int32, (n, n), 0)
    for base in range(0, n, b):
        for s, rest in enumerate(rests):
            panels[s].append(factor_panel(rest[:b], base))
        if base + b < n:
            for s, rest in enumerate(rests):
                update = rank_update(panels[s][-1])[base + b :]
                rest = rest[b:]
                at = lane[: rest.shape[0]]
                rests[s] = jnp.where((at >= base) & (at < base + b), 0.0, rest) - update
    return [jnp.where(lane <= row, jnp.concatenate(p, axis=0), 0.0) for p in panels]


def basis_kernel(own, layers, m_ref, start_ref, *refs):
    gram_refs, stacked_refs, out_ref = refs[:own], refs[own : 2 * own], refs[2 * own]
    grams = []
    for ref in gram_refs:
        block = {}
        column = 0
        for i in range(layers):
            for j in range(i + 1):
                block[i, j] = ref[:, column : column + HD]
                column += HD
        rows = []
        for i in range(layers):
            rows.append(
                jnp.concatenate(
                    [
                        block[i, j] if j <= i else jnp.transpose(block[j, i].astype(F32)).astype(BF16)
                        for j in range(layers)
                    ],
                    axis=1,
                )
            )
        grams.append(jnp.concatenate(rows, axis=0))
    rank = start_ref.shape[2]
    images = [jnp.dot(grams[s], start_ref[s], preferred_element_type=F32) for s in range(own)]
    for step in range(ITERS):
        if step:
            images = [
                jnp.dot(grams[s], jnp.concatenate(split3(images[s]), axis=1), preferred_element_type=F32)
                for s in range(own)
            ]
            images = [x[:, :rank] + x[:, rank : 2 * rank] + x[:, 2 * rank :] for x in images]
        inner = [
            lax.dot_general(x, x, (((0,), (0,)), ((), ())), precision=HIGHEST, preferred_element_type=F32)
            for x in images
        ]
        inverse = inverse_cholesky(inner)
        images = [
            lax.dot_general(x, f, (((1,), (1,)), ((), ())), precision=HIGHEST, preferred_element_type=F32)
            for x, f in zip(images, inverse)
        ]
    for s in range(own):
        out_ref[:, s * HD : (s + 1) * HD] = jnp.dot(
            stacked_refs[s][...], images[s].astype(BF16), preferred_element_type=F32
        ).astype(BF16)


def latents_of(start, grams, stacked, me):
    own = len(grams)
    tokens = stacked[0].shape[0]
    layers = stacked[0].shape[1] // HD
    whole = lambda a: pl.BlockSpec(a.shape, lambda i, m: (0, 0))
    return pl.pallas_call(
        functools.partial(basis_kernel, own, layers),
        out_shape=jax.ShapeDtypeStruct((tokens, own * HD), BF16),
        grid_spec=pltpu.PrefetchScalarGridSpec(
            num_scalar_prefetch=1,
            grid=(1,),
            in_specs=[pl.BlockSpec((own,) + start.shape[1:], lambda i, m: (m[0], 0, 0))]
            + [whole(a) for a in grams + stacked],
            out_specs=pl.BlockSpec((tokens, own * HD), lambda i, m: (0, 0)),
        ),
        compiler_params=pltpu.CompilerParams(vmem_limit_bytes=40 * MIB),
        name="basis_latents",
    )(me, start, *grams, *stacked).reshape(tokens, own, HD)


def groups_of(slot, layers, own):
    if slot + 1 < own:
        return [[0], [1], list(range(2, layers))]
    return [list(range(0, layers - 1)), [layers - 1]]


def on_device(hidden, norm_gain, proj_weight, start_block):
    layers, tokens, width = hidden.shape
    mp = lax.axis_size("mp")
    own = proj_weight.shape[2] // HD // mp
    me = lax.axis_index("mp").astype(jnp.int32).reshape(1)
    mp_bits = [1 << i for i in range(mp.bit_length() - 1)]

    squares, pieces = [], [[] for _ in range(own)]
    for slot in range(own):
        for group in groups_of(slot, layers, own):
            outs = partial_products(hidden, norm_gain, proj_weight, me, slot, group, own, slot == 0)
            if slot == 0:
                squares.append(outs[2])
            contributions = [outs[0]]
            for bit in mp_bits:
                if bit == 1:
                    send = outs[1]
                else:
                    half = contributions[-1].shape[2] // 2
                    send = sum(c[:, :, half : 2 * half].astype(F32) for c in contributions).astype(BF16)
                contributions.append(exchange(send, "mp", bit))
            pieces[slot].append(contributions)
        if slot == 0:
            totals = jnp.concatenate(squares, axis=0)
            for bit in mp_bits:
                totals = totals + exchange(totals, "mp", bit)

    grams, stacked = [], []
    for slot in range(own):
        rows, gram = stacked_and_gram(pieces[slot], totals, width * mp)
        stacked.append(rows)
        grams.append(sum_over_seq(gram))
    return latents_of(start_block, grams, stacked, me)


def solution(mesh):
    return jax.shard_map(
        on_device,
        mesh=mesh,
        in_specs=(P(None, "seq", "mp"), P(None, "mp"), P(None, "mp", None), P()),
        out_specs=P("seq", "mp", None),
        check_vma=False,
    )
```

time: 308 us -> 120 us (0.39)
  waiting for transfers between devices: 163 us -> 31.2 us
  other arithmetic: 93 us -> 2.71 us
  Pallas kernels: 0 us -> 47 us
  matrix products: 25.7 us -> 0 us
  starting transfers between devices: 0.22 us -> 23.6 us
  between operations: 14.2 us -> 0.2 us
  local copies, waits for them, and re-layouts: 3.48 us -> 14.9 us
  blocking collectives: 8.49 us -> 0 us
    another operation x12 -> x0, other arithmetic: 87 us -> none  [the longest x7 47.5 us: orthonormal_basis(): lower_factor = jnp.linalg.cholesky(inner_block)]
    unnamed x3 -> x0, waiting for transfers between devices: 84.6 us -> none
    psum x1 -> x0, waiting for transfers between devices: 78.4 us -> none  [on_device(): lax.psum(partial_gram.astype(jnp.bfloat16), 'seq').astype(jnp.float32)]
    pallas_call x0 -> x8, Pallas kernels: none -> 47 us  [the longest x5 31.5 us: partial_products(): pl.pallas_call(functools.partial(partial_kernel, first, steps, mp, with_s...]
    ppermute x0 -> x22, waiting for transfers between devices: none -> 31.2 us  [exchange(): return lax.ppermute(x, axis, [(j, j ^ bit) for j in range(size)])]
    dot_general x7 -> x0, matrix products: 24.4 us -> none  [the longest x1 16.4 us: on_device(): jnp.einsum('ltw,lwsh->slth', normed, weight_matrices, preferred_element_t...]
    ppermute x0 -> x22, starting transfers between devices: none -> 23.6 us  [exchange(): return lax.ppermute(x, axis, [(j, j ^ bit) for j in range(size)])]
    unnamed x6 -> x22, local copies, waits for them, and re-layouts: 1.89 us -> 14.1 us
  transfers between devices with their start and end apart: 2 -> 22, of which waited for: 2 -> 10; matrix products, arithmetic and copies ran while one was open for 0% -> 2% of each run, Pallas kernels for 0% -> 13%
where the time goes in v1:
time: 120 us
  Pallas kernels  47 us (39%)
  waiting for transfers between devices  31.2 us (26%)
  starting transfers between devices  23.6 us (20%)
  local copies, waits for them, and re-layouts  14.9 us (12%)
  other arithmetic  2.71 us (2%)
    pallas_call x5, Pallas kernels, partial_products(): pl.pallas_call(functools.partial(partial_kernel, first, steps, mp, with_s...  31.5 us
    ppermute x22, waiting for transfers between devices, exchange(): return lax.ppermute(x, axis, [(j, j ^ bit) for j in range(size)])  31.2 us
    ppermute x22, starting transfers between devices, exchange(): return lax.ppermute(x, axis, [(j, j ^ bit) for j in range(size)])  23.6 us
    unnamed x22, local copies, waits for them, and re-layouts  14.1 us
    pallas_call x1, Pallas kernels, latents_of(): pl.pallas_call(functools.partial(basis_kernel, own, layers), out_shape=ja...  12.7 us
    pallas_call x2, Pallas kernels, stacked_and_gram(): pl.pallas_call(functools.partial(gram_kernel, shapes, width), out_shape=[...  2.72 us
  transfers between devices with their start and end apart: 22, of which 10 were waited for; matrix products, arithmetic and copies ran while one was open for 2% of the time, Pallas kernels for 13%

profile of v1, /device:TPU:0, one launch (start us, length us, event | category | flops | bytes accessed | tf_op | source)
XLA Modules:
  0.0 119.7 jit_solution(5914496307859004379)
XLA Ops:
  0.0 5.8 %copy-done = bf16[4,2048,1024]{2,1,0:T(8,128)(2,1)S(1)} copy-done((bf16[4,2048,1024]{2,1,0:T(8,128)(2,1)S(1)}, bf16[4,2048,1024]{2,1,0:T(8,128)(2,1)}, u32[]{:S(2)}) %copy-start) | copy-done | bytes 16777240
  5.8 3.4 %copy-done.1 = bf16[4,512,2048]{2,1,0:T(8,128)(2,1)S(1)} copy-done((bf16[4,512,2048]{2,1,0:T(8,128)(2,1)S(1)}, bf16[4,512,2048]{2,1,0:T(8,128)(2,1)}, u32[]{:S(2)}) %copy-start.1) | copy-done | bytes 8388632
  9.2 0.7 copy-done.7
  9.9 4.7 %partial_s0_l1.1 = (bf16[1,512,256]{2,1,0:T(8,128)(2,1)S(1)}, bf16[1,512,256]{2,1,0:T(8,128)(2,1)}, f32[1,8,512]{2,1,0:T(8,128)S(1)}) custom-call(s32[1]{0:T(128)} %bitcast.m_ref, bf16[4,512,2048]{2,1,0:T(8,128)(2,1)S(1)} %copy-done.1, bf16[4,2048]{1,0:T(4,128)(2,1)S(1)} %copy-done.7, bf16[4,2048,1024]{2,1,0:T(8,128)(2,1)S(1)} %copy-done, ...), custom_call_target="tpu_custom_call" | custom-call | flops 1073741824 | bytes 4194304 | tf_op jit(solution)/shard_map/partial_s0_l1/pallas_call | solution.py:94
  14.6 0.7 copy-done.3
  15.3 4.7 %partial_s0_l0.1 = (bf16[1,512,256]{2,1,0:T(8,128)(2,1)S(1)}, bf16[1,512,256]{2,1,0:T(8,128)(2,1)}, f32[1,8,512]{2,1,0:T(8,128)S(1)}) custom-call(s32[1]{0:T(128)} %bitcast.m_ref, bf16[4,512,2048]{2,1,0:T(8,128)(2,1)S(1)} %copy-done.1, bf16[4,2048]{1,0:T(4,128)(2,1)S(1)} %copy-done.7, bf16[4,2048,1024]{2,1,0:T(8,128)(2,1)S(1)} %copy-done, ...), custom_call_target="tpu_custom_call" | custom-call | flops 1073741824 | bytes 4194304 | tf_op jit(solution)/shard_map/partial_s0_l0/pallas_call | solution.py:94
  19.9 0.7 copy-done.5
  20.6 8.9 %partial_s0_l2.1 = (bf16[2,512,256]{2,1,0:T(8,128)(2,1)S(1)}, bf16[2,512,256]{2,1,0:T(8,128)(2,1)}, f32[2,8,512]{2,1,0:T(8,128)S(1)}) custom-call(s32[1]{0:T(128)} %bitcast.m_ref, bf16[4,512,2048]{2,1,0:T(8,128)(2,1)S(1)} %copy-done.1, bf16[4,2048]{1,0:T(4,128)(2,1)S(1)} %copy-done.8, bf16[4,2048,1024]{2,1,0:T(8,128)(2,1)S(1)} %copy-done, ...), custom_call_target="tpu_custom_call" | custom-call | flops 2147483648 | bytes 8388608 | tf_op jit(solution)/shard_map/partial_s0_l2/pallas_call | solution.py:94
  29.5 0.5 collective-permute-start
  30.0 3.8 %partial_s1_l3.1 = (bf16[1,512,256]{2,1,0:T(8,128)(2,1)S(1)}, bf16[1,512,256]{2,1,0:T(8,128)(2,1)}) custom-call(s32[1]{0:T(128)} %bitcast.m_ref, bf16[4,512,2048]{2,1,0:T(8,128)(2,1)S(1)} %copy-done.1, bf16[4,2048]{1,0:T(4,128)(2,1)S(1)} %copy-done.8, bf16[4,2048,1024]{2,1,0:T(8,128)(2,1)S(1)} %copy-done, bf16[4,2048,1024]{2,1,0:T(8,128)(2,1)S(1)} %copy-done, ...), custom_call_target="tpu_custom_call" | custom-call | flops 1073741824 | bytes 4194304 | tf_op jit(solution)/shard_map/partial_s1_l3/pallas_call | solution.py:94
  33.9 0.5 collective-permute-start.4
  34.4 0.5 collective-permute-start.6
  34.9 2.6 %collective-permute-start.1 = (f32[4,8,512]{2,1,0:T(8,128)S(1)}, f32[4,8,512]{2,1,0:T(8,128)S(1)}, u32[]{:S(2)}, u32[]{:S(2)}) collective-permute-start(f32[4,8,512]{2,1,0:T(8,128)S(1)} %add.53), channel_id=1, source_target_pairs={{0,2},{1,3},{2,0},{3,1},{4,6},{5,7},{6,4},{7,5},{8,10},{9,11},{10,... | collective-permute-start | bytes 196616 | tf_op jit(solution)/shard_map/ppermute | solution.py:26
  37.5 9.5 %partial_s1_l0.1 = (bf16[3,512,256]{2,1,0:T(8,128)(2,1)S(1)}, bf16[3,512,256]{2,1,0:T(8,128)(2,1)S(1)}) custom-call(s32[1]{0:T(128)} %bitcast.m_ref, bf16[4,512,2048]{2,1,0:T(8,128)(2,1)S(1)} %copy-done.1, bf16[4,2048]{1,0:T(4,128)(2,1)S(1)} %copy-done.8, bf16[4,2048,1024]{2,1,0:T(8,128)(2,1)S(1)} %copy-done, bf16[4,2048,1024]{2,1,0:T(8,128)(2,1)S(1)} %copy-done, ...), custom_call_target="tpu_custom_call" | custom-call | flops 3221225472 | bytes 12582912 | tf_op jit(solution)/shard_map/partial_s1_l0/pallas_call | solution.py:94
  47.0 0.9 copy-done.9
  48.1 1.1 add_convert_fusion.3
  49.2 0.3 collective-permute-start.5
  49.6 1.9 %collective-permute-start.7 = (bf16[2,512,128]{2,1,0:T(8,128)(2,1)S(1)}, bf16[2,512,128]{2,1,0:T(8,128)(2,1)S(1)}, u32[]{:S(2)}, u32[]{:S(2)}) collective-permute-start(bf16[2,512,128]{2,1,0:T(8,128)(2,1)S(1)} %add_convert_fusion.1), channel_id=1, source_target_pairs={{0,2},{1,3},{2,0},{3,1},{4,6},{5,7},{6,4},{7,5},{8,10},{9,11},{10,... | collective-permute-start | bytes 786440 | tf_op jit(solution)/shard_map/ppermute | solution.py:26
  51.4 1.0 add_convert_fusion.4
  52.5 0.3 collective-permute-start.3
  52.8 1.9 %collective-permute-start.16 = (bf16[1,512,128]{2,1,0:T(8,128)(2,1)S(1)}, bf16[1,512,128]{2,1,0:T(8,128)(2,1)S(1)}, u32[]{:S(2)}, u32[]{:S(2)}) collective-permute-start(bf16[1,512,128]{2,1,0:T(8,128)(2,1)S(1)} %add_convert_fusion.2), channel_id=1, source_target_pairs={{0,2},{1,3},{2,0},{3,1},{4,6},{5,7},{6,4},{7,5},{8,10},{9,11},{10,... | collective-permute-start | bytes 393224 | tf_op jit(solution)/shard_map/ppermute | solution.py:26
  54.7 0.9 collective-permute-done.5.refs_5_
  55.6 8.4 %collective-permute-done.3.refs_2_ = bf16[1,512,128]{2,1,0:T(8,128)(2,1)S(1)} collective-permute-done((bf16[1,512,128]{2,1,0:T(8,128)(2,1)S(1)}, bf16[1,512,128]{2,1,0:T(8,128)(2,1)S(1)}, u32[]{:S(2)}, u32[]{:S(2)}) %collective-permute-start.3) | collective-permute-done | bytes 131104 | tf_op jit(solution)/shard_map/ppermute | solution.py:26
  64.0 0.9 copy-done.4
  65.0 0.9 copy-done.6
  65.9 1.9 %stacked_gram.2 = (bf16[512,512]{1,0:T(8,128)(2,1)S(1)}, bf16[128,1280]{1,0:T(8,128)(2,1)S(1)}) custom-call(f32[4,8,512]{2,1,0:T(8,128)S(1)} %add.54.squares_ref, bf16[1,512,256]{2,1,0:T(8,128)(2,1)S(1)} %copy-done.6, bf16[1,512,256]{2,1,0:T(8,128)(2,1)} %collective-permute-done.2.refs_1_, bf16[1,512,128]{2,1,0:T(8,128)(2,1)S(1)} %collective-permute-done.3.refs_2_, ...), custom_call_target="tpu_custom_call" | custom-call | tf_op jit(solution)/shard_map/stacked_gram/pallas_call | solution.py:150
  67.8 1.6 %collective-permute-start.8 = (bf16[64,1280]{1,0:T(8,128)(2,1)S(1)}, bf16[64,1280]{1,0:T(8,128)(2,1)S(1)}, u32[]{:S(2)}, u32[]{:S(2)}) collective-permute-start(bf16[64,1280]{1,0:T(8,128)(2,1)S(1)} %constant_dynamic-slice_fusion.1), channel_id=1, source_target_pairs={{0,4},{4,0},{8,12},{12,8},{16,20},{20,16},{24,28},{28,24},{1,5},{5... | collective-permute-start | bytes 491528 | tf_op jit(solution)/shard_map/ppermute | solution.py:26
  69.5 0.6 collective-permute-start.14
  70.1 3.1 %collective-permute-done.8 = bf16[64,1280]{1,0:T(8,128)(2,1)S(1)} collective-permute-done((bf16[64,1280]{1,0:T(8,128)(2,1)S(1)}, bf16[64,1280]{1,0:T(8,128)(2,1)S(1)}, u32[]{:S(2)}, u32[]{:S(2)}) %collective-permute-start.8) | collective-permute-done | bytes 163872 | tf_op jit(solution)/shard_map/ppermute | solution.py:26
  73.3 1.6 %collective-permute-start.9 = (bf16[32,1280]{1,0:T(8,128)(2,1)S(1)}, bf16[32,1280]{1,0:T(8,128)(2,1)S(1)}, u32[]{:S(2)}, u32[]{:S(2)}) collective-permute-start(bf16[32,1280]{1,0:T(8,128)(2,1)S(1)} %dynamic-slice_convert_fusion.1), channel_id=1, source_target_pairs={{0,8},{4,12},{8,0},{12,4},{16,24},{20,28},{24,16},{28,20},{1,9},{5... | collective-permute-start | bytes 245768 | tf_op jit(solution)/shard_map/ppermute | solution.py:26
  74.9 4.1 %collective-permute-done.14.refs_2_ = bf16[3,512,128]{2,1,0:T(8,128)(2,1)S(1)} collective-permute-done((bf16[3,512,128]{2,1,0:T(8,128)(2,1)S(1)}, bf16[3,512,128]{2,1,0:T(8,128)(2,1)S(1)}, u32[]{:S(2)}, u32[]{:S(2)}) %collective-permute-start.14) | collective-permute-done | bytes 393248 | tf_op jit(solution)/shard_map/ppermute | solution.py:26
  79.0 0.9 stacked_gram.3
  79.9 0.6 collective-permute-start.17
  80.5 2.6 %collective-permute-start.10 = (bf16[32,1280]{1,0:T(8,128)(2,1)S(1)}, bf16[32,1280]{1,0:T(8,128)(2,1)S(1)}, u32[]{:S(2)}, u32[]{:S(2)}) collective-permute-start(bf16[32,1280]{1,0:T(8,128)(2,1)S(1)} %add_convert_fusion.8), channel_id=1, source_target_pairs={{0,16},{4,20},{8,24},{12,28},{16,0},{20,4},{24,8},{28,12},{1,17},{... | collective-permute-start | bytes 245768 | tf_op jit(solution)/shard_map/ppermute | solution.py:26
  83.2 2.1 %collective-permute-done.17 = bf16[64,1280]{1,0:T(8,128)(2,1)S(1)} collective-permute-done((bf16[64,1280]{1,0:T(8,128)(2,1)S(1)}, bf16[64,1280]{1,0:T(8,128)(2,1)S(1)}, u32[]{:S(2)}, u32[]{:S(2)}) %collective-permute-start.17) | collective-permute-done | bytes 163872 | tf_op jit(solution)/shard_map/ppermute | solution.py:26
  85.4 1.6 %collective-permute-start.18 = (bf16[32,1280]{1,0:T(8,128)(2,1)S(1)}, bf16[32,1280]{1,0:T(8,128)(2,1)S(1)}, u32[]{:S(2)}, u32[]{:S(2)}) collective-permute-start(bf16[32,1280]{1,0:T(8,128)(2,1)S(1)} %dynamic-slice_convert_fusion), channel_id=1, source_target_pairs={{0,8},{4,12},{8,0},{12,4},{16,24},{20,28},{24,16},{28,20},{1,9},{5... | collective-permute-start | bytes 245768 | tf_op jit(solution)/shard_map/ppermute | solution.py:26
  87.1 1.2 collective-permute-start.11
  88.2 2.3 %collective-permute-done.18 = bf16[32,1280]{1,0:T(8,128)(2,1)S(1)} collective-permute-done((bf16[32,1280]{1,0:T(8,128)(2,1)S(1)}, bf16[32,1280]{1,0:T(8,128)(2,1)S(1)}, u32[]{:S(2)}, u32[]{:S(2)}) %collective-permute-start.18) | collective-permute-done | bytes 81952 | tf_op jit(solution)/shard_map/ppermute | solution.py:26
  90.5 2.0 %collective-permute-start.19 = (bf16[32,1280]{1,0:T(8,128)(2,1)S(1)}, bf16[32,1280]{1,0:T(8,128)(2,1)S(1)}, u32[]{:S(2)}, u32[]{:S(2)}) collective-permute-start(bf16[32,1280]{1,0:T(8,128)(2,1)S(1)} %add_convert_fusion.6), channel_id=1, source_target_pairs={{0,16},{4,20},{8,24},{12,28},{16,0},{20,4},{24,8},{28,12},{1,17},{... | collective-permute-start | bytes 245768 | tf_op jit(solution)/shard_map/ppermute | solution.py:26
  92.6 3.3 %collective-permute-done.19 = bf16[32,1280]{1,0:T(8,128)(2,1)S(1)} collective-permute-done((bf16[32,1280]{1,0:T(8,128)(2,1)S(1)}, bf16[32,1280]{1,0:T(8,128)(2,1)S(1)}, u32[]{:S(2)}, u32[]{:S(2)}) %collective-permute-start.19) | collective-permute-done | bytes 81952 | tf_op jit(solution)/shard_map/ppermute | solution.py:26
  96.0 2.2 %collective-permute-start.20 = (bf16[32,1280]{1,0:T(8,128)(2,1)S(1)}, bf16[32,1280]{1,0:T(8,128)(2,1)S(1)}, u32[]{:S(2)}, u32[]{:S(2)}) collective-permute-start(bf16[32,1280]{1,0:T(8,128)(2,1)S(1)} %add_convert_fusion.5), channel_id=1, source_target_pairs={{0,8},{4,12},{8,0},{12,4},{16,24},{20,28},{24,16},{28,20},{1,9},{5... | collective-permute-start | bytes 245768 | tf_op jit(solution)/shard_map/ppermute | solution.py:26
  98.1 0.2 collective-permute-start.12
  98.3 2.2 %collective-permute-done.20 = bf16[32,1280]{1,0:T(8,128)(2,1)S(1)} collective-permute-done((bf16[32,1280]{1,0:T(8,128)(2,1)S(1)}, bf16[32,1280]{1,0:T(8,128)(2,1)S(1)}, u32[]{:S(2)}, u32[]{:S(2)}) %collective-permute-start.20) | collective-permute-done | bytes 81952 | tf_op jit(solution)/shard_map/ppermute | solution.py:26
  100.6 0.7 collective-permute-start.21
  101.3 2.2 %collective-permute-done.12 = bf16[64,1280]{1,0:T(8,128)(2,1)S(1)} collective-permute-done((bf16[64,1280]{1,0:T(8,128)(2,1)S(1)}, bf16[64,1280]{1,0:T(8,128)(2,1)S(1)}, u32[]{:S(2)}, u32[]{:S(2)}) %collective-permute-start.12) | collective-permute-done | bytes 163872 | tf_op jit(solution)/shard_map/ppermute | solution.py:26
  103.5 2.4 %collective-permute-done.21 = bf16[64,1280]{1,0:T(8,128)(2,1)S(1)} collective-permute-done((bf16[64,1280]{1,0:T(8,128)(2,1)S(1)}, bf16[64,1280]{1,0:T(8,128)(2,1)S(1)}, u32[]{:S(2)}, u32[]{:S(2)}) %collective-permute-start.21) | collective-permute-done | bytes 163872 | tf_op jit(solution)/shard_map/ppermute | solution.py:26
  106.2 12.7 %basis_latents.1 = bf16[512,256]{1,0:T(8,128)(2,1)S(1)} custom-call(s32[1]{0:T(128)} %bitcast.m_ref, bf16[8,512,128]{2,1,0:T(8,128)(2,1)S(1)} %copy-done.2, bf16[128,1280]{1,0:T(8,128)(2,1)S(1)} %pad_maximum_fusion.refs_0_, bf16[128,1280]{1,0:T(8,128)(2,1)S(1)} %pad_maximum_fusion.1.refs_1_, bf16[512,512]{1,0:T(8,128)(2,1)S(1)} %get-tuple-element.37.refs_2_, ...), custom_call_target="tpu_custom_call" | custom-call | tf_op jit(solution)/shard_map/basis_latents/pallas_call | solution.py:294
  118.9 0.8 reshape.7
  (52 shorter events, 1.0 us)
Async XLA Ops:
  0.0 5.8 %copy-start = (bf16[4,2048,1024]{2,1,0:T(8,128)(2,1)S(1)}, bf16[4,2048,1024]{2,1,0:T(8,128)(2,1)}, u32[]{:S(2)}) copy-start(bf16[4,2048,1024]{2,1,0:T(8,128)(2,1)} %refs_3_.9) | copy-start | bytes 50331652
  5.8 3.4 %copy-start.1 = (bf16[4,512,2048]{2,1,0:T(8,128)(2,1)S(1)}, bf16[4,512,2048]{2,1,0:T(8,128)(2,1)}, u32[]{:S(2)}) copy-start(bf16[4,512,2048]{2,1,0:T(8,128)(2,1)} %hid_ref.9) | copy-start | bytes 25165828
  9.2 0.7 copy-start.7
  14.6 0.7 copy-start.3
  15.2 5.4 %copy-start.8 = (bf16[4,2048]{1,0:T(4,128)(2,1)S(1)}, bf16[4,2048]{1,0:T(4,128)(2,1)}, u32[]{:S(2)}) copy-start(bf16[4,2048]{1,0:T(4,128)(2,1)} %gain_ref.9) | copy-start | bytes 49156
  19.9 0.7 copy-start.5
  29.5 5.3 %collective-permute-start = (f32[4,8,512]{2,1,0:T(8,128)S(1)}, f32[4,8,512]{2,1,0:T(8,128)S(1)}, u32[]{:S(2)}, u32[]{:S(2)}) collective-permute-start(f32[4,8,512]{2,1,0:T(8,128)S(1)} %constant_dynamic-update-slice_fusion), channel_id=1, source_target_pairs={{0,1},{1,0},{2,3},{3,2},{4,5},{5,4},{6,7},{7,6},{8,9},{9,8},{10,11... | collective-permute-start | bytes 196616 | tf_op jit(solution)/shard_map/ppermute | solution.py:26
  33.8 18.9 %collective-permute-start.15 = (bf16[1,512,256]{2,1,0:T(8,128)(2,1)}, bf16[1,512,256]{2,1,0:T(8,128)(2,1)S(1)}, u32[]{:S(2)}, u32[]{:S(2)}) collective-permute-start(bf16[1,512,256]{2,1,0:T(8,128)(2,1)} %get-tuple-element.35), channel_id=1, source_target_pairs={{0,1},{1,0},{2,3},{3,2},{4,5},{5,4},{6,7},{7,6},{8,9},{9,8},{10,11... | collective-permute-start | bytes 786440 | tf_op jit(solution)/shard_map/ppermute | solution.py:26
  33.9 14.2 %collective-permute-start.4 = (bf16[1,512,256]{2,1,0:T(8,128)(2,1)}, bf16[1,512,256]{2,1,0:T(8,128)(2,1)}, u32[]{:S(2)}, u32[]{:S(2)}) collective-permute-start(bf16[1,512,256]{2,1,0:T(8,128)(2,1)} %get-tuple-element.28), channel_id=1, source_target_pairs={{0,1},{1,0},{2,3},{3,2},{4,5},{5,4},{6,7},{7,6},{8,9},{9,8},{10,11... | collective-permute-start | bytes 786440 | tf_op jit(solution)/shard_map/ppermute | solution.py:26
  34.4 17.1 %collective-permute-start.2 = (bf16[1,512,256]{2,1,0:T(8,128)(2,1)}, bf16[1,512,256]{2,1,0:T(8,128)(2,1)}, u32[]{:S(2)}, u32[]{:S(2)}) collective-permute-start(bf16[1,512,256]{2,1,0:T(8,128)(2,1)} %get-tuple-element.26), channel_id=1, source_target_pairs={{0,1},{1,0},{2,3},{3,2},{4,5},{5,4},{6,7},{7,6},{8,9},{9,8},{10,11... | collective-permute-start | bytes 786440 | tf_op jit(solution)/shard_map/ppermute | solution.py:26
  34.4 15.1 %collective-permute-start.6 = (bf16[2,512,256]{2,1,0:T(8,128)(2,1)}, bf16[2,512,256]{2,1,0:T(8,128)(2,1)S(1)}, u32[]{:S(2)}, u32[]{:S(2)}) collective-permute-start(bf16[2,512,256]{2,1,0:T(8,128)(2,1)} %get-tuple-element.30), channel_id=1, source_target_pairs={{0,1},{1,0},{2,3},{3,2},{4,5},{5,4},{6,7},{7,6},{8,9},{9,8},{10,11... | collective-permute-start | bytes 1572872 | tf_op jit(solution)/shard_map/ppermute | solution.py:26
  34.9 13.0 %collective-permute-start.1 = (f32[4,8,512]{2,1,0:T(8,128)S(1)}, f32[4,8,512]{2,1,0:T(8,128)S(1)}, u32[]{:S(2)}, u32[]{:S(2)}) collective-permute-start(f32[4,8,512]{2,1,0:T(8,128)S(1)} %add.53), channel_id=1, source_target_pairs={{0,2},{1,3},{2,0},{3,1},{4,6},{5,7},{6,4},{7,5},{8,10},{9,11},{10,... | collective-permute-start | bytes 196616 | tf_op jit(solution)/shard_map/ppermute | solution.py:26
  47.0 0.9 copy-start.9
  47.9 58.3 %copy-start.2 = (bf16[8,512,128]{2,1,0:T(8,128)(2,1)S(1)}, bf16[8,512,128]{2,1,0:T(8,128)(2,1)}, u32[]{:S(2)}) copy-start(bf16[8,512,128]{2,1,0:T(8,128)(2,1)} %start_ref.1) | copy-start | bytes 3145732
  47.9 21.5 %collective-permute-start.13 = (bf16[3,512,256]{2,1,0:T(8,128)(2,1)}, bf16[3,512,256]{2,1,0:T(8,128)(2,1)S(1)}, u32[]{:S(2)}, u32[]{:S(2)}) collective-permute-start(bf16[3,512,256]{2,1,0:T(8,128)(2,1)} %copy-done.9), channel_id=1, source_target_pairs={{0,1},{1,0},{2,3},{3,2},{4,5},{5,4},{6,7},{7,6},{8,9},{9,8},{10,11... | collective-permute-start | bytes 2359304 | tf_op jit(solution)/shard_map/ppermute | solution.py:26
  49.2 6.4 %collective-permute-start.5 = (bf16[1,512,128]{2,1,0:T(8,128)(2,1)S(1)}, bf16[1,512,128]{2,1,0:T(8,128)(2,1)S(1)}, u32[]{:S(2)}, u32[]{:S(2)}) collective-permute-start(bf16[1,512,128]{2,1,0:T(8,128)(2,1)S(1)} %add_convert_fusion.3), channel_id=1, source_target_pairs={{0,2},{1,3},{2,0},{3,1},{4,6},{5,7},{6,4},{7,5},{8,10},{9,11},{10,... | collective-permute-start | bytes 393224 | tf_op jit(solution)/shard_map/ppermute | solution.py:26
  49.6 14.5 %collective-permute-start.7 = (bf16[2,512,128]{2,1,0:T(8,128)(2,1)S(1)}, bf16[2,512,128]{2,1,0:T(8,128)(2,1)S(1)}, u32[]{:S(2)}, u32[]{:S(2)}) collective-permute-start(bf16[2,512,128]{2,1,0:T(8,128)(2,1)S(1)} %add_convert_fusion.1), channel_id=1, source_target_pairs={{0,2},{1,3},{2,0},{3,1},{4,6},{5,7},{6,4},{7,5},{8,10},{9,11},{10,... | collective-permute-start | bytes 786440 | tf_op jit(solution)/shard_map/ppermute | solution.py:26
  52.5 11.6 %collective-permute-start.3 = (bf16[1,512,128]{2,1,0:T(8,128)(2,1)S(1)}, bf16[1,512,128]{2,1,0:T(8,128)(2,1)S(1)}, u32[]{:S(2)}, u32[]{:S(2)}) collective-permute-start(bf16[1,512,128]{2,1,0:T(8,128)(2,1)S(1)} %add_convert_fusion.4), channel_id=1, source_target_pairs={{0,2},{1,3},{2,0},{3,1},{4,6},{5,7},{6,4},{7,5},{8,10},{9,11},{10,... | collective-permute-start | bytes 393224 | tf_op jit(solution)/shard_map/ppermute | solution.py:26
  52.8 22.1 %collective-permute-start.16 = (bf16[1,512,128]{2,1,0:T(8,128)(2,1)S(1)}, bf16[1,512,128]{2,1,0:T(8,128)(2,1)S(1)}, u32[]{:S(2)}, u32[]{:S(2)}) collective-permute-start(bf16[1,512,128]{2,1,0:T(8,128)(2,1)S(1)} %add_convert_fusion.2), channel_id=1, source_target_pairs={{0,2},{1,3},{2,0},{3,1},{4,6},{5,7},{6,4},{7,5},{8,10},{9,11},{10,... | collective-permute-start | bytes 393224 | tf_op jit(solution)/shard_map/ppermute | solution.py:26
  64.0 1.0 copy-start.4
  65.0 0.9 copy-start.6
  67.8 5.4 %collective-permute-start.8 = (bf16[64,1280]{1,0:T(8,128)(2,1)S(1)}, bf16[64,1280]{1,0:T(8,128)(2,1)S(1)}, u32[]{:S(2)}, u32[]{:S(2)}) collective-permute-start(bf16[64,1280]{1,0:T(8,128)(2,1)S(1)} %constant_dynamic-slice_fusion.1), channel_id=1, source_target_pairs={{0,4},{4,0},{8,12},{12,8},{16,20},{20,16},{24,28},{28,24},{1,5},{5... | collective-permute-start | bytes 491528 | tf_op jit(solution)/shard_map/ppermute | solution.py:26
  69.5 9.5 %collective-permute-start.14 = (bf16[3,512,128]{2,1,0:T(8,128)(2,1)S(1)}, bf16[3,512,128]{2,1,0:T(8,128)(2,1)S(1)}, u32[]{:S(2)}, u32[]{:S(2)}) collective-permute-start(bf16[3,512,128]{2,1,0:T(8,128)(2,1)S(1)} %add_convert_fusion), channel_id=1, source_target_pairs={{0,2},{1,3},{2,0},{3,1},{4,6},{5,7},{6,4},{7,5},{8,10},{9,11},{10,... | collective-permute-start | bytes 1179656 | tf_op jit(solution)/shard_map/ppermute | solution.py:26
  73.3 7.2 %collective-permute-start.9 = (bf16[32,1280]{1,0:T(8,128)(2,1)S(1)}, bf16[32,1280]{1,0:T(8,128)(2,1)S(1)}, u32[]{:S(2)}, u32[]{:S(2)}) collective-permute-start(bf16[32,1280]{1,0:T(8,128)(2,1)S(1)} %dynamic-slice_convert_fusion.1), channel_id=1, source_target_pairs={{0,8},{4,12},{8,0},{12,4},{16,24},{20,28},{24,16},{28,20},{1,9},{5... | collective-permute-start | bytes 245768 | tf_op jit(solution)/shard_map/ppermute | solution.py:26
  79.9 5.4 %collective-permute-start.17 = (bf16[64,1280]{1,0:T(8,128)(2,1)S(1)}, bf16[64,1280]{1,0:T(8,128)(2,1)S(1)}, u32[]{:S(2)}, u32[]{:S(2)}) collective-permute-start(bf16[64,1280]{1,0:T(8,128)(2,1)S(1)} %constant_dynamic-slice_fusion), channel_id=1, source_target_pairs={{0,4},{4,0},{8,12},{12,8},{16,20},{20,16},{24,28},{28,24},{1,5},{5... | collective-permute-start | bytes 491528 | tf_op jit(solution)/shard_map/ppermute | solution.py:26
  80.5 6.5 %collective-permute-start.10 = (bf16[32,1280]{1,0:T(8,128)(2,1)S(1)}, bf16[32,1280]{1,0:T(8,128)(2,1)S(1)}, u32[]{:S(2)}, u32[]{:S(2)}) collective-permute-start(bf16[32,1280]{1,0:T(8,128)(2,1)S(1)} %add_convert_fusion.8), channel_id=1, source_target_pairs={{0,16},{4,20},{8,24},{12,28},{16,0},{20,4},{24,8},{28,12},{1,17},{... | collective-permute-start | bytes 245768 | tf_op jit(solution)/shard_map/ppermute | solution.py:26
  85.4 5.1 %collective-permute-start.18 = (bf16[32,1280]{1,0:T(8,128)(2,1)S(1)}, bf16[32,1280]{1,0:T(8,128)(2,1)S(1)}, u32[]{:S(2)}, u32[]{:S(2)}) collective-permute-start(bf16[32,1280]{1,0:T(8,128)(2,1)S(1)} %dynamic-slice_convert_fusion), channel_id=1, source_target_pairs={{0,8},{4,12},{8,0},{12,4},{16,24},{20,28},{24,16},{28,20},{1,9},{5... | collective-permute-start | bytes 245768 | tf_op jit(solution)/shard_map/ppermute | solution.py:26
  87.1 5.5 %collective-permute-start.11 = (bf16[32,1280]{1,0:T(8,128)(2,1)S(1)}, bf16[32,1280]{1,0:T(8,128)(2,1)S(1)}, u32[]{:S(2)}, u32[]{:S(2)}) collective-permute-start(bf16[32,1280]{1,0:T(8,128)(2,1)S(1)} %add_convert_fusion.7), channel_id=1, source_target_pairs={{0,8},{4,12},{8,0},{12,4},{16,24},{20,28},{24,16},{28,20},{1,9},{5... | collective-permute-start | bytes 245768 | tf_op jit(solution)/shard_map/ppermute | solution.py:26
  90.5 5.4 %collective-permute-start.19 = (bf16[32,1280]{1,0:T(8,128)(2,1)S(1)}, bf16[32,1280]{1,0:T(8,128)(2,1)S(1)}, u32[]{:S(2)}, u32[]{:S(2)}) collective-permute-start(bf16[32,1280]{1,0:T(8,128)(2,1)S(1)} %add_convert_fusion.6), channel_id=1, source_target_pairs={{0,16},{4,20},{8,24},{12,28},{16,0},{20,4},{24,8},{28,12},{1,17},{... | collective-permute-start | bytes 245768 | tf_op jit(solution)/shard_map/ppermute | solution.py:26
  96.0 4.6 %collective-permute-start.20 = (bf16[32,1280]{1,0:T(8,128)(2,1)S(1)}, bf16[32,1280]{1,0:T(8,128)(2,1)S(1)}, u32[]{:S(2)}, u32[]{:S(2)}) collective-permute-start(bf16[32,1280]{1,0:T(8,128)(2,1)S(1)} %add_convert_fusion.5), channel_id=1, source_target_pairs={{0,8},{4,12},{8,0},{12,4},{16,24},{20,28},{24,16},{28,20},{1,9},{5... | collective-permute-start | bytes 245768 | tf_op jit(solution)/shard_map/ppermute | solution.py:26
  98.1 5.4 %collective-permute-start.12 = (bf16[64,1280]{1,0:T(8,128)(2,1)S(1)}, bf16[64,1280]{1,0:T(8,128)(2,1)S(1)}, u32[]{:S(2)}, u32[]{:S(2)}) collective-permute-start(bf16[64,1280]{1,0:T(8,128)(2,1)S(1)} %pad_maximum_fusion.2), channel_id=1, source_target_pairs={{0,4},{4,0},{8,12},{12,8},{16,20},{20,16},{24,28},{28,24},{1,5},{5... | collective-permute-start | bytes 491528 | tf_op jit(solution)/shard_map/ppermute | solution.py:26
  100.6 5.4 %collective-permute-start.21 = (bf16[64,1280]{1,0:T(8,128)(2,1)S(1)}, bf16[64,1280]{1,0:T(8,128)(2,1)S(1)}, u32[]{:S(2)}, u32[]{:S(2)}) collective-permute-start(bf16[64,1280]{1,0:T(8,128)(2,1)S(1)} %pad_maximum_fusion.3), channel_id=1, source_target_pairs={{0,4},{4,0},{8,12},{12,8},{16,20},{20,16},{24,28},{28,24},{1,5},{5... | collective-permute-start | bytes 491528 | tf_op jit(solution)/shard_map/ppermute | solution.py:26

commit v2 on v1

v2 whole, which is shorter than its diff:
```python
import functools

import jax
import jax.numpy as jnp
from jax import lax
from jax.experimental import pallas as pl
from jax.experimental.pallas import tpu as pltpu
from jax.sharding import PartitionSpec as P

HD = 128
ITERS = 2
EPSILON = 1e-05
F32 = jnp.float32
BF16 = jnp.bfloat16
HIGHEST = lax.Precision.HIGHEST
MIB = 1 << 20


def halving_order(count):
    bits = count.bit_length() - 1
    return sorted(range(count), key=lambda r: int(format(r, f"0{bits}b")[::-1], 2)) if bits else [0]


def exchange(x, axis, bit):
    size = lax.axis_size(axis)
    return lax.ppermute(x, axis, [(j, j ^ bit) for j in range(size)])


def partial_kernel(own, parcels, m_ref, gain_ref, hid_ref, w_ref, *refs):
    outs, squares_ref = refs[: 2 * len(parcels)], refs[2 * len(parcels)]
    rows_ref, cols_ref, sems = refs[-3:]
    layers, tokens, width = rows_ref.shape
    mp = cols_ref.shape[2] // HD // own
    order = halving_order(mp)
    place = {}
    for i, (slot, members) in enumerate(parcels):
        for j, layer in enumerate(members):
            place[slot, layer] = (outs[2 * i].at[j], outs[2 * i + 1].at[j])
    copies = {}
    for layer in range(layers):
        here = [pltpu.make_async_copy(hid_ref.at[layer], rows_ref.at[layer], sems.at[layer, 0])]
        for slot in range(own):
            for i, r in enumerate(order):
                column = pl.multiple_of((own * (m_ref[0] ^ r) + slot) * HD, HD)
                to = slot * mp + i
                here.append(
                    pltpu.make_async_copy(
                        w_ref.at[layer, :, pl.ds(column, HD)],
                        cols_ref.at[layer, :, pl.ds(to * HD, HD)],
                        sems.at[layer, 1 + to],
                    )
                )
        for copy in here:
            copy.start()
        copies[layer] = here
    half = mp // 2 * HD
    gains = gain_ref[...]
    for layer in range(layers):
        copies[layer][0].wait()
        rows = rows_ref[layer]
        scaled = rows * gains[layer : layer + 1]
        totals = []
        for slot in range(own):
            for copy in copies[layer][1 + slot * mp : 1 + (slot + 1) * mp]:
                copy.wait()
            weights = cols_ref[layer, :, slot * mp * HD : (slot + 1) * mp * HD]
            totals.append(jnp.dot(scaled, weights, preferred_element_type=F32))
        wide = rows.astype(F32)
        squares = None
        for i in range(width // HD):
            x = wide[:, i * HD : (i + 1) * HD]
            squares = x * x if squares is None else squares + x * x
        for slot in range(own):
            keep, send = place[slot, layer]
            keep[...] = totals[slot][:, :half].astype(BF16)
            send[...] = totals[slot][:, half:].astype(BF16)
        squares_ref[layer : layer + 1, :] = lax.dot_general(
            jnp.ones((8, HD), F32),
            squares,
            (((1,), (1,)), ((), ())),
            precision=HIGHEST,
            preferred_element_type=F32,
        )[:1]


def partial_products(hidden, gains, weights, me, own, parcels):
    layers, tokens, width = hidden.shape
    mp = lax.axis_size("mp")
    half = mp // 2 * HD
    outs = [jax.ShapeDtypeStruct((len(members), tokens, half), BF16) for _, members in parcels for _ in range(2)]
    outs.append(jax.ShapeDtypeStruct((layers, tokens), F32))
    vmem = pl.BlockSpec(memory_space=pltpu.VMEM)
    hbm = pl.BlockSpec(memory_space=pltpu.HBM)
    return pl.pallas_call(
        functools.partial(partial_kernel, own, parcels),
        out_shape=outs,
        in_specs=[pl.BlockSpec(memory_space=pltpu.SMEM), vmem, hbm, hbm],
        out_specs=[vmem] * len(outs),
        scratch_shapes=[
            pltpu.VMEM((layers, tokens, width), BF16),
            pltpu.VMEM((layers, width, own * mp * HD), BF16),
            pltpu.SemaphoreType.DMA((layers, own * mp + 1)),
        ],
        compiler_params=pltpu.CompilerParams(vmem_limit_bytes=32 * MIB),
        cost_estimate=pl.CostEstimate(
            flops=2 * layers * tokens * width * own * mp * HD,
            bytes_accessed=layers * width * (tokens + own * mp * HD) * 2,
            transcendentals=0,
        ),
        name="partial_products",
    )(me, gains, *[pltpu.with_memory_space_constraint(x, pltpu.HBM) for x in (hidden, weights)])


def extra_rows(tokens):
    return -(-3 * (tokens // HD) // 16) * 16


def merge_kernel(parts, tokens, with_totals, *refs):
    own_ref, out_ref = refs[-2:]
    layers, _, half = out_ref.shape
    for layer in range(layers):
        total = sum(r[layer].astype(F32) for r in refs[:parts])
        own_ref[layer] = total[:, :half].astype(BF16)
        out_ref[layer, :tokens, :] = total[:, half:].astype(BF16)
    if with_totals:
        totals = refs[parts][...]
        cuts = tokens // HD
        rows = out_ref.shape[1] - tokens
        for layer in range(layers):
            line = jnp.concatenate([totals[layer : layer + 1, i * HD : (i + 1) * HD] for i in range(cuts)], axis=0)
            pieces = [p.astype(F32) for p in split3(line)]
            pad = [jnp.zeros((rows - 3 * cuts, HD), F32)] if rows > 3 * cuts else []
            block = jnp.concatenate(pieces + pad, axis=0).astype(BF16)
            out_ref[layer, tokens:, :HD] = block
            if out_ref.shape[2] > HD:
                out_ref[layer, tokens:, HD:] = jnp.zeros((rows, out_ref.shape[2] - HD), BF16)


def next_send(arrays, totals, tokens):
    layers, _, width = arrays[0].shape
    half = width // 2
    rows = tokens + (extra_rows(tokens) if totals is not None else 0)
    extra = [] if totals is None else [totals]
    return pl.pallas_call(
        functools.partial(merge_kernel, len(arrays), tokens, totals is not None),
        out_shape=[
            jax.ShapeDtypeStruct((layers, tokens, half), BF16),
            jax.ShapeDtypeStruct((layers, rows, half), BF16),
        ],
        grid=(1,),
        in_specs=[pl.BlockSpec((layers, tokens, width), lambda i: (0, 0, 0)) for _ in arrays]
        + [pl.BlockSpec(t.shape, lambda i: (0, 0)) for t in extra],
        out_specs=[
            pl.BlockSpec((layers, tokens, half), lambda i: (0, 0, 0)),
            pl.BlockSpec((layers, rows, half), lambda i: (0, 0, 0)),
        ],
        compiler_params=pltpu.CompilerParams(vmem_limit_bytes=16 * MIB),
        name="next_send",
    )(*arrays, *extra)


def carried_totals(received, tokens):
    cuts = tokens // HD
    pieces = received[:, tokens : tokens + 3 * cuts, :HD].astype(F32)
    return pieces.reshape(-1, 3, tokens).sum(1)


def gram_kernel(shapes, width, squares_ref, *refs):
    stacked_ref, gram_ref = refs[-2:]
    refs = refs[:-2]
    layers = squares_ref.shape[0]
    factor = lax.rsqrt(squares_ref[...] / width + EPSILON)
    factor = jnp.transpose(jnp.concatenate([factor] * (8 // layers), axis=0))
    at, blocks = 0, []
    for count, parts in shapes:
        for i in range(count):
            total = sum(refs[at + j][i].astype(F32) for j in range(parts))
            layer = len(blocks)
            blocks.append((total * factor[:, layer : layer + 1]).astype(BF16))
        at += parts
    stacked = jnp.concatenate(blocks, axis=1)
    stacked_ref[...] = stacked
    column = 0
    for i, block in enumerate(blocks):
        upto = (i + 1) * HD
        gram_ref[:, column : column + upto] = lax.dot_general(
            block, stacked[:, :upto], (((0,), (0,)), ((), ())), preferred_element_type=F32
        ).astype(BF16)
        column += upto


def stacked_and_gram(contributions, squares, width):
    layers, tokens = squares.shape
    shapes = [(parts[0].shape[0], len(parts)) for parts in contributions]
    arrays = [a for parts in contributions for a in parts]
    packed = layers * (layers + 1) // 2 * HD
    return pl.pallas_call(
        functools.partial(gram_kernel, shapes, width),
        out_shape=[
            pltpu.HBM((tokens, layers * HD), BF16),
            jax.ShapeDtypeStruct((HD, packed), BF16),
        ],
        grid=(1,),
        in_specs=[pl.BlockSpec(squares.shape, lambda i: (0, 0))]
        + [pl.BlockSpec((a.shape[0], tokens, HD), lambda i: (0, 0, 0)) for a in arrays],
        out_specs=[
            pl.BlockSpec((tokens, layers * HD), lambda i: (0, 0)),
            pl.BlockSpec((HD, packed), lambda i: (0, 0)),
        ],
        compiler_params=pltpu.CompilerParams(vmem_limit_bytes=16 * MIB),
        name="stacked_gram",
    )(squares, *arrays)


def sum_over_seq(x):
    size = lax.axis_size("seq")
    me = lax.axis_index("seq")
    bits = [1 << i for i in range(size.bit_length() - 1)]
    for bit in bits[:-1]:
        half = x.shape[0] // 2
        mine = jnp.where((me & bit) != 0, half, 0)
        got = exchange(lax.dynamic_slice_in_dim(x, half - mine, half, 0).astype(BF16), "seq", bit)
        x = lax.dynamic_slice_in_dim(x, mine, half, 0).astype(F32) + got.astype(F32)
    x = x.astype(BF16)
    x = (x.astype(F32) + exchange(x, "seq", bits[-1]).astype(F32)).astype(BF16)
    for bit in bits[:-1][::-1]:
        got = exchange(x, "seq", bit)
        upper = (me & bit) != 0
        x = jnp.concatenate([jnp.where(upper, got, x), jnp.where(upper, x, got)], axis=0)
    return x


def split3(x):
    high = x.astype(BF16)
    rest = x - high.astype(F32)
    middle = rest.astype(BF16)
    return high, middle, (rest - middle.astype(F32)).astype(BF16)


def rank_update(x):
    h, m, l = split3(x)
    left = jnp.concatenate([h, h, m, h, m, l], axis=0)
    right = jnp.concatenate([h, m, h, l, m, h], axis=0)
    return lax.dot_general(left, right, (((0,), (0,)), ((), ())), preferred_element_type=F32)


def reciprocal(d):
    r = pl.reciprocal(d, approx=True)
    return r * (2.0 - d * r)


def factor_panel(rows, base):
    b, n = rows.shape
    lane = lax.broadcasted_iota(jnp.int32, (b, n), 1)
    row = lax.broadcasted_iota(jnp.int32, (b, n), 0)
    columns = [jnp.broadcast_to(rows[:, base + j : base + j + 1], (b, n)) for j in range(b)]
    pivots = jnp.zeros((b, n), F32)
    for k in range(b):
        pivot = jnp.broadcast_to(columns[k][k : k + 1, :], (b, n))
        pivots = jnp.where(row == k, pivot, pivots)
        here = lane == base + k
        rows = jnp.where(here & (row >= k), jnp.where(row == k, 1.0, 0.0), rows)
        if k < b - 1:
            multiplier = jnp.where(row > k, columns[k] * reciprocal(pivot), 0.0)
            rows = rows - multiplier * jnp.broadcast_to(rows[k : k + 1, :], (b, n))
            for j in range(k + 1, b):
                columns[j] = columns[j] - multiplier * jnp.broadcast_to(columns[j][k : k + 1, :], (b, n))
    rows = jnp.where((lane > base + row) & (lane < base + b), 0.0, rows)
    return rows * lax.rsqrt(pivots)


def inverse_cholesky(matrices, b=16):
    n = matrices[0].shape[0]
    panels = [[] for _ in matrices]
    rests = list(matrices)
    lane = lax.broadcasted_iota(jnp.int32, (n, n), 1)
    row = lax.broadcasted_iota(jnp.int32, (n, n), 0)
    for base in range(0, n, b):
        for s, rest in enumerate(rests):
            panels[s].append(factor_panel(rest[:b], base))
        if base + b < n:
            for s, rest in enumerate(rests):
                update = rank_update(panels[s][-1])[base + b :]
                rest = rest[b:]
                at = lane[: rest.shape[0]]
                rests[s] = jnp.where((at >= base) & (at < base + b), 0.0, rest) - update
    return [jnp.where(lane <= row, jnp.concatenate(p, axis=0), 0.0) for p in panels]


def basis_kernel(own, layers, start_ref, *refs):
    gram_refs, stacked_refs, out_ref = refs[:own], refs[own : 2 * own], refs[2 * own]
    rows_ref, sems = refs[2 * own + 1 :]
    copies = [pltpu.make_async_copy(stacked_refs[s], rows_ref.at[s], sems.at[s]) for s in range(own)]
    for copy in copies:
        copy.start()
    grams = []
    for ref in gram_refs:
        block = {}
        column = 0
        for i in range(layers):
            for j in range(i + 1):
                block[i, j] = ref[:, column : column + HD]
                column += HD
        rows = []
        for i in range(layers):
            rows.append(
                jnp.concatenate(
                    [
                        block[i, j] if j <= i else jnp.transpose(block[j, i].astype(F32)).astype(BF16)
                        for j in range(layers)
                    ],
                    axis=1,
                )
            )
        grams.append(jnp.concatenate(rows, axis=0))
    rank = start_ref.shape[2]
    images = [jnp.dot(grams[s], start_ref[s], preferred_element_type=F32) for s in range(own)]
    for step in range(ITERS):
        if step:
            images = [
                jnp.dot(grams[s], jnp.concatenate(split3(images[s]), axis=1), preferred_element_type=F32)
                for s in range(own)
            ]
            images = [x[:, :rank] + x[:, rank : 2 * rank] + x[:, 2 * rank :] for x in images]
        inner = [
            lax.dot_general(x, x, (((0,), (0,)), ((), ())), precision=HIGHEST, preferred_element_type=F32)
            for x in images
        ]
        inverse = inverse_cholesky(inner)
        images = [
            lax.dot_general(x, f, (((1,), (1,)), ((), ())), precision=HIGHEST, preferred_element_type=F32)
            for x, f in zip(images, inverse)
        ]
    for s in range(own):
        copies[s].wait()
        out_ref[:, s, :] = jnp.dot(
            rows_ref[s], images[s].astype(BF16), preferred_element_type=F32
        ).astype(BF16)


def latents_of(start, grams, stacked):
    own = len(grams)
    tokens = stacked[0].shape[0]
    layers = stacked[0].shape[1] // HD
    whole = lambda a: pl.BlockSpec(a.shape, lambda i: (0,) * a.ndim)
    return pl.pallas_call(
        functools.partial(basis_kernel, own, layers),
        out_shape=jax.ShapeDtypeStruct((tokens, own, HD), BF16),
        grid=(1,),
        in_specs=[whole(a) for a in [start] + grams] + [pl.BlockSpec(memory_space=pltpu.HBM)] * own,
        out_specs=pl.BlockSpec((tokens, own, HD), lambda i: (0, 0, 0)),
        scratch_shapes=[pltpu.VMEM((own,) + stacked[0].shape, BF16), pltpu.SemaphoreType.DMA((own,))],
        compiler_params=pltpu.CompilerParams(vmem_limit_bytes=16 * MIB),
        name="basis_latents",
    )(start, *grams, *[pltpu.with_memory_space_constraint(x, pltpu.HBM) for x in stacked])


def parcels_of(layers, own):
    return [(slot, list(range(layers))) for slot in range(own)]


def on_device(hidden, norm_gain, proj_weight, start_block):
    layers, tokens, width = hidden.shape
    mp = lax.axis_size("mp")
    own = proj_weight.shape[2] // HD // mp
    me = lax.axis_index("mp").astype(jnp.int32).reshape(1)
    mp_bits = [1 << i for i in range(mp.bit_length() - 1)]

    outs = partial_products(hidden, norm_gain, proj_weight, me, own, parcels_of(layers, own))
    totals = outs[-1]
    pieces = [[outs[2 * slot]] for slot in range(own)]
    for bit in mp_bits:
        for slot in range(own):
            if bit == 1:
                got = exchange(outs[2 * slot + 1], "mp", bit)
                if slot == 0:
                    totals = totals + exchange(totals, "mp", bit)
            else:
                own_sum, send = next_send(pieces[slot], totals if slot == 0 else None, tokens)
                pieces[slot] = [own_sum]
                got = exchange(send, "mp", bit)
                if slot == 0:
                    totals = totals + carried_totals(got, tokens)
            pieces[slot].append(got)
    pieces = [[parts] for parts in pieces]

    grams, stacked = [], []
    for slot in range(own):
        rows, gram = stacked_and_gram(pieces[slot], totals, width * mp)
        stacked.append(rows)
        grams.append(sum_over_seq(gram))
    start = lax.dynamic_slice_in_dim(start_block, me[0] * own, own, 0)
    return latents_of(start, grams, stacked)


def solution(mesh):
    return jax.shard_map(
        on_device,
        mesh=mesh,
        in_specs=(P(None, "seq", "mp"), P(None, "mp"), P(None, "mp", None), P()),
        out_specs=P("seq", "mp", None),
        check_vma=False,
    )
```

time: 120 us -> 91.8 us (0.77)
  local copies, waits for them, and re-layouts: 14.9 us -> 0.91 us
  Pallas kernels: 47 us -> 35 us
  waiting for transfers between devices: 31.2 us -> 34.2 us
  starting transfers between devices: 23.6 us -> 20.8 us
  other arithmetic: 2.71 us -> 0.42 us
    pallas_call x5 -> x3, Pallas kernels: 31.5 us -> 17.4 us  [the longest x1 15.3 us: partial_products(): pl.pallas_call(functools.partial(partial_kernel, own, parcels), out_shape...]
    unnamed x22 -> x4, local copies, waits for them, and re-layouts: 14.1 us -> 0.81 us
    ppermute x22 -> x15, waiting for transfers between devices: 31.2 us -> 34.2 us  [exchange(): return lax.ppermute(x, axis, [(j, j ^ bit) for j in range(size)])]
    ppermute x22 -> x15, starting transfers between devices: 23.6 us -> 20.8 us  [exchange(): return lax.ppermute(x, axis, [(j, j ^ bit) for j in range(size)])]
    convert_element_type x5 -> x0, other arithmetic: 2.32 us -> none  [on_device(): sum((c[:, :, half:2 * half].astype(F32) for c in contributions))]
    pallas_call x1, Pallas kernels: 12.7 us -> 14.5 us  [latents_of(): pl.pallas_call(functools.partial(basis_kernel, own, layers), out_shape=ja...]
  transfers between devices with their start and end apart: 22 -> 15, of which waited for: 10 -> 10; matrix products, arithmetic and copies ran while one was open for 2% -> 0% of each run, Pallas kernels for 13% -> 6%
where the time goes in v2:
time: 91.8 us; the launch traced here: 91.6 us
  Pallas kernels  35 us (38%)
  waiting for transfers between devices  34.2 us (37%)
  starting transfers between devices  20.8 us (23%)
    ppermute x15, waiting for transfers between devices, exchange(): return lax.ppermute(x, axis, [(j, j ^ bit) for j in range(size)])  34.2 us
    ppermute x15, starting transfers between devices, exchange(): return lax.ppermute(x, axis, [(j, j ^ bit) for j in range(size)])  20.8 us
    pallas_call x1, Pallas kernels, partial_products(): pl.pallas_call(functools.partial(partial_kernel, own, parcels), out_shape...  15.3 us
    pallas_call x1, Pallas kernels, latents_of(): pl.pallas_call(functools.partial(basis_kernel, own, layers), out_shape=ja...  14.5 us
    pallas_call x2, Pallas kernels, stacked_and_gram(): pl.pallas_call(functools.partial(gram_kernel, shapes, width), out_shape=[...  3.15 us
    pallas_call x2, Pallas kernels, next_send(): pl.pallas_call(functools.partial(merge_kernel, len(arrays), tokens, total...  2.09 us
  transfers between devices with their start and end apart: 15, of which 10 were waited for; matrix products, arithmetic and copies ran while one was open for 0% of the time, Pallas kernels for 6%

profile of v2, /device:TPU:0, one launch (start us, length us, event | category | flops | bytes accessed | tf_op | source)
XLA Modules:
  0.0 91.6 jit_solution(15566240193869068841)
XLA Ops:
  0.0 0.0 copy-start
  0.0 0.0 copy-start.1
  0.0 0.8 copy-done.1
  0.8 15.3 %partial_products.1 = (bf16[4,512,256]{2,1,0:T(8,128)(2,1)S(1)}, bf16[4,512,256]{2,1,0:T(8,128)(2,1)S(1)}, bf16[4,512,256]{2,1,0:T(8,128)(2,1)S(1)}, bf16[4,512,256]{2,1,0:T(8,128)(2,1)S(1)}, f32[4,512]{1,0:T(4,128)S(1)}) custom-call(s32[1]{0:T(128)} %bitcast.m_ref, bf16[4,2048]{1,0:T(4,128)(2,1)S(1)} %copy-done.1, bf16[4,512,2048]{2,1,0:T(8,128)(2,1)} %hid_ref.1, ...), custom_call_target="tpu_custom_call" | custom-call | flops 8589934592 | bytes 25165824 | tf_op jit(solution)/shard_map/partial_products/pallas_call | solution.py:94
  16.1 0.5 collective-permute-start.1
  16.6 0.1 collective-permute-start.8
  16.7 0.4 collective-permute-start
  17.1 3.3 %collective-permute-done = f32[4,512]{1,0:T(4,128)S(1)} collective-permute-done((f32[4,512]{1,0:T(4,128)S(1)}, f32[4,512]{1,0:T(4,128)S(1)}, u32[]{:S(2)}, u32[]{:S(2)}) %collective-permute-start) | collective-permute-done | bytes 8224 | tf_op jit(solution)/shard_map/ppermute | solution.py:26
  20.4 0.0 collective-permute-done.1.refs_1_
  20.4 1.0 %next_send.2 = (bf16[4,512,128]{2,1,0:T(8,128)(2,1)S(1)}, bf16[4,528,128]{2,1,0:T(8,128)(2,1)}) custom-call(bf16[4,512,256]{2,1,0:T(8,128)(2,1)S(1)} %get-tuple-element.19.refs_0_, bf16[4,512,256]{2,1,0:T(8,128)(2,1)S(1)} %collective-permute-done.1.refs_1_, f32[4,512]{1,0:T(4,128)S(1)} %add.42.refs_2_), custom_call_target="tpu_custom_call" | custom-call | tf_op jit(solution)/shard_map/next_send/pallas_call | solution.py:144
  21.4 2.9 %collective-permute-start.2 = (bf16[4,528,128]{2,1,0:T(8,128)(2,1)}, bf16[4,528,128]{2,1,0:T(8,128)(2,1)S(1)}, u32[]{:S(2)}, u32[]{:S(2)}) collective-permute-start(bf16[4,528,128]{2,1,0:T(8,128)(2,1)} %get-tuple-element.21), channel_id=1, source_target_pairs={{0,2},{1,3},{2,0},{3,1},{4,6},{5,7},{6,4},{7,5},{8,10},{9,11},{10,... | collective-permute-start | bytes 1622024 | tf_op jit(solution)/shard_map/ppermute | solution.py:26
  24.3 0.0 collective-permute-done.8.refs_1_
  24.3 1.1 %next_send.3 = (bf16[4,512,128]{2,1,0:T(8,128)(2,1)S(1)}, bf16[4,512,128]{2,1,0:T(8,128)(2,1)}) custom-call(bf16[4,512,256]{2,1,0:T(8,128)(2,1)S(1)} %get-tuple-element.24.refs_0_, bf16[4,512,256]{2,1,0:T(8,128)(2,1)S(1)} %collective-permute-done.8.refs_1_), custom_call_target="tpu_custom_call" | custom-call | tf_op jit(solution)/shard_map/next_send/pallas_call | solution.py:144
  25.4 0.0 collective-permute-start.9
  25.4 12.2 %collective-permute-done.2.refs_1_ = bf16[4,528,128]{2,1,0:T(8,128)(2,1)S(1)} collective-permute-done((bf16[4,528,128]{2,1,0:T(8,128)(2,1)}, bf16[4,528,128]{2,1,0:T(8,128)(2,1)S(1)}, u32[]{:S(2)}, u32[]{:S(2)}) %collective-permute-start.2) | collective-permute-done | bytes 540704 | tf_op jit(solution)/shard_map/ppermute | solution.py:26
  37.6 1.5 %stacked_gram.2 = (bf16[512,512]{1,0:T(8,128)(2,1)}, bf16[128,1280]{1,0:T(8,128)(2,1)S(1)}) custom-call(f32[4,512]{1,0:T(4,128)S(1)} %add.43.squares_ref, bf16[4,512,128]{2,1,0:T(8,128)(2,1)S(1)} %get-tuple-element.22.refs_0_, bf16[4,528,128]{2,1,0:T(8,128)(2,1)S(1)} %collective-permute-done.2.refs_1_), custom_call_target="tpu_custom_call" | custom-call | tf_op jit(solution)/shard_map/stacked_gram/pallas_call | solution.py:197
  39.1 2.2 %collective-permute-start.3 = (bf16[64,1280]{1,0:T(8,128)(2,1)S(1)}, bf16[64,1280]{1,0:T(8,128)(2,1)S(1)}, u32[]{:S(2)}, u32[]{:S(2)}) collective-permute-start(bf16[64,1280]{1,0:T(8,128)(2,1)S(1)} %constant_dynamic-slice_fusion.1), channel_id=1, source_target_pairs={{0,4},{4,0},{8,12},{12,8},{16,20},{20,16},{24,28},{28,24},{1,5},{5... | collective-permute-start | bytes 491528 | tf_op jit(solution)/shard_map/ppermute | solution.py:26
  41.3 7.0 %collective-permute-done.9.refs_1_ = bf16[4,512,128]{2,1,0:T(8,128)(2,1)S(1)} collective-permute-done((bf16[4,512,128]{2,1,0:T(8,128)(2,1)}, bf16[4,512,128]{2,1,0:T(8,128)(2,1)S(1)}, u32[]{:S(2)}, u32[]{:S(2)}) %collective-permute-start.9) | collective-permute-done | bytes 524320 | tf_op jit(solution)/shard_map/ppermute | solution.py:26
  48.3 1.7 %stacked_gram.3 = (bf16[512,512]{1,0:T(8,128)(2,1)}, bf16[128,1280]{1,0:T(8,128)(2,1)S(1)}) custom-call(f32[4,512]{1,0:T(4,128)S(1)} %add.43.squares_ref, bf16[4,512,128]{2,1,0:T(8,128)(2,1)S(1)} %get-tuple-element.26.refs_0_, bf16[4,512,128]{2,1,0:T(8,128)(2,1)S(1)} %collective-permute-done.9.refs_1_), custom_call_target="tpu_custom_call" | custom-call | tf_op jit(solution)/shard_map/stacked_gram/pallas_call | solution.py:197
  50.0 1.8 %collective-permute-start.10 = (bf16[64,1280]{1,0:T(8,128)(2,1)S(1)}, bf16[64,1280]{1,0:T(8,128)(2,1)S(1)}, u32[]{:S(2)}, u32[]{:S(2)}) collective-permute-start(bf16[64,1280]{1,0:T(8,128)(2,1)S(1)} %constant_dynamic-slice_fusion), channel_id=1, source_target_pairs={{0,4},{4,0},{8,12},{12,8},{16,20},{20,16},{24,28},{28,24},{1,5},{5... | collective-permute-start | bytes 491528 | tf_op jit(solution)/shard_map/ppermute | solution.py:26
  51.8 0.0 collective-permute-done.3
  51.9 1.6 %collective-permute-start.4 = (bf16[32,1280]{1,0:T(8,128)(2,1)S(1)}, bf16[32,1280]{1,0:T(8,128)(2,1)S(1)}, u32[]{:S(2)}, u32[]{:S(2)}) collective-permute-start(bf16[32,1280]{1,0:T(8,128)(2,1)S(1)} %dynamic-slice_convert_fusion.1), channel_id=1, source_target_pairs={{0,8},{4,12},{8,0},{12,4},{16,24},{20,28},{24,16},{28,20},{1,9},{5... | collective-permute-start | bytes 245768 | tf_op jit(solution)/shard_map/ppermute | solution.py:26
  53.5 2.2 %collective-permute-done.10 = bf16[64,1280]{1,0:T(8,128)(2,1)S(1)} collective-permute-done((bf16[64,1280]{1,0:T(8,128)(2,1)S(1)}, bf16[64,1280]{1,0:T(8,128)(2,1)S(1)}, u32[]{:S(2)}, u32[]{:S(2)}) %collective-permute-start.10) | collective-permute-done | bytes 163872 | tf_op jit(solution)/shard_map/ppermute | solution.py:26
  55.8 1.6 %collective-permute-start.11 = (bf16[32,1280]{1,0:T(8,128)(2,1)S(1)}, bf16[32,1280]{1,0:T(8,128)(2,1)S(1)}, u32[]{:S(2)}, u32[]{:S(2)}) collective-permute-start(bf16[32,1280]{1,0:T(8,128)(2,1)S(1)} %dynamic-slice_convert_fusion), channel_id=1, source_target_pairs={{0,8},{4,12},{8,0},{12,4},{16,24},{20,28},{24,16},{28,20},{1,9},{5... | collective-permute-start | bytes 245768 | tf_op jit(solution)/shard_map/ppermute | solution.py:26
  57.4 0.0 collective-permute-done.4
  57.4 2.6 %collective-permute-start.5 = (bf16[32,1280]{1,0:T(8,128)(2,1)S(1)}, bf16[32,1280]{1,0:T(8,128)(2,1)S(1)}, u32[]{:S(2)}, u32[]{:S(2)}) collective-permute-start(bf16[32,1280]{1,0:T(8,128)(2,1)S(1)} %add_convert_fusion.3), channel_id=1, source_target_pairs={{0,16},{4,20},{8,24},{12,28},{16,0},{20,4},{24,8},{28,12},{1,17},{... | collective-permute-start | bytes 245768 | tf_op jit(solution)/shard_map/ppermute | solution.py:26
  60.1 0.6 collective-permute-done.11
  60.7 2.5 %collective-permute-start.12 = (bf16[32,1280]{1,0:T(8,128)(2,1)S(1)}, bf16[32,1280]{1,0:T(8,128)(2,1)S(1)}, u32[]{:S(2)}, u32[]{:S(2)}) collective-permute-start(bf16[32,1280]{1,0:T(8,128)(2,1)S(1)} %add_convert_fusion.1), channel_id=1, source_target_pairs={{0,16},{4,20},{8,24},{12,28},{16,0},{20,4},{24,8},{28,12},{1,17},{... | collective-permute-start | bytes 245768 | tf_op jit(solution)/shard_map/ppermute | solution.py:26
  63.2 1.9 %collective-permute-done.5 = bf16[32,1280]{1,0:T(8,128)(2,1)S(1)} collective-permute-done((bf16[32,1280]{1,0:T(8,128)(2,1)S(1)}, bf16[32,1280]{1,0:T(8,128)(2,1)S(1)}, u32[]{:S(2)}, u32[]{:S(2)}) %collective-permute-start.5) | collective-permute-done | bytes 81952 | tf_op jit(solution)/shard_map/ppermute | solution.py:26
  65.1 0.1 collective-permute-start.6
  65.2 0.9 collective-permute-done.12
  66.1 1.9 %collective-permute-start.13 = (bf16[32,1280]{1,0:T(8,128)(2,1)S(1)}, bf16[32,1280]{1,0:T(8,128)(2,1)S(1)}, u32[]{:S(2)}, u32[]{:S(2)}) collective-permute-start(bf16[32,1280]{1,0:T(8,128)(2,1)S(1)} %add_convert_fusion), channel_id=1, source_target_pairs={{0,8},{4,12},{8,0},{12,4},{16,24},{20,28},{24,16},{28,20},{1,9},{5... | collective-permute-start | bytes 245768 | tf_op jit(solution)/shard_map/ppermute | solution.py:26
  68.0 1.6 %collective-permute-done.6 = bf16[32,1280]{1,0:T(8,128)(2,1)S(1)} collective-permute-done((bf16[32,1280]{1,0:T(8,128)(2,1)S(1)}, bf16[32,1280]{1,0:T(8,128)(2,1)S(1)}, u32[]{:S(2)}, u32[]{:S(2)}) %collective-permute-start.6) | collective-permute-done | bytes 81952 | tf_op jit(solution)/shard_map/ppermute | solution.py:26
  69.7 1.6 %collective-permute-start.7 = (bf16[64,1280]{1,0:T(8,128)(2,1)S(1)}, bf16[64,1280]{1,0:T(8,128)(2,1)S(1)}, u32[]{:S(2)}, u32[]{:S(2)}) collective-permute-start(bf16[64,1280]{1,0:T(8,128)(2,1)S(1)} %pad_maximum_fusion.2), channel_id=1, source_target_pairs={{0,4},{4,0},{8,12},{12,8},{16,20},{20,16},{24,28},{28,24},{1,5},{5... | collective-permute-start | bytes 491528 | tf_op jit(solution)/shard_map/ppermute | solution.py:26
  71.3 0.0 collective-permute-done.13
  71.3 1.0 %collective-permute-start.14 = (bf16[64,1280]{1,0:T(8,128)(2,1)S(1)}, bf16[64,1280]{1,0:T(8,128)(2,1)S(1)}, u32[]{:S(2)}, u32[]{:S(2)}) collective-permute-start(bf16[64,1280]{1,0:T(8,128)(2,1)S(1)} %pad_maximum_fusion.3), channel_id=1, source_target_pairs={{0,4},{4,0},{8,12},{12,8},{16,20},{20,16},{24,28},{28,24},{1,5},{5... | collective-permute-start | bytes 491528 | tf_op jit(solution)/shard_map/ppermute | solution.py:26
  72.3 0.0 copy-done
  72.3 2.8 %collective-permute-done.7 = bf16[64,1280]{1,0:T(8,128)(2,1)S(1)} collective-permute-done((bf16[64,1280]{1,0:T(8,128)(2,1)S(1)}, bf16[64,1280]{1,0:T(8,128)(2,1)S(1)}, u32[]{:S(2)}, u32[]{:S(2)}) %collective-permute-start.7) | collective-permute-done | bytes 163872 | tf_op jit(solution)/shard_map/ppermute | solution.py:26
  75.1 1.8 %collective-permute-done.14 = bf16[64,1280]{1,0:T(8,128)(2,1)S(1)} collective-permute-done((bf16[64,1280]{1,0:T(8,128)(2,1)S(1)}, bf16[64,1280]{1,0:T(8,128)(2,1)S(1)}, u32[]{:S(2)}, u32[]{:S(2)}) %collective-permute-start.14) | collective-permute-done | bytes 163872 | tf_op jit(solution)/shard_map/ppermute | solution.py:26
  76.8 0.1 broadcast_select_fusion.1
  77.0 14.5 %basis_latents.1 = bf16[512,2,128]{2,1,0:T(2,128)(2,1)} custom-call(bf16[2,512,128]{2,1,0:T(8,128)(2,1)S(1)} %constant_dynamic-slice_fusion.2.start_ref, bf16[128,1280]{1,0:T(8,128)(2,1)S(1)} %pad_maximum_fusion.refs_0_, bf16[128,1280]{1,0:T(8,128)(2,1)S(1)} %pad_maximum_fusion.1.refs_1_, bf16[512,512]{1,0:T(8,128)(2,1)} %get-tuple-element.29.refs_2_, ...), custom_call_target="tpu_custom_call" | custom-call | tf_op jit(solution)/shard_map/basis_latents/pallas_call | solution.py:346
  (22 shorter events, 0.4 us)
Async XLA Ops:
  0.0 72.3 %copy-start = (bf16[8,512,128]{2,1,0:T(8,128)(2,1)S(1)}, bf16[8,512,128]{2,1,0:T(8,128)(2,1)}, u32[]{:S(2)}) copy-start(bf16[8,512,128]{2,1,0:T(8,128)(2,1)} %param.7) | copy-start | bytes 3145732
  0.0 0.8 copy-start.1
  16.1 4.3 %collective-permute-start.1 = (bf16[4,512,256]{2,1,0:T(8,128)(2,1)S(1)}, bf16[4,512,256]{2,1,0:T(8,128)(2,1)S(1)}, u32[]{:S(2)}, u32[]{:S(2)}) collective-permute-start(bf16[4,512,256]{2,1,0:T(8,128)(2,1)S(1)} %get-tuple-element.20), channel_id=1, source_target_pairs={{0,1},{1,0},{2,3},{3,2},{4,5},{5,4},{6,7},{7,6},{8,9},{9,8},{10,11... | collective-permute-start | bytes 3145736 | tf_op jit(solution)/shard_map/ppermute | solution.py:26
  16.6 7.7 %collective-permute-start.8 = (bf16[4,512,256]{2,1,0:T(8,128)(2,1)S(1)}, bf16[4,512,256]{2,1,0:T(8,128)(2,1)S(1)}, u32[]{:S(2)}, u32[]{:S(2)}) collective-permute-start(bf16[4,512,256]{2,1,0:T(8,128)(2,1)S(1)} %get-tuple-element.25), channel_id=1, source_target_pairs={{0,1},{1,0},{2,3},{3,2},{4,5},{5,4},{6,7},{7,6},{8,9},{9,8},{10,11... | collective-permute-start | bytes 3145736 | tf_op jit(solution)/shard_map/ppermute | solution.py:26
  16.7 3.7 %collective-permute-start = (f32[4,512]{1,0:T(4,128)S(1)}, f32[4,512]{1,0:T(4,128)S(1)}, u32[]{:S(2)}, u32[]{:S(2)}) collective-permute-start(f32[4,512]{1,0:T(4,128)S(1)} %get-tuple-element.18), channel_id=1, source_target_pairs={{0,1},{1,0},{2,3},{3,2},{4,5},{5,4},{6,7},{7,6},{8,9},{9,8},{10,11... | collective-permute-start | bytes 24584 | tf_op jit(solution)/shard_map/ppermute | solution.py:26
  21.4 16.1 %collective-permute-start.2 = (bf16[4,528,128]{2,1,0:T(8,128)(2,1)}, bf16[4,528,128]{2,1,0:T(8,128)(2,1)S(1)}, u32[]{:S(2)}, u32[]{:S(2)}) collective-permute-start(bf16[4,528,128]{2,1,0:T(8,128)(2,1)} %get-tuple-element.21), channel_id=1, source_target_pairs={{0,2},{1,3},{2,0},{3,1},{4,6},{5,7},{6,4},{7,5},{8,10},{9,11},{10,... | collective-permute-start | bytes 1622024 | tf_op jit(solution)/shard_map/ppermute | solution.py:26
  25.4 22.9 %collective-permute-start.9 = (bf16[4,512,128]{2,1,0:T(8,128)(2,1)}, bf16[4,512,128]{2,1,0:T(8,128)(2,1)S(1)}, u32[]{:S(2)}, u32[]{:S(2)}) collective-permute-start(bf16[4,512,128]{2,1,0:T(8,128)(2,1)} %get-tuple-element.27), channel_id=1, source_target_pairs={{0,2},{1,3},{2,0},{3,1},{4,6},{5,7},{6,4},{7,5},{8,10},{9,11},{10,... | collective-permute-start | bytes 1572872 | tf_op jit(solution)/shard_map/ppermute | solution.py:26
  39.1 12.7 %collective-permute-start.3 = (bf16[64,1280]{1,0:T(8,128)(2,1)S(1)}, bf16[64,1280]{1,0:T(8,128)(2,1)S(1)}, u32[]{:S(2)}, u32[]{:S(2)}) collective-permute-start(bf16[64,1280]{1,0:T(8,128)(2,1)S(1)} %constant_dynamic-slice_fusion.1), channel_id=1, source_target_pairs={{0,4},{4,0},{8,12},{12,8},{16,20},{20,16},{24,28},{28,24},{1,5},{5... | collective-permute-start | bytes 491528 | tf_op jit(solution)/shard_map/ppermute | solution.py:26
  50.0 5.8 %collective-permute-start.10 = (bf16[64,1280]{1,0:T(8,128)(2,1)S(1)}, bf16[64,1280]{1,0:T(8,128)(2,1)S(1)}, u32[]{:S(2)}, u32[]{:S(2)}) collective-permute-start(bf16[64,1280]{1,0:T(8,128)(2,1)S(1)} %constant_dynamic-slice_fusion), channel_id=1, source_target_pairs={{0,4},{4,0},{8,12},{12,8},{16,20},{20,16},{24,28},{28,24},{1,5},{5... | collective-permute-start | bytes 491528 | tf_op jit(solution)/shard_map/ppermute | solution.py:26
  51.9 5.5 %collective-permute-start.4 = (bf16[32,1280]{1,0:T(8,128)(2,1)S(1)}, bf16[32,1280]{1,0:T(8,128)(2,1)S(1)}, u32[]{:S(2)}, u32[]{:S(2)}) collective-permute-start(bf16[32,1280]{1,0:T(8,128)(2,1)S(1)} %dynamic-slice_convert_fusion.1), channel_id=1, source_target_pairs={{0,8},{4,12},{8,0},{12,4},{16,24},{20,28},{24,16},{28,20},{1,9},{5... | collective-permute-start | bytes 245768 | tf_op jit(solution)/shard_map/ppermute | solution.py:26
  55.8 4.9 %collective-permute-start.11 = (bf16[32,1280]{1,0:T(8,128)(2,1)S(1)}, bf16[32,1280]{1,0:T(8,128)(2,1)S(1)}, u32[]{:S(2)}, u32[]{:S(2)}) collective-permute-start(bf16[32,1280]{1,0:T(8,128)(2,1)S(1)} %dynamic-slice_convert_fusion), channel_id=1, source_target_pairs={{0,8},{4,12},{8,0},{12,4},{16,24},{20,28},{24,16},{28,20},{1,9},{5... | collective-permute-start | bytes 245768 | tf_op jit(solution)/shard_map/ppermute | solution.py:26
  57.4 7.7 %collective-permute-start.5 = (bf16[32,1280]{1,0:T(8,128)(2,1)S(1)}, bf16[32,1280]{1,0:T(8,128)(2,1)S(1)}, u32[]{:S(2)}, u32[]{:S(2)}) collective-permute-start(bf16[32,1280]{1,0:T(8,128)(2,1)S(1)} %add_convert_fusion.3), channel_id=1, source_target_pairs={{0,16},{4,20},{8,24},{12,28},{16,0},{20,4},{24,8},{28,12},{1,17},{... | collective-permute-start | bytes 245768 | tf_op jit(solution)/shard_map/ppermute | solution.py:26
  60.7 5.4 %collective-permute-start.12 = (bf16[32,1280]{1,0:T(8,128)(2,1)S(1)}, bf16[32,1280]{1,0:T(8,128)(2,1)S(1)}, u32[]{:S(2)}, u32[]{:S(2)}) collective-permute-start(bf16[32,1280]{1,0:T(8,128)(2,1)S(1)} %add_convert_fusion.1), channel_id=1, source_target_pairs={{0,16},{4,20},{8,24},{12,28},{16,0},{20,4},{24,8},{28,12},{1,17},{... | collective-permute-start | bytes 245768 | tf_op jit(solution)/shard_map/ppermute | solution.py:26
  65.1 4.5 %collective-permute-start.6 = (bf16[32,1280]{1,0:T(8,128)(2,1)S(1)}, bf16[32,1280]{1,0:T(8,128)(2,1)S(1)}, u32[]{:S(2)}, u32[]{:S(2)}) collective-permute-start(bf16[32,1280]{1,0:T(8,128)(2,1)S(1)} %add_convert_fusion.2), channel_id=1, source_target_pairs={{0,8},{4,12},{8,0},{12,4},{16,24},{20,28},{24,16},{28,20},{1,9},{5... | collective-permute-start | bytes 245768 | tf_op jit(solution)/shard_map/ppermute | solution.py:26
  66.1 5.1 %collective-permute-start.13 = (bf16[32,1280]{1,0:T(8,128)(2,1)S(1)}, bf16[32,1280]{1,0:T(8,128)(2,1)S(1)}, u32[]{:S(2)}, u32[]{:S(2)}) collective-permute-start(bf16[32,1280]{1,0:T(8,128)(2,1)S(1)} %add_convert_fusion), channel_id=1, source_target_pairs={{0,8},{4,12},{8,0},{12,4},{16,24},{20,28},{24,16},{28,20},{1,9},{5... | collective-permute-start | bytes 245768 | tf_op jit(solution)/shard_map/ppermute | solution.py:26
  69.7 5.4 %collective-permute-start.7 = (bf16[64,1280]{1,0:T(8,128)(2,1)S(1)}, bf16[64,1280]{1,0:T(8,128)(2,1)S(1)}, u32[]{:S(2)}, u32[]{:S(2)}) collective-permute-start(bf16[64,1280]{1,0:T(8,128)(2,1)S(1)} %pad_maximum_fusion.2), channel_id=1, source_target_pairs={{0,4},{4,0},{8,12},{12,8},{16,20},{20,16},{24,28},{28,24},{1,5},{5... | collective-permute-start | bytes 491528 | tf_op jit(solution)/shard_map/ppermute | solution.py:26
  71.3 5.5 %collective-permute-start.14 = (bf16[64,1280]{1,0:T(8,128)(2,1)S(1)}, bf16[64,1280]{1,0:T(8,128)(2,1)S(1)}, u32[]{:S(2)}, u32[]{:S(2)}) collective-permute-start(bf16[64,1280]{1,0:T(8,128)(2,1)S(1)} %pad_maximum_fusion.3), channel_id=1, source_target_pairs={{0,4},{4,0},{8,12},{12,8},{16,20},{20,16},{24,28},{28,24},{1,5},{5... | collective-permute-start | bytes 491528 | tf_op jit(solution)/shard_map/ppermute | solution.py:26

commit v3 on v2

v3 whole, which is shorter than its diff:
```python
import functools

import jax
import jax.numpy as jnp
from jax import lax
from jax.experimental import pallas as pl
from jax.experimental.pallas import tpu as pltpu
from jax.sharding import PartitionSpec as P

HD = 128
ITERS = 2
EPSILON = 1e-05
F32 = jnp.float32
BF16 = jnp.bfloat16
HIGHEST = lax.Precision.HIGHEST
MIB = 1 << 20
LEAD = 0


def halving_order(count):
    bits = count.bit_length() - 1
    return sorted(range(count), key=lambda r: int(format(r, f"0{bits}b")[::-1], 2)) if bits else [0]


def exchange(x, axis, bit):
    size = lax.axis_size(axis)
    return lax.ppermute(x, axis, [(j, j ^ bit) for j in range(size)])


def partial_kernel(own, slot, cuts, with_squares, m_ref, gain_ref, hid_ref, w_ref, *refs):
    rows_ref, cols_ref, sems = refs[-3:]
    layers, tokens, width = rows_ref.shape
    mp = cols_ref.shape[2] // HD
    order = halving_order(mp)
    send = [(ref, i) for ref, count in zip(refs[1:], cuts) for i in range(count)]
    copies = {}
    for layer in range(layers):
        here = [pltpu.make_async_copy(hid_ref.at[layer], rows_ref.at[layer], sems.at[layer, 0])]
        for i, r in enumerate(order):
            column = pl.multiple_of((own * (m_ref[0] ^ r) + slot) * HD, HD)
            here.append(
                pltpu.make_async_copy(
                    w_ref.at[layer, :, pl.ds(column, HD)],
                    cols_ref.at[layer, :, pl.ds(i * HD, HD)],
                    sems.at[layer, 1 + i],
                )
            )
        for copy in here:
            copy.start()
        copies[layer] = here
    half = mp // 2 * HD
    gains = gain_ref[...]
    for layer in range(layers):
        copies[layer][0].wait()
        rows = rows_ref[layer]
        scaled = rows * gains[layer : layer + 1]
        for copy in copies[layer][1:]:
            copy.wait()
        total = jnp.dot(scaled, cols_ref[layer], preferred_element_type=F32)
        refs[0][layer] = total[:, :half].astype(BF16)
        ref, i = send[layer]
        ref[i] = total[:, half:].astype(BF16)
        if not with_squares:
            continue
        wide = rows.astype(F32)
        squares = None
        for i in range(width // HD):
            x = wide[:, i * HD : (i + 1) * HD]
            squares = x * x if squares is None else squares + x * x
        refs[1 + len(cuts)][layer : layer + 1, :] = lax.dot_general(
            jnp.ones((8, HD), F32),
            squares,
            (((1,), (1,)), ((), ())),
            precision=HIGHEST,
            preferred_element_type=F32,
        )[:1]


def partial_products(hidden, gains, weights, me, own, slot, cuts, with_squares):
    layers, tokens, width = hidden.shape
    mp = lax.axis_size("mp")
    half = mp // 2 * HD
    outs = [jax.ShapeDtypeStruct((n, tokens, half), BF16) for n in [layers] + cuts]
    outs += [jax.ShapeDtypeStruct((layers, tokens), F32)] * with_squares
    vmem = pl.BlockSpec(memory_space=pltpu.VMEM)
    hbm = pl.BlockSpec(memory_space=pltpu.HBM)
    return pl.pallas_call(
        functools.partial(partial_kernel, own, slot, cuts, with_squares),
        out_shape=outs,
        in_specs=[pl.BlockSpec(memory_space=pltpu.SMEM), vmem, hbm, hbm],
        out_specs=[vmem] * len(outs),
        scratch_shapes=[
            pltpu.VMEM((layers, tokens, width), BF16),
            pltpu.VMEM((layers, width, mp * HD), BF16),
            pltpu.SemaphoreType.DMA((layers, mp + 1)),
        ],
        compiler_params=pltpu.CompilerParams(vmem_limit_bytes=32 * MIB),
        cost_estimate=pl.CostEstimate(
            flops=2 * layers * tokens * width * mp * HD,
            bytes_accessed=layers * width * (tokens + mp * HD) * 2,
            transcendentals=0,
        ),
        name="partial_products",
    )(me, gains, *[pltpu.with_memory_space_constraint(x, pltpu.HBM) for x in (hidden, weights)])


def extra_rows(tokens):
    return -(-3 * (tokens // HD) // 16) * 16


def by_layer(groups, refs):
    parts, at = [], 0
    for counts in groups:
        parts.append([refs[at + n].at[i] for n, count in enumerate(counts) for i in range(count)])
        at += len(counts)
    return parts, at


def merge_kernel(groups, tokens, cuts, with_totals, *refs):
    own_ref, out_refs = refs[-1 - len(cuts)], refs[-len(cuts) :]
    layers, _, half = own_ref.shape
    out = [(ref, i) for ref, count in zip(out_refs, cuts) for i in range(count)]
    parts, at = by_layer(groups, refs)
    for layer in range(layers):
        total = sum(p[layer][...].astype(F32) for p in parts)
        own_ref[layer] = total[:, :half].astype(BF16)
        ref, i = out[layer]
        ref[i, :tokens, :] = total[:, half:].astype(BF16)
    if with_totals:
        totals = refs[at][...]
        pieces_of = tokens // HD
        rows = out_refs[0].shape[1] - tokens
        for layer in range(layers):
            line = jnp.concatenate(
                [totals[layer : layer + 1, i * HD : (i + 1) * HD] for i in range(pieces_of)], axis=0
            )
            pieces = [p.astype(F32) for p in split3(line)]
            pad = [jnp.zeros((rows - 3 * pieces_of, HD), F32)] if rows > 3 * pieces_of else []
            ref, i = out[layer]
            ref[i, tokens:, :HD] = jnp.concatenate(pieces + pad, axis=0).astype(BF16)
            if half > HD:
                ref[i, tokens:, HD:] = jnp.zeros((rows, half - HD), BF16)


def next_send(pieces, totals, tokens, cuts):
    groups = [[a.shape[0] for a in group] for group in pieces]
    arrays = [a for group in pieces for a in group]
    layers, width = sum(groups[0]), arrays[0].shape[2]
    half = width // 2
    rows = tokens + (extra_rows(tokens) if totals is not None else 0)
    extra = [] if totals is None else [totals]
    block = lambda *shape: pl.BlockSpec(shape, lambda i: (0,) * len(shape))
    return pl.pallas_call(
        functools.partial(merge_kernel, groups, tokens, cuts, totals is not None),
        out_shape=[jax.ShapeDtypeStruct((layers, tokens, half), BF16)]
        + [jax.ShapeDtypeStruct((count, rows, half), BF16) for count in cuts],
        grid=(1,),
        in_specs=[block(a.shape[0], tokens, width) for a in arrays] + [block(*t.shape) for t in extra],
        out_specs=[block(layers, tokens, half)] + [block(count, rows, half) for count in cuts],
        compiler_params=pltpu.CompilerParams(vmem_limit_bytes=16 * MIB),
        name="next_send",
    )(*arrays, *extra)


def carried_totals(received, tokens):
    cuts = tokens // HD
    pieces = received[:, tokens : tokens + 3 * cuts, :HD].astype(F32)
    return pieces.reshape(-1, 3, tokens).sum(1)


def gram_kernel(groups, width, squares_ref, *refs):
    stacked_ref, gram_ref = refs[-2:]
    layers = squares_ref.shape[0]
    factor = lax.rsqrt(squares_ref[...] / width + EPSILON)
    factor = jnp.transpose(jnp.concatenate([factor] * (8 // layers), axis=0))
    parts, _ = by_layer(groups, refs)
    blocks = []
    for layer in range(layers):
        total = sum(p[layer][...].astype(F32) for p in parts)
        blocks.append((total * factor[:, layer : layer + 1]).astype(BF16))
    stacked = jnp.concatenate(blocks, axis=1)
    stacked_ref[...] = stacked
    column = 0
    for i, block in enumerate(blocks):
        upto = (i + 1) * HD
        gram_ref[:, column : column + upto] = lax.dot_general(
            block, stacked[:, :upto], (((0,), (0,)), ((), ())), preferred_element_type=F32
        ).astype(BF16)
        column += upto


def stacked_and_gram(pieces, squares, width):
    layers, tokens = squares.shape
    groups = [[a.shape[0] for a in group] for group in pieces]
    arrays = [a for group in pieces for a in group]
    packed = layers * (layers + 1) // 2 * HD
    return pl.pallas_call(
        functools.partial(gram_kernel, groups, width),
        out_shape=[
            pltpu.HBM((tokens, layers * HD), BF16),
            jax.ShapeDtypeStruct((HD, packed), BF16),
        ],
        grid=(1,),
        in_specs=[pl.BlockSpec(squares.shape, lambda i: (0, 0))]
        + [pl.BlockSpec((a.shape[0], tokens, HD), lambda i: (0, 0, 0)) for a in arrays],
        out_specs=[
            pl.BlockSpec((tokens, layers * HD), lambda i: (0, 0)),
            pl.BlockSpec((HD, packed), lambda i: (0, 0)),
        ],
        compiler_params=pltpu.CompilerParams(vmem_limit_bytes=16 * MIB),
        name="stacked_gram",
    )(squares, *arrays)


def sum_over_seq(x, ahead):
    size = lax.axis_size("seq")
    me = lax.axis_index("seq")
    bits = [1 << i for i in range(size.bit_length() - 1)]
    arrived = []

    def step(send, bit):
        if len(arrived) + LEAD < len(ahead) - 1:
            send = lax.optimization_barrier((send, ahead[len(arrived) + LEAD]))[0]
        arrived.append(exchange(send, "seq", bit))
        return arrived[-1]

    for bit in bits[:-1]:
        half = x.shape[0] // 2
        mine = jnp.where((me & bit) != 0, half, 0)
        got = step(lax.dynamic_slice_in_dim(x, half - mine, half, 0).astype(BF16), bit)
        x = lax.dynamic_slice_in_dim(x, mine, half, 0).astype(F32) + got.astype(F32)
    x = x.astype(BF16)
    x = (x.astype(F32) + step(x, bits[-1]).astype(F32)).astype(BF16)
    for bit in bits[:-1][::-1]:
        got = step(x, bit)
        upper = (me & bit) != 0
        x = jnp.concatenate([jnp.where(upper, got, x), jnp.where(upper, x, got)], axis=0)
    return x, arrived


def split3(x):
    high = x.astype(BF16)
    rest = x - high.astype(F32)
    middle = rest.astype(BF16)
    return high, middle, (rest - middle.astype(F32)).astype(BF16)


def rank_update(x):
    h, m, l = split3(x)
    left = jnp.concatenate([h, h, m, h, m, l], axis=0)
    right = jnp.concatenate([h, m, h, l, m, h], axis=0)
    return lax.dot_general(left, right, (((0,), (0,)), ((), ())), preferred_element_type=F32)


def reciprocal(d):
    r = pl.reciprocal(d, approx=True)
    return r * (2.0 - d * r)


def factor_panel(rows, base):
    b, n = rows.shape
    lane = lax.broadcasted_iota(jnp.int32, (8, n), 1)
    row = lax.broadcasted_iota(jnp.int32, (8, n), 0)

    def spread(x, k):
        return jnp.broadcast_to(x[k : k + 1, :], (8, n))

    tiles = [rows[i : i + 8] for i in range(0, b, 8)]
    columns = [[jnp.broadcast_to(t[:, base + j : base + j + 1], (8, n)) for t in tiles] for j in range(b)]
    pivots = [jnp.zeros((8, n), F32) for _ in tiles]
    for k in range(b):
        top, at = k // 8, k % 8
        pivot = spread(columns[k][top], at)
        pivots[top] = jnp.where(row == at, pivot, pivots[top])
        here = lane == base + k
        tiles[top] = jnp.where(here & (row >= at), jnp.where(row == at, 1.0, 0.0), tiles[top])
        if k == b - 1:
            break
        inverse = reciprocal(pivot)
        chosen = spread(tiles[top], at)
        others = [spread(columns[j][top], at) for j in range(k + 1, b)]
        for i in range(top, len(tiles)):
            multiplier = columns[k][i] * inverse
            if i == top:
                multiplier = jnp.where(row > at, multiplier, 0.0)
            else:
                tiles[i] = jnp.where(here, 0.0, tiles[i])
            tiles[i] = tiles[i] - multiplier * chosen
            for j in range(k + 1, b):
                columns[j][i] = columns[j][i] - multiplier * others[j - k - 1]
    for i in range(len(tiles)):
        tiles[i] = jnp.where((lane > base + 8 * i + row) & (lane < base + b), 0.0, tiles[i])
        tiles[i] = tiles[i] * lax.rsqrt(pivots[i])
    return jnp.concatenate(tiles, axis=0)


def inverse_cholesky(matrices, b=16):
    n = matrices[0].shape[0]
    panels = [[] for _ in matrices]
    rests = list(matrices)
    lane = lax.broadcasted_iota(jnp.int32, (n, n), 1)
    row = lax.broadcasted_iota(jnp.int32, (n, n), 0)
    for base in range(0, n, b):
        for s, rest in enumerate(rests):
            panels[s].append(factor_panel(rest[:b], base))
        if base + b < n:
            for s, rest in enumerate(rests):
                update = rank_update(panels[s][-1])[base + b :]
                rest = rest[b:]
                at = lane[: rest.shape[0]]
                rests[s] = jnp.where((at >= base) & (at < base + b), 0.0, rest) - update
    return [jnp.where(lane <= row, jnp.concatenate(p, axis=0), 0.0) for p in panels]


def basis_kernel(own, layers, start_ref, *refs):
    gram_refs, stacked_refs, out_ref = refs[:own], refs[own : 2 * own], refs[2 * own]
    rows_ref, sems = refs[2 * own + 1 :]
    copies = [pltpu.make_async_copy(stacked_refs[s], rows_ref.at[s], sems.at[s]) for s in range(own)]
    for copy in copies:
        copy.start()
    grams = []
    for ref in gram_refs:
        block = {}
        column = 0
        for i in range(layers):
            for j in range(i + 1):
                block[i, j] = ref[:, column : column + HD]
                column += HD
        rows = []
        for i in range(layers):
            rows.append(
                jnp.concatenate(
                    [
                        block[i, j] if j <= i else jnp.transpose(block[j, i].astype(F32)).astype(BF16)
                        for j in range(layers)
                    ],
                    axis=1,
                )
            )
        grams.append(jnp.concatenate(rows, axis=0))
    rank = start_ref.shape[1]

    def through_gram(x, gram):
        y = jnp.dot(jnp.concatenate(split3(x), axis=0), gram, preferred_element_type=F32)
        return y[:rank] + y[rank : 2 * rank] + y[2 * rank :]

    images = [jnp.dot(start_ref[s], grams[s], preferred_element_type=F32) for s in range(own)]
    for step in range(ITERS):
        inner = [
            lax.dot_general(x, x, (((1,), (1,)), ((), ())), precision=HIGHEST, preferred_element_type=F32)
            for x in images
        ]
        if step < ITERS - 1:
            images = [through_gram(x, g) for x, g in zip(images, grams)]
        images = [
            jnp.dot(f, x, precision=HIGHEST, preferred_element_type=F32)
            for x, f in zip(images, inverse_cholesky(inner))
        ]
    for s in range(own):
        copies[s].wait()
        out_ref[:, s, :] = lax.dot_general(
            rows_ref[s], images[s].astype(BF16), (((1,), (1,)), ((), ())), preferred_element_type=F32
        ).astype(BF16)


def latents_of(start, grams, stacked):
    own = len(grams)
    tokens = stacked[0].shape[0]
    layers = stacked[0].shape[1] // HD
    whole = lambda a: pl.BlockSpec(a.shape, lambda i: (0,) * a.ndim)
    return pl.pallas_call(
        functools.partial(basis_kernel, own, layers),
        out_shape=jax.ShapeDtypeStruct((tokens, own, HD), BF16),
        grid=(1,),
        in_specs=[whole(a) for a in [start] + grams] + [pl.BlockSpec(memory_space=pltpu.HBM)] * own,
        out_specs=pl.BlockSpec((tokens, own, HD), lambda i: (0, 0, 0)),
        scratch_shapes=[pltpu.VMEM((own,) + stacked[0].shape, BF16), pltpu.SemaphoreType.DMA((own,))],
        compiler_params=pltpu.CompilerParams(vmem_limit_bytes=16 * MIB),
        name="basis_latents",
    )(start, *grams, *[pltpu.with_memory_space_constraint(x, pltpu.HBM) for x in stacked])


def on_device(hidden, norm_gain, proj_weight, start_block):
    layers, tokens, width = hidden.shape
    mp = lax.axis_size("mp")
    own = proj_weight.shape[2] // HD // mp
    me = lax.axis_index("mp").astype(jnp.int32).reshape(1)
    mp_bits = [1 << i for i in range(mp.bit_length() - 1)]

    pieces, totals, sent = [], None, []
    for slot in range(own):
        here = me if slot == 0 else lax.optimization_barrier((me, sent[-1]))[0]
        cuts = [layers] if slot == 0 else [layers // 2, layers - layers // 2]
        held, *sent = partial_products(hidden, norm_gain, proj_weight, here, own, slot, cuts, slot == 0)
        if slot == 0:
            totals = sent.pop()
            totals = totals + exchange(totals, "mp", 1)
        got = [exchange(send, "mp", 1) for send in sent]
        for bit in mp_bits[1:]:
            cuts = [layers] if slot == 0 or bit != mp_bits[-1] else [layers // 2, layers - layers // 2]
            arrays = [[held], got]
            if slot:
                arrays = lax.optimization_barrier((arrays, pieces[slot - 1][-1]))[0]
            held, *sent = next_send(arrays, totals if slot == 0 else None, tokens, cuts)
            got = [exchange(send, "mp", bit) for send in sent]
            if slot == 0:
                totals = totals + carried_totals(got[0], tokens)
        pieces.append([[held], got])

    grams, stacked, arrived = [], [], []
    for slot in range(own):
        later = slot + 1 < own
        if later:
            totals = lax.optimization_barrier((totals, pieces[slot + 1][0]))[0]
        rows, gram = stacked_and_gram(pieces[slot], totals, width * mp)
        stacked.append(rows)
        if later:
            gram = lax.optimization_barrier((gram, pieces[slot + 1][1][0]))[0]
        gram, arrived = sum_over_seq(gram, arrived)
        grams.append(gram)
    start = jnp.swapaxes(lax.dynamic_slice_in_dim(start_block, me[0] * own, own, 0), 1, 2)
    return latents_of(start, grams, stacked)


def solution(mesh):
    return jax.shard_map(
        on_device,
        mesh=mesh,
        in_specs=(P(None, "seq", "mp"), P(None, "mp"), P(None, "mp", None), P()),
        out_specs=P("seq", "mp", None),
        check_vma=False,
    )
```

time: 91.8 us -> 87.5 us (0.953)
  waiting for transfers between devices: 34.2 us -> 25.4 us
  starting transfers between devices: 20.8 us -> 24.9 us
    ppermute x15 -> x17, waiting for transfers between devices: 34.2 us -> 25.4 us  [exchange(): return lax.ppermute(x, axis, [(j, j ^ bit) for j in range(size)])]
    ppermute x15 -> x17, starting transfers between devices: 20.8 us -> 24.9 us  [exchange(): return lax.ppermute(x, axis, [(j, j ^ bit) for j in range(size)])]
    pallas_call x5 -> x6, Pallas kernels: 20.5 us -> 22.3 us  [the longest x2 18.1 us: partial_products(): pl.pallas_call(functools.partial(partial_kernel, own, slot, cuts, with_sq...]
    pallas_call x1, Pallas kernels: 14.5 us -> 12.9 us  [latents_of(): pl.pallas_call(functools.partial(basis_kernel, own, layers), out_shape=ja...]
  transfers between devices with their start and end apart: 15 -> 17, of which waited for: 10 -> 13; matrix products, arithmetic and copies ran while one was open for 0% -> 0% of each run, Pallas kernels for 6% -> 12%
where the time goes in v3:
time: 87.5 us; the launch traced here: 87.2 us
  Pallas kernels  35.2 us (40%)
  waiting for transfers between devices  25.4 us (29%)
  starting transfers between devices  24.9 us (28%)
  local copies, waits for them, and re-layouts  1.05 us (1%)
    ppermute x17, waiting for transfers between devices, exchange(): return lax.ppermute(x, axis, [(j, j ^ bit) for j in range(size)])  25.4 us
    ppermute x17, starting transfers between devices, exchange(): return lax.ppermute(x, axis, [(j, j ^ bit) for j in range(size)])  24.9 us
    pallas_call x2, Pallas kernels, partial_products(): pl.pallas_call(functools.partial(partial_kernel, own, slot, cuts, with_sq...  18.1 us
    pallas_call x1, Pallas kernels, latents_of(): pl.pallas_call(functools.partial(basis_kernel, own, layers), out_shape=ja...  12.9 us
    pallas_call x2, Pallas kernels, stacked_and_gram(): pl.pallas_call(functools.partial(gram_kernel, groups, width), out_shape=[...  2.96 us
  transfers between devices with their start and end apart: 17, of which 13 were waited for; matrix products, arithmetic and copies ran while one was open for 0% of the time, Pallas kernels for 12%

profile of v3, /device:TPU:0, one launch (start us, length us, event | category | flops | bytes accessed | tf_op | source)
XLA Modules:
  0.0 87.2 jit_solution(3676347085209472352)
XLA Ops:
  0.0 0.0 copy-start
  0.0 0.0 copy-start.1
  0.0 0.8 copy-done.1
  0.8 10.3 %partial_products.2 = (bf16[4,512,256]{2,1,0:T(8,128)(2,1)S(1)}, bf16[4,512,256]{2,1,0:T(8,128)(2,1)S(1)}, f32[4,512]{1,0:T(4,128)S(1)}) custom-call(s32[1]{0:T(128)} %bitcast.1.m_ref, bf16[4,2048]{1,0:T(4,128)(2,1)S(1)} %copy-done.1, bf16[4,512,2048]{2,1,0:T(8,128)(2,1)} %hid_ref.3, bf16[4,2048,1024]{2,1,0:T(8,128)(2,1)} %w_ref.3), custom_call_target="tpu_custom_call" | custom-call | flops 4294967296 | bytes 16777216 | tf_op jit(solution)/shard_map/partial_products/pallas_call | solution.py:87
  11.1 0.5 collective-permute-start.1
  11.6 0.1 collective-permute-start
  11.7 2.2 %collective-permute-done = f32[4,512]{1,0:T(4,128)S(1)} collective-permute-done((f32[4,512]{1,0:T(4,128)S(1)}, f32[4,512]{1,0:T(4,128)S(1)}, u32[]{:S(2)}, u32[]{:S(2)}) %collective-permute-start) | collective-permute-done | bytes 8224 | tf_op jit(solution)/shard_map/ppermute | solution.py:27
  13.9 0.0 collective-permute-done.1.refs_1_
  13.9 0.3 next_send.2
  14.2 2.9 %collective-permute-start.2 = (bf16[4,528,128]{2,1,0:T(8,128)(2,1)S(1)}, bf16[4,528,128]{2,1,0:T(8,128)(2,1)S(1)}, u32[]{:S(2)}, u32[]{:S(2)}) collective-permute-start(bf16[4,528,128]{2,1,0:T(8,128)(2,1)S(1)} %get-tuple-element.33), channel_id=1, source_target_pairs={{0,2},{1,3},{2,0},{3,1},{4,6},{5,7},{6,4},{7,5},{8,10},{9,11},{10,... | collective-permute-start | bytes 1622024 | tf_op jit(solution)/shard_map/ppermute | solution.py:27
  17.1 7.9 %partial_products.3 = (bf16[4,512,256]{2,1,0:T(8,128)(2,1)S(1)}, bf16[2,512,256]{2,1,0:T(8,128)(2,1)S(1)}, bf16[2,512,256]{2,1,0:T(8,128)(2,1)S(1)}) custom-call(s32[1]{0:T(128)} %bitcast.1.m_ref, bf16[4,2048]{1,0:T(4,128)(2,1)S(1)} %copy-done.1, bf16[4,512,2048]{2,1,0:T(8,128)(2,1)} %hid_ref.3, bf16[4,2048,1024]{2,1,0:T(8,128)(2,1)} %w_ref.3), custom_call_target="tpu_custom_call" | custom-call | flops 4294967296 | bytes 16777216 | tf_op jit(solution)/shard_map/partial_products/pallas_call | solution.py:87
  25.0 0.1 collective-permute-start.3
  25.1 0.5 collective-permute-start.4
  25.6 1.4 %collective-permute-done.3.refs_1_ = bf16[2,512,256]{2,1,0:T(8,128)(2,1)S(1)} collective-permute-done((bf16[2,512,256]{2,1,0:T(8,128)(2,1)S(1)}, bf16[2,512,256]{2,1,0:T(8,128)(2,1)S(1)}, u32[]{:S(2)}, u32[]{:S(2)}) %collective-permute-start.3) | collective-permute-done | bytes 524320 | tf_op jit(solution)/shard_map/ppermute | solution.py:27
  27.0 0.7 collective-permute-done.4.refs_2_
  27.7 2.0 %collective-permute-done.2.refs_1_ = bf16[4,528,128]{2,1,0:T(8,128)(2,1)S(1)} collective-permute-done((bf16[4,528,128]{2,1,0:T(8,128)(2,1)S(1)}, bf16[4,528,128]{2,1,0:T(8,128)(2,1)S(1)}, u32[]{:S(2)}, u32[]{:S(2)}) %collective-permute-start.2) | collective-permute-done | bytes 540704 | tf_op jit(solution)/shard_map/ppermute | solution.py:27
  29.7 0.9 %next_send.3 = (bf16[4,512,128]{2,1,0:T(8,128)(2,1)S(1)}, bf16[2,512,128]{2,1,0:T(8,128)(2,1)}, bf16[2,512,128]{2,1,0:T(8,128)(2,1)}) custom-call(bf16[4,512,256]{2,1,0:T(8,128)(2,1)S(1)} %get-tuple-element.38.refs_0_, bf16[2,512,256]{2,1,0:T(8,128)(2,1)S(1)} %collective-permute-done.3.refs_1_, bf16[2,512,256]{2,1,0:T(8,128)(2,1)S(1)} %collective-permute-done.4.refs_2_), custom_call_target="tpu_custom_call" | custom-call | tf_op jit(solution)/shard_map/next_send/pallas_call | solution.py:153
  30.6 1.7 %collective-permute-start.5 = (bf16[2,512,128]{2,1,0:T(8,128)(2,1)}, bf16[2,512,128]{2,1,0:T(8,128)(2,1)S(1)}, u32[]{:S(2)}, u32[]{:S(2)}) collective-permute-start(bf16[2,512,128]{2,1,0:T(8,128)(2,1)} %get-tuple-element.45), channel_id=1, source_target_pairs={{0,2},{1,3},{2,0},{3,1},{4,6},{5,7},{6,4},{7,5},{8,10},{9,11},{10,... | collective-permute-start | bytes 786440 | tf_op jit(solution)/shard_map/ppermute | solution.py:27
  32.4 0.4 collective-permute-start.11
  32.8 1.5 %stacked_gram.2 = (bf16[512,512]{1,0:T(8,128)(2,1)}, bf16[128,1280]{1,0:T(8,128)(2,1)S(1)}) custom-call(f32[4,512]{1,0:T(4,128)S(1)} %add.43.squares_ref, bf16[4,512,128]{2,1,0:T(8,128)(2,1)S(1)} %get-tuple-element.43.refs_0_, bf16[4,528,128]{2,1,0:T(8,128)(2,1)S(1)} %collective-permute-done.2.refs_1_), custom_call_target="tpu_custom_call" | custom-call | tf_op jit(solution)/shard_map/stacked_gram/pallas_call | solution.py:197
  34.2 5.8 %collective-permute-done.5.refs_1_ = bf16[2,512,128]{2,1,0:T(8,128)(2,1)S(1)} collective-permute-done((bf16[2,512,128]{2,1,0:T(8,128)(2,1)}, bf16[2,512,128]{2,1,0:T(8,128)(2,1)S(1)}, u32[]{:S(2)}, u32[]{:S(2)}) %collective-permute-start.5) | collective-permute-done | bytes 262176 | tf_op jit(solution)/shard_map/ppermute | solution.py:27
  40.0 1.9 %collective-permute-start.6 = (bf16[64,1280]{1,0:T(8,128)(2,1)S(1)}, bf16[64,1280]{1,0:T(8,128)(2,1)S(1)}, u32[]{:S(2)}, u32[]{:S(2)}) collective-permute-start(bf16[64,1280]{1,0:T(8,128)(2,1)S(1)} %constant_dynamic-slice_fusion.1), channel_id=1, source_target_pairs={{0,4},{4,0},{8,12},{12,8},{16,20},{20,16},{24,28},{28,24},{1,5},{5... | collective-permute-start | bytes 491528 | tf_op jit(solution)/shard_map/ppermute | solution.py:27
  41.9 2.4 %collective-permute-done.11.refs_2_ = bf16[2,512,128]{2,1,0:T(8,128)(2,1)S(1)} collective-permute-done((bf16[2,512,128]{2,1,0:T(8,128)(2,1)}, bf16[2,512,128]{2,1,0:T(8,128)(2,1)S(1)}, u32[]{:S(2)}, u32[]{:S(2)}) %collective-permute-start.11) | collective-permute-done | bytes 262176 | tf_op jit(solution)/shard_map/ppermute | solution.py:27
  44.3 1.5 %stacked_gram.3 = (bf16[512,512]{1,0:T(8,128)(2,1)}, bf16[128,1280]{1,0:T(8,128)(2,1)S(1)}) custom-call(f32[4,512]{1,0:T(4,128)S(1)} %add.43.squares_ref, bf16[4,512,128]{2,1,0:T(8,128)(2,1)S(1)} %get-tuple-element.41.refs_0_, bf16[2,512,128]{2,1,0:T(8,128)(2,1)S(1)} %collective-permute-done.5.refs_1_, bf16[2,512,128]{2,1,0:T(8,128)(2,1)S(1)} %collective-permute-done.11.refs_2_), custom_call_target="tpu_custom_call" | custom-call | tf_op jit(solution)/shard_map/stacked_gram/pallas_call | solution.py:197
  45.7 0.0 collective-permute-done.6
  45.8 1.6 %collective-permute-start.7 = (bf16[32,1280]{1,0:T(8,128)(2,1)S(1)}, bf16[32,1280]{1,0:T(8,128)(2,1)S(1)}, u32[]{:S(2)}, u32[]{:S(2)}) collective-permute-start(bf16[32,1280]{1,0:T(8,128)(2,1)S(1)} %dynamic-slice_convert_fusion.1), channel_id=1, source_target_pairs={{0,8},{4,12},{8,0},{12,4},{16,24},{20,28},{24,16},{28,20},{1,9},{5... | collective-permute-start | bytes 245768 | tf_op jit(solution)/shard_map/ppermute | solution.py:27
  47.4 1.6 %collective-permute-start.12 = (bf16[64,1280]{1,0:T(8,128)(2,1)S(1)}, bf16[64,1280]{1,0:T(8,128)(2,1)S(1)}, u32[]{:S(2)}, u32[]{:S(2)}) collective-permute-start(bf16[64,1280]{1,0:T(8,128)(2,1)S(1)} %constant_dynamic-slice_fusion), channel_id=1, source_target_pairs={{0,4},{4,0},{8,12},{12,8},{16,20},{20,16},{24,28},{28,24},{1,5},{5... | collective-permute-start | bytes 491528 | tf_op jit(solution)/shard_map/ppermute | solution.py:27
  49.0 1.3 %collective-permute-done.7 = bf16[32,1280]{1,0:T(8,128)(2,1)S(1)} collective-permute-done((bf16[32,1280]{1,0:T(8,128)(2,1)S(1)}, bf16[32,1280]{1,0:T(8,128)(2,1)S(1)}, u32[]{:S(2)}, u32[]{:S(2)}) %collective-permute-start.7) | collective-permute-done | bytes 81952 | tf_op jit(solution)/shard_map/ppermute | solution.py:27
  50.3 2.9 %collective-permute-start.8 = (bf16[32,1280]{1,0:T(8,128)(2,1)S(1)}, bf16[32,1280]{1,0:T(8,128)(2,1)S(1)}, u32[]{:S(2)}, u32[]{:S(2)}) collective-permute-start(bf16[32,1280]{1,0:T(8,128)(2,1)S(1)} %add_convert_fusion.3), channel_id=1, source_target_pairs={{0,16},{4,20},{8,24},{12,28},{16,0},{20,4},{24,8},{28,12},{1,17},{... | collective-permute-start | bytes 245768 | tf_op jit(solution)/shard_map/ppermute | solution.py:27
  53.2 0.0 collective-permute-done.12
  53.3 1.4 %collective-permute-start.13 = (bf16[32,1280]{1,0:T(8,128)(2,1)S(1)}, bf16[32,1280]{1,0:T(8,128)(2,1)S(1)}, u32[]{:S(2)}, u32[]{:S(2)}) collective-permute-start(bf16[32,1280]{1,0:T(8,128)(2,1)S(1)} %dynamic-slice_convert_fusion), channel_id=1, source_target_pairs={{0,8},{4,12},{8,0},{12,4},{16,24},{20,28},{24,16},{28,20},{1,9},{5... | collective-permute-start | bytes 245768 | tf_op jit(solution)/shard_map/ppermute | solution.py:27
  54.7 1.1 %collective-permute-done.8 = bf16[32,1280]{1,0:T(8,128)(2,1)S(1)} collective-permute-done((bf16[32,1280]{1,0:T(8,128)(2,1)S(1)}, bf16[32,1280]{1,0:T(8,128)(2,1)S(1)}, u32[]{:S(2)}, u32[]{:S(2)}) %collective-permute-start.8) | collective-permute-done | bytes 81952 | tf_op jit(solution)/shard_map/ppermute | solution.py:27
  55.8 1.7 %collective-permute-start.9 = (bf16[32,1280]{1,0:T(8,128)(2,1)S(1)}, bf16[32,1280]{1,0:T(8,128)(2,1)S(1)}, u32[]{:S(2)}, u32[]{:S(2)}) collective-permute-start(bf16[32,1280]{1,0:T(8,128)(2,1)S(1)} %add_convert_fusion.2), channel_id=1, source_target_pairs={{0,8},{4,12},{8,0},{12,4},{16,24},{20,28},{24,16},{28,20},{1,9},{5... | collective-permute-start | bytes 245768 | tf_op jit(solution)/shard_map/ppermute | solution.py:27
  57.5 0.9 %collective-permute-done.13 = bf16[32,1280]{1,0:T(8,128)(2,1)S(1)} collective-permute-done((bf16[32,1280]{1,0:T(8,128)(2,1)S(1)}, bf16[32,1280]{1,0:T(8,128)(2,1)S(1)}, u32[]{:S(2)}, u32[]{:S(2)}) %collective-permute-start.13) | collective-permute-done | bytes 81952 | tf_op jit(solution)/shard_map/ppermute | solution.py:27
  58.4 2.6 %collective-permute-start.14 = (bf16[32,1280]{1,0:T(8,128)(2,1)S(1)}, bf16[32,1280]{1,0:T(8,128)(2,1)S(1)}, u32[]{:S(2)}, u32[]{:S(2)}) collective-permute-start(bf16[32,1280]{1,0:T(8,128)(2,1)S(1)} %add_convert_fusion.1), channel_id=1, source_target_pairs={{0,16},{4,20},{8,24},{12,28},{16,0},{20,4},{24,8},{28,12},{1,17},{... | collective-permute-start | bytes 245768 | tf_op jit(solution)/shard_map/ppermute | solution.py:27
  61.0 0.0 collective-permute-done.9
  61.1 2.8 %collective-permute-done.14 = bf16[32,1280]{1,0:T(8,128)(2,1)S(1)} collective-permute-done((bf16[32,1280]{1,0:T(8,128)(2,1)S(1)}, bf16[32,1280]{1,0:T(8,128)(2,1)S(1)}, u32[]{:S(2)}, u32[]{:S(2)}) %collective-permute-start.14) | collective-permute-done | bytes 81952 | tf_op jit(solution)/shard_map/ppermute | solution.py:27
  63.9 1.7 %collective-permute-start.15 = (bf16[32,1280]{1,0:T(8,128)(2,1)S(1)}, bf16[32,1280]{1,0:T(8,128)(2,1)S(1)}, u32[]{:S(2)}, u32[]{:S(2)}) collective-permute-start(bf16[32,1280]{1,0:T(8,128)(2,1)S(1)} %add_convert_fusion), channel_id=1, source_target_pairs={{0,8},{4,12},{8,0},{12,4},{16,24},{20,28},{24,16},{28,20},{1,9},{5... | collective-permute-start | bytes 245768 | tf_op jit(solution)/shard_map/ppermute | solution.py:27
  65.6 1.6 %collective-permute-start.10 = (bf16[64,1280]{1,0:T(8,128)(2,1)S(1)}, bf16[64,1280]{1,0:T(8,128)(2,1)S(1)}, u32[]{:S(2)}, u32[]{:S(2)}) collective-permute-start(bf16[64,1280]{1,0:T(8,128)(2,1)S(1)} %pad_maximum_fusion.2), channel_id=1, source_target_pairs={{0,4},{4,0},{8,12},{12,8},{16,20},{20,16},{24,28},{28,24},{1,5},{5... | collective-permute-start | bytes 491528 | tf_op jit(solution)/shard_map/ppermute | solution.py:27
  67.2 1.2 %collective-permute-done.15 = bf16[32,1280]{1,0:T(8,128)(2,1)S(1)} collective-permute-done((bf16[32,1280]{1,0:T(8,128)(2,1)S(1)}, bf16[32,1280]{1,0:T(8,128)(2,1)S(1)}, u32[]{:S(2)}, u32[]{:S(2)}) %collective-permute-start.15) | collective-permute-done | bytes 81952 | tf_op jit(solution)/shard_map/ppermute | solution.py:27
  68.4 1.8 %collective-permute-start.16 = (bf16[64,1280]{1,0:T(8,128)(2,1)S(1)}, bf16[64,1280]{1,0:T(8,128)(2,1)S(1)}, u32[]{:S(2)}, u32[]{:S(2)}) collective-permute-start(bf16[64,1280]{1,0:T(8,128)(2,1)S(1)} %pad_maximum_fusion.3), channel_id=1, source_target_pairs={{0,4},{4,0},{8,12},{12,8},{16,20},{20,16},{24,28},{28,24},{1,5},{5... | collective-permute-start | bytes 491528 | tf_op jit(solution)/shard_map/ppermute | solution.py:27
  70.2 0.0 copy-done
  70.2 0.1 copy.7
  70.4 0.6 collective-permute-done.10
  71.0 3.0 %collective-permute-done.16 = bf16[64,1280]{1,0:T(8,128)(2,1)S(1)} collective-permute-done((bf16[64,1280]{1,0:T(8,128)(2,1)S(1)}, bf16[64,1280]{1,0:T(8,128)(2,1)S(1)}, u32[]{:S(2)}, u32[]{:S(2)}) %collective-permute-start.16) | collective-permute-done | bytes 163872 | tf_op jit(solution)/shard_map/ppermute | solution.py:27
  74.0 0.1 broadcast_select_fusion.1
  74.2 12.9 %basis_latents.1 = bf16[512,2,128]{2,1,0:T(2,128)(2,1)} custom-call(bf16[2,128,512]{2,1,0:T(8,128)(2,1)S(1)} %bitcast.2, bf16[128,1280]{1,0:T(8,128)(2,1)S(1)} %pad_maximum_fusion.refs_0_, bf16[128,1280]{1,0:T(8,128)(2,1)S(1)} %pad_maximum_fusion.1.refs_1_, bf16[512,512]{1,0:T(8,128)(2,1)} %get-tuple-element.53.refs_2_, ...), custom_call_target="tpu_custom_call" | custom-call | tf_op jit(solution)/shard_map/basis_latents/pallas_call | solution.py:371
  (22 shorter events, 0.4 us)
Async XLA Ops:
  0.0 70.2 %copy-start = (bf16[8,512,128]{2,1,0:T(8,128)(2,1)S(1)}, bf16[8,512,128]{2,1,0:T(8,128)(2,1)}, u32[]{:S(2)}) copy-start(bf16[8,512,128]{2,1,0:T(8,128)(2,1)} %param.7) | copy-start | bytes 3145732
  0.0 0.8 copy-start.1
  11.1 2.8 %collective-permute-start.1 = (bf16[4,512,256]{2,1,0:T(8,128)(2,1)S(1)}, bf16[4,512,256]{2,1,0:T(8,128)(2,1)S(1)}, u32[]{:S(2)}, u32[]{:S(2)}) collective-permute-start(bf16[4,512,256]{2,1,0:T(8,128)(2,1)S(1)} %get-tuple-element.32), channel_id=1, source_target_pairs={{0,1},{1,0},{2,3},{3,2},{4,5},{5,4},{6,7},{7,6},{8,9},{9,8},{10,11... | collective-permute-start | bytes 3145736 | tf_op jit(solution)/shard_map/ppermute | solution.py:27
  11.6 2.3 %collective-permute-start = (f32[4,512]{1,0:T(4,128)S(1)}, f32[4,512]{1,0:T(4,128)S(1)}, u32[]{:S(2)}, u32[]{:S(2)}) collective-permute-start(f32[4,512]{1,0:T(4,128)S(1)} %get-tuple-element.30), channel_id=1, source_target_pairs={{0,1},{1,0},{2,3},{3,2},{4,5},{5,4},{6,7},{7,6},{8,9},{9,8},{10,11... | collective-permute-start | bytes 24584 | tf_op jit(solution)/shard_map/ppermute | solution.py:27
  14.2 15.5 %collective-permute-start.2 = (bf16[4,528,128]{2,1,0:T(8,128)(2,1)S(1)}, bf16[4,528,128]{2,1,0:T(8,128)(2,1)S(1)}, u32[]{:S(2)}, u32[]{:S(2)}) collective-permute-start(bf16[4,528,128]{2,1,0:T(8,128)(2,1)S(1)} %get-tuple-element.33), channel_id=1, source_target_pairs={{0,2},{1,3},{2,0},{3,1},{4,6},{5,7},{6,4},{7,5},{8,10},{9,11},{10,... | collective-permute-start | bytes 1622024 | tf_op jit(solution)/shard_map/ppermute | solution.py:27
  25.0 2.0 %collective-permute-start.3 = (bf16[2,512,256]{2,1,0:T(8,128)(2,1)S(1)}, bf16[2,512,256]{2,1,0:T(8,128)(2,1)S(1)}, u32[]{:S(2)}, u32[]{:S(2)}) collective-permute-start(bf16[2,512,256]{2,1,0:T(8,128)(2,1)S(1)} %get-tuple-element.36), channel_id=1, source_target_pairs={{0,1},{1,0},{2,3},{3,2},{4,5},{5,4},{6,7},{7,6},{8,9},{9,8},{10,11... | collective-permute-start | bytes 1572872 | tf_op jit(solution)/shard_map/ppermute | solution.py:27
  25.1 2.6 %collective-permute-start.4 = (bf16[2,512,256]{2,1,0:T(8,128)(2,1)S(1)}, bf16[2,512,256]{2,1,0:T(8,128)(2,1)S(1)}, u32[]{:S(2)}, u32[]{:S(2)}) collective-permute-start(bf16[2,512,256]{2,1,0:T(8,128)(2,1)S(1)} %get-tuple-element.37), channel_id=1, source_target_pairs={{0,1},{1,0},{2,3},{3,2},{4,5},{5,4},{6,7},{7,6},{8,9},{9,8},{10,11... | collective-permute-start | bytes 1572872 | tf_op jit(solution)/shard_map/ppermute | solution.py:27
  30.6 9.4 %collective-permute-start.5 = (bf16[2,512,128]{2,1,0:T(8,128)(2,1)}, bf16[2,512,128]{2,1,0:T(8,128)(2,1)S(1)}, u32[]{:S(2)}, u32[]{:S(2)}) collective-permute-start(bf16[2,512,128]{2,1,0:T(8,128)(2,1)} %get-tuple-element.45), channel_id=1, source_target_pairs={{0,2},{1,3},{2,0},{3,1},{4,6},{5,7},{6,4},{7,5},{8,10},{9,11},{10,... | collective-permute-start | bytes 786440 | tf_op jit(solution)/shard_map/ppermute | solution.py:27
  32.4 11.9 %collective-permute-start.11 = (bf16[2,512,128]{2,1,0:T(8,128)(2,1)}, bf16[2,512,128]{2,1,0:T(8,128)(2,1)S(1)}, u32[]{:S(2)}, u32[]{:S(2)}) collective-permute-start(bf16[2,512,128]{2,1,0:T(8,128)(2,1)} %get-tuple-element.47), channel_id=1, source_target_pairs={{0,2},{1,3},{2,0},{3,1},{4,6},{5,7},{6,4},{7,5},{8,10},{9,11},{10,... | collective-permute-start | bytes 786440 | tf_op jit(solution)/shard_map/ppermute | solution.py:27
  40.0 5.7 %collective-permute-start.6 = (bf16[64,1280]{1,0:T(8,128)(2,1)S(1)}, bf16[64,1280]{1,0:T(8,128)(2,1)S(1)}, u32[]{:S(2)}, u32[]{:S(2)}) collective-permute-start(bf16[64,1280]{1,0:T(8,128)(2,1)S(1)} %constant_dynamic-slice_fusion.1), channel_id=1, source_target_pairs={{0,4},{4,0},{8,12},{12,8},{16,20},{20,16},{24,28},{28,24},{1,5},{5... | collective-permute-start | bytes 491528 | tf_op jit(solution)/shard_map/ppermute | solution.py:27
  45.8 4.5 %collective-permute-start.7 = (bf16[32,1280]{1,0:T(8,128)(2,1)S(1)}, bf16[32,1280]{1,0:T(8,128)(2,1)S(1)}, u32[]{:S(2)}, u32[]{:S(2)}) collective-permute-start(bf16[32,1280]{1,0:T(8,128)(2,1)S(1)} %dynamic-slice_convert_fusion.1), channel_id=1, source_target_pairs={{0,8},{4,12},{8,0},{12,4},{16,24},{20,28},{24,16},{28,20},{1,9},{5... | collective-permute-start | bytes 245768 | tf_op jit(solution)/shard_map/ppermute | solution.py:27
  47.4 5.8 %collective-permute-start.12 = (bf16[64,1280]{1,0:T(8,128)(2,1)S(1)}, bf16[64,1280]{1,0:T(8,128)(2,1)S(1)}, u32[]{:S(2)}, u32[]{:S(2)}) collective-permute-start(bf16[64,1280]{1,0:T(8,128)(2,1)S(1)} %constant_dynamic-slice_fusion), channel_id=1, source_target_pairs={{0,4},{4,0},{8,12},{12,8},{16,20},{20,16},{24,28},{28,24},{1,5},{5... | collective-permute-start | bytes 491528 | tf_op jit(solution)/shard_map/ppermute | solution.py:27
  50.3 5.4 %collective-permute-start.8 = (bf16[32,1280]{1,0:T(8,128)(2,1)S(1)}, bf16[32,1280]{1,0:T(8,128)(2,1)S(1)}, u32[]{:S(2)}, u32[]{:S(2)}) collective-permute-start(bf16[32,1280]{1,0:T(8,128)(2,1)S(1)} %add_convert_fusion.3), channel_id=1, source_target_pairs={{0,16},{4,20},{8,24},{12,28},{16,0},{20,4},{24,8},{28,12},{1,17},{... | collective-permute-start | bytes 245768 | tf_op jit(solution)/shard_map/ppermute | solution.py:27
  53.3 5.1 %collective-permute-start.13 = (bf16[32,1280]{1,0:T(8,128)(2,1)S(1)}, bf16[32,1280]{1,0:T(8,128)(2,1)S(1)}, u32[]{:S(2)}, u32[]{:S(2)}) collective-permute-start(bf16[32,1280]{1,0:T(8,128)(2,1)S(1)} %dynamic-slice_convert_fusion), channel_id=1, source_target_pairs={{0,8},{4,12},{8,0},{12,4},{16,24},{20,28},{24,16},{28,20},{1,9},{5... | collective-permute-start | bytes 245768 | tf_op jit(solution)/shard_map/ppermute | solution.py:27
  55.8 5.3 %collective-permute-start.9 = (bf16[32,1280]{1,0:T(8,128)(2,1)S(1)}, bf16[32,1280]{1,0:T(8,128)(2,1)S(1)}, u32[]{:S(2)}, u32[]{:S(2)}) collective-permute-start(bf16[32,1280]{1,0:T(8,128)(2,1)S(1)} %add_convert_fusion.2), channel_id=1, source_target_pairs={{0,8},{4,12},{8,0},{12,4},{16,24},{20,28},{24,16},{28,20},{1,9},{5... | collective-permute-start | bytes 245768 | tf_op jit(solution)/shard_map/ppermute | solution.py:27
  58.4 5.4 %collective-permute-start.14 = (bf16[32,1280]{1,0:T(8,128)(2,1)S(1)}, bf16[32,1280]{1,0:T(8,128)(2,1)S(1)}, u32[]{:S(2)}, u32[]{:S(2)}) collective-permute-start(bf16[32,1280]{1,0:T(8,128)(2,1)S(1)} %add_convert_fusion.1), channel_id=1, source_target_pairs={{0,16},{4,20},{8,24},{12,28},{16,0},{20,4},{24,8},{28,12},{1,17},{... | collective-permute-start | bytes 245768 | tf_op jit(solution)/shard_map/ppermute | solution.py:27
  63.9 4.5 %collective-permute-start.15 = (bf16[32,1280]{1,0:T(8,128)(2,1)S(1)}, bf16[32,1280]{1,0:T(8,128)(2,1)S(1)}, u32[]{:S(2)}, u32[]{:S(2)}) collective-permute-start(bf16[32,1280]{1,0:T(8,128)(2,1)S(1)} %add_convert_fusion), channel_id=1, source_target_pairs={{0,8},{4,12},{8,0},{12,4},{16,24},{20,28},{24,16},{28,20},{1,9},{5... | collective-permute-start | bytes 245768 | tf_op jit(solution)/shard_map/ppermute | solution.py:27
  65.6 5.4 %collective-permute-start.10 = (bf16[64,1280]{1,0:T(8,128)(2,1)S(1)}, bf16[64,1280]{1,0:T(8,128)(2,1)S(1)}, u32[]{:S(2)}, u32[]{:S(2)}) collective-permute-start(bf16[64,1280]{1,0:T(8,128)(2,1)S(1)} %pad_maximum_fusion.2), channel_id=1, source_target_pairs={{0,4},{4,0},{8,12},{12,8},{16,20},{20,16},{24,28},{28,24},{1,5},{5... | collective-permute-start | bytes 491528 | tf_op jit(solution)/shard_map/ppermute | solution.py:27
  68.4 5.6 %collective-permute-start.16 = (bf16[64,1280]{1,0:T(8,128)(2,1)S(1)}, bf16[64,1280]{1,0:T(8,128)(2,1)S(1)}, u32[]{:S(2)}, u32[]{:S(2)}) collective-permute-start(bf16[64,1280]{1,0:T(8,128)(2,1)S(1)} %pad_maximum_fusion.3), channel_id=1, source_target_pairs={{0,4},{4,0},{8,12},{12,8},{16,20},{20,16},{24,28},{28,24},{1,5},{5... | collective-permute-start | bytes 491528 | tf_op jit(solution)/shard_map/ppermute | solution.py:27

commit v4 on v3

--- a/solution.py
+++ b/solution.py
@@ -14,7 +14,6 @@
 BF16 = jnp.bfloat16
 HIGHEST = lax.Precision.HIGHEST
 MIB = 1 << 20
-LEAD = 0
 
 
 def halving_order(count):
@@ -104,138 +103,130 @@
     )(me, gains, *[pltpu.with_memory_space_constraint(x, pltpu.HBM) for x in (hidden, weights)])
 
 
-def extra_rows(tokens):
-    return -(-3 * (tokens // HD) // 16) * 16
-
-
 def by_layer(groups, refs):
     parts, at = [], 0
     for counts in groups:
         parts.append([refs[at + n].at[i] for n, count in enumerate(counts) for i in range(count)])
         at += len(counts)
-    return parts, at
-
-
-def merge_kernel(groups, tokens, cuts, with_totals, *refs):
+    return parts
+
+
+def merge_kernel(groups, cuts, tokens, *refs):
     own_ref, out_refs = refs[-1 - len(cuts)], refs[-len(cuts) :]
     layers, _, half = own_ref.shape
-    out = [(ref, i) for ref, count in zip(out_refs, cuts) for i in range(count)]
-    parts, at = by_layer(groups, refs)
+    out = [ref.at[i] for ref, count in zip(out_refs, cuts) for i in range(count)]
+    parts = by_layer(groups, refs)
     for layer in range(layers):
         total = sum(p[layer][...].astype(F32) for p in parts)
         own_ref[layer] = total[:, :half].astype(BF16)
-        ref, i = out[layer]
-        ref[i, :tokens, :] = total[:, half:].astype(BF16)
-    if with_totals:
-        totals = refs[at][...]
-        pieces_of = tokens // HD
-        rows = out_refs[0].shape[1] - tokens
-        for layer in range(layers):
-            line = jnp.concatenate(
-                [totals[layer : layer + 1, i * HD : (i + 1) * HD] for i in range(pieces_of)], axis=0
+        out[layer][:tokens, :] = total[:, half:].astype(BF16)
+    extra = out_refs[0].shape[1] - tokens
+    if extra:
+        totals = refs[sum(len(counts) for counts in groups)][...]
+        lines = [
+            p.astype(F32)
+            for layer in range(layers)
+            for p in split3(
+                jnp.concatenate(
+                    [totals[layer : layer + 1, i * HD : (i + 1) * HD] for i in range(tokens // HD)], axis=0
+                )
             )
-            pieces = [p.astype(F32) for p in split3(line)]
-            pad = [jnp.zeros((rows - 3 * pieces_of, HD), F32)] if rows > 3 * pieces_of else []
-            ref, i = out[layer]
-            ref[i, tokens:, :HD] = jnp.concatenate(pieces + pad, axis=0).astype(BF16)
-            if half > HD:
-                ref[i, tokens:, HD:] = jnp.zeros((rows, half - HD), BF16)
-
-
-def next_send(pieces, totals, tokens, cuts):
+        ]
+        out_refs[0][:, tokens:, :] = jnp.zeros((cuts[0], extra, half), BF16)
+        out_refs[0][0, tokens:, :HD] = jnp.concatenate(lines, axis=0).astype(BF16)
+
+
+def next_send(pieces, tokens, cuts, totals):
     groups = [[a.shape[0] for a in group] for group in pieces]
     arrays = [a for group in pieces for a in group]
     layers, width = sum(groups[0]), arrays[0].shape[2]
     half = width // 2
-    rows = tokens + (extra_rows(tokens) if totals is not None else 0)
+    block = lambda *shape: pl.BlockSpec(shape, lambda i: (0,) * len(shape))
+    outs = [(layers, tokens, half)] + [(n, tokens, half) for n in cuts]
     extra = [] if totals is None else [totals]
-    block = lambda *shape: pl.BlockSpec(shape, lambda i: (0,) * len(shape))
+    if extra:
+        outs[1] = (cuts[0], tokens + 3 * layers * (tokens // HD), half)
     return pl.pallas_call(
-        functools.partial(merge_kernel, groups, tokens, cuts, totals is not None),
-        out_shape=[jax.ShapeDtypeStruct((layers, tokens, half), BF16)]
-        + [jax.ShapeDtypeStruct((count, rows, half), BF16) for count in cuts],
+        functools.partial(merge_kernel, groups, cuts, tokens),
+        out_shape=[jax.ShapeDtypeStruct(shape, BF16) for shape in outs],
         grid=(1,),
         in_specs=[block(a.shape[0], tokens, width) for a in arrays] + [block(*t.shape) for t in extra],
-        out_specs=[block(layers, tokens, half)] + [block(count, rows, half) for count in cuts],
+        out_specs=[block(*shape) for shape in outs],
         compiler_params=pltpu.CompilerParams(vmem_limit_bytes=16 * MIB),
         name="next_send",
     )(*arrays, *extra)
 
 
-def carried_totals(received, tokens):
-    cuts = tokens // HD
-    pieces = received[:, tokens : tokens + 3 * cuts, :HD].astype(F32)
-    return pieces.reshape(-1, 3, tokens).sum(1)
-
-
-def gram_kernel(groups, width, squares_ref, *refs):
-    stacked_ref, gram_ref = refs[-2:]
+def carried_totals(received, tokens, layers):
+    return received[0, tokens:, :HD].astype(F32).reshape(layers, 3, tokens).sum(1)
+
+
+def gram_kernel(parts, width, squares_ref, *refs):
     layers = squares_ref.shape[0]
     factor = lax.rsqrt(squares_ref[...] / width + EPSILON)
     factor = jnp.transpose(jnp.concatenate([factor] * (8 // layers), axis=0))
-    parts, _ = by_layer(groups, refs)
-    blocks = []
-    for layer in range(layers):
-        total = sum(p[layer][...].astype(F32) for p in parts)
-        blocks.append((total * factor[:, layer : layer + 1]).astype(BF16))
-    stacked = jnp.concatenate(blocks, axis=1)
-    stacked_ref[...] = stacked
-    column = 0
-    for i, block in enumerate(blocks):
-        upto = (i + 1) * HD
-        gram_ref[:, column : column + upto] = lax.dot_general(
-            block, stacked[:, :upto], (((0,), (0,)), ((), ())), preferred_element_type=F32
-        ).astype(BF16)
-        column += upto
-
-
-def stacked_and_gram(pieces, squares, width):
+    inputs, outs, gram_ref = refs[: -1 - len(parts)], refs[-1 - len(parts) : -1], refs[-1]
+    column, before = 0, None
+    for (first, count), stacked_ref in zip(parts, outs):
+        held_ref, got_ref, inputs = inputs[0], inputs[1], inputs[2:]
+        blocks = []
+        for i in range(count):
+            total = held_ref[i].astype(F32) + got_ref[i].astype(F32)
+            blocks.append((total * factor[:, first + i : first + i + 1]).astype(BF16))
+        stacked = jnp.concatenate(blocks, axis=1)
+        stacked_ref[...] = stacked
+        if first:
+            stacked = jnp.concatenate([before, stacked], axis=1)
+        before = stacked
+        for i, block in enumerate(blocks):
+            upto = (first + i + 1) * HD
+            gram_ref[:, column : column + upto] = lax.dot_general(
+                block, stacked[:, :upto], (((0,), (0,)), ((), ())), preferred_element_type=F32
+            ).astype(BF16)
+            column += upto
+
+
+def stacked_and_gram(parts, squares, width):
     layers, tokens = squares.shape
-    groups = [[a.shape[0] for a in group] for group in pieces]
-    arrays = [a for group in pieces for a in group]
-    packed = layers * (layers + 1) // 2 * HD
+    at = lambda *index: lambda i: index
+    arrays, in_specs, out_shape, out_specs, spans = [squares], [pl.BlockSpec(squares.shape, at(0, 0))], [], [], []
+    columns = 0
+    for held, got, first in parts:
+        count = got.shape[0]
+        arrays += [held, got]
+        in_specs.append(pl.BlockSpec((count, tokens, HD), at(first // count, 0, 0)))
+        in_specs.append(pl.BlockSpec((count, tokens, HD), at(0, 0, 0)))
+        out_shape.append(pltpu.HBM((tokens, count * HD), BF16))
+        out_specs.append(pl.BlockSpec((tokens, count * HD), at(0, 0)))
+        spans.append((first, count))
+        columns += sum(first + i + 1 for i in range(count)) * HD
     return pl.pallas_call(
-        functools.partial(gram_kernel, groups, width),
-        out_shape=[
-            pltpu.HBM((tokens, layers * HD), BF16),
-            jax.ShapeDtypeStruct((HD, packed), BF16),
-        ],
+        functools.partial(gram_kernel, spans, width),
+        out_shape=out_shape + [jax.ShapeDtypeStruct((HD, columns), BF16)],
         grid=(1,),
-        in_specs=[pl.BlockSpec(squares.shape, lambda i: (0, 0))]
-        + [pl.BlockSpec((a.shape[0], tokens, HD), lambda i: (0, 0, 0)) for a in arrays],
-        out_specs=[
-            pl.BlockSpec((tokens, layers * HD), lambda i: (0, 0)),
-            pl.BlockSpec((HD, packed), lambda i: (0, 0)),
-        ],
+        in_specs=in_specs,
+        out_specs=out_specs + [pl.BlockSpec((HD, columns), at(0, 0))],
         compiler_params=pltpu.CompilerParams(vmem_limit_bytes=16 * MIB),
         name="stacked_gram",
-    )(squares, *arrays)
-
-
-def sum_over_seq(x, ahead):
+    )(*arrays)
+
+
+def sum_over_seq(x):
     size = lax.axis_size("seq")
     me = lax.axis_index("seq")
     bits = [1 << i for i in range(size.bit_length() - 1)]
-    arrived = []
-
-    def step(send, bit):
-        if len(arrived) + LEAD < len(ahead) - 1:
-            send = lax.optimization_barrier((send, ahead[len(arrived) + LEAD]))[0]
-        arrived.append(exchange(send, "seq", bit))
-        return arrived[-1]
-
     for bit in bits[:-1]:
         half = x.shape[0] // 2
         mine = jnp.where((me & bit) != 0, half, 0)
-        got = step(lax.dynamic_slice_in_dim(x, half - mine, half, 0).astype(BF16), bit)
+        got = exchange(lax.dynamic_slice_in_dim(x, half - mine, half, 0).astype(BF16), "seq", bit)
         x = lax.dynamic_slice_in_dim(x, mine, half, 0).astype(F32) + got.astype(F32)
     x = x.astype(BF16)
-    x = (x.astype(F32) + step(x, bits[-1]).astype(F32)).astype(BF16)
+    x = (x.astype(F32) + exchange(x, "seq", bits[-1]).astype(F32)).astype(BF16)
     for bit in bits[:-1][::-1]:
-        got = step(x, bit)
+        got = exchange(x, "seq", bit)
         upper = (me & bit) != 0
         x = jnp.concatenate([jnp.where(upper, got, x), jnp.where(upper, x, got)], axis=0)
-    return x, arrived
+    return x
 
 
 def split3(x):
@@ -312,31 +303,36 @@
     return [jnp.where(lane <= row, jnp.concatenate(p, axis=0), 0.0) for p in panels]
 
 
-def basis_kernel(own, layers, start_ref, *refs):
-    gram_refs, stacked_refs, out_ref = refs[:own], refs[own : 2 * own], refs[2 * own]
-    rows_ref, sems = refs[2 * own + 1 :]
-    copies = [pltpu.make_async_copy(stacked_refs[s], rows_ref.at[s], sems.at[s]) for s in range(own)]
-    for copy in copies:
+def basis_kernel(own, layers, chains, start_ref, *refs):
+    grams_in = refs[: len(chains)]
+    stacked_in = refs[len(chains) : -3]
+    out_ref, rows_ref, sems = refs[-3:]
+    block, copies = {}, [[] for _ in range(own)]
+    at = 0
+    for chain, ref in zip(chains, grams_in):
+        column = 0
+        for slot, first, count in chain:
+            to = rows_ref.at[slot, :, pl.ds(first * HD, count * HD)]
+            copies[slot].append(pltpu.make_async_copy(stacked_in[at], to, sems.at[at]))
+            at += 1
+            for i in range(first, first + count):
+                for j in range(i + 1):
+                    block[slot, i, j] = ref[:, column : column + HD]
+                    column += HD
+    for copy in sum(copies, []):
         copy.start()
     grams = []
-    for ref in gram_refs:
-        block = {}
-        column = 0
-        for i in range(layers):
-            for j in range(i + 1):
-                block[i, j] = ref[:, column : column + HD]
-                column += HD
-        rows = []
-        for i in range(layers):
-            rows.append(
-                jnp.concatenate(
-                    [
-                        block[i, j] if j <= i else jnp.transpose(block[j, i].astype(F32)).astype(BF16)
-                        for j in range(layers)
-                    ],
-                    axis=1,
-                )
+    for slot in range(own):
+        rows = [
+            jnp.concatenate(
+                [
+                    block[slot, i, j] if j <= i else jnp.transpose(block[slot, j, i].astype(F32)).astype(BF16)
+                    for j in range(layers)
+                ],
+                axis=1,
             )
+            for i in range(layers)
+        ]
         grams.append(jnp.concatenate(rows, axis=0))
     rank = start_ref.shape[1]
 
@@ -357,24 +353,26 @@
             for x, f in zip(images, inverse_cholesky(inner))
         ]
     for s in range(own):
-        copies[s].wait()
+        for copy in copies[s]:
+            copy.wait()
         out_ref[:, s, :] = lax.dot_general(
             rows_ref[s], images[s].astype(BF16), (((1,), (1,)), ((), ())), preferred_element_type=F32
         ).astype(BF16)
 
 
-def latents_of(start, grams, stacked):
-    own = len(grams)
-    tokens = stacked[0].shape[0]
-    layers = stacked[0].shape[1] // HD
+def latents_of(start, chains, grams, stacked, tokens, layers):
+    own = start.shape[0]
     whole = lambda a: pl.BlockSpec(a.shape, lambda i: (0,) * a.ndim)
     return pl.pallas_call(
-        functools.partial(basis_kernel, own, layers),
+        functools.partial(basis_kernel, own, layers, chains),
         out_shape=jax.ShapeDtypeStruct((tokens, own, HD), BF16),
         grid=(1,),
-        in_specs=[whole(a) for a in [start] + grams] + [pl.BlockSpec(memory_space=pltpu.HBM)] * own,
+        in_specs=[whole(a) for a in [start] + grams] + [pl.BlockSpec(memory_space=pltpu.HBM)] * len(stacked),
         out_specs=pl.BlockSpec((tokens, own, HD), lambda i: (0, 0, 0)),
-        scratch_shapes=[pltpu.VMEM((own,) + stacked[0].shape, BF16), pltpu.SemaphoreType.DMA((own,))],
+        scratch_shapes=[
+            pltpu.VMEM((own, tokens, layers * HD), BF16),
+            pltpu.SemaphoreType.DMA((len(stacked),)),
+        ],
         compiler_params=pltpu.CompilerParams(vmem_limit_bytes=16 * MIB),
         name="basis_latents",
     )(start, *grams, *[pltpu.with_memory_space_constraint(x, pltpu.HBM) for x in stacked])
@@ -387,39 +385,40 @@
     me = lax.axis_index("mp").astype(jnp.int32).reshape(1)
     mp_bits = [1 << i for i in range(mp.bit_length() - 1)]
 
-    pieces, totals, sent = [], None, []
+    half = layers // 2
+    held, got, sent = [None] * own, [None] * own, []
     for slot in range(own):
+        last = slot == own - 1
         here = me if slot == 0 else lax.optimization_barrier((me, sent[-1]))[0]
-        cuts = [layers] if slot == 0 else [layers // 2, layers - layers // 2]
-        held, *sent = partial_products(hidden, norm_gain, proj_weight, here, own, slot, cuts, slot == 0)
-        if slot == 0:
+        cuts = [half, layers - half] if last else [layers]
+        parcels = [1] * layers if last else cuts
+        held[slot], *sent = partial_products(hidden, norm_gain, proj_weight, here, own, slot, parcels, last)
+        if last:
             totals = sent.pop()
             totals = totals + exchange(totals, "mp", 1)
-        got = [exchange(send, "mp", 1) for send in sent]
+        got[slot] = [exchange(send, "mp", 1) for send in sent]
         for bit in mp_bits[1:]:
-            cuts = [layers] if slot == 0 or bit != mp_bits[-1] else [layers // 2, layers - layers // 2]
-            arrays = [[held], got]
+            pieces = [[held[slot]], got[slot]]
             if slot:
-                arrays = lax.optimization_barrier((arrays, pieces[slot - 1][-1]))[0]
-            held, *sent = next_send(arrays, totals if slot == 0 else None, tokens, cuts)
-            got = [exchange(send, "mp", bit) for send in sent]
-            if slot == 0:
-                totals = totals + carried_totals(got[0], tokens)
-        pieces.append([[held], got])
-
-    grams, stacked, arrived = [], [], []
-    for slot in range(own):
-        later = slot + 1 < own
-        if later:
-            totals = lax.optimization_barrier((totals, pieces[slot + 1][0]))[0]
-        rows, gram = stacked_and_gram(pieces[slot], totals, width * mp)
-        stacked.append(rows)
-        if later:
-            gram = lax.optimization_barrier((gram, pieces[slot + 1][1][0]))[0]
-        gram, arrived = sum_over_seq(gram, arrived)
-        grams.append(gram)
+                pieces = lax.optimization_barrier((pieces, got[slot - 1]))[0]
+            held[slot], *sent = next_send(pieces, tokens, cuts, totals if last else None)
+            got[slot] = [exchange(send, "mp", bit) for send in sent]
+            if last:
+                totals = totals + carried_totals(got[slot][0], tokens, layers)
+
+    chains = [[(slot, 0, layers)] for slot in range(own - 1)]
+    chains.append([(own - 1, 0, half), (own - 1, half, layers - half)])
+    grams, stacked = [], []
+    for chain in chains:
+        parts = [
+            (held[slot], got[slot][1 if first else 0], first)
+            for slot, first, _ in chain
+        ]
+        *rows, gram = stacked_and_gram(parts, totals, width * mp)
+        stacked += rows
+        grams.append(sum_over_seq(gram))
     start = jnp.swapaxes(lax.dynamic_slice_in_dim(start_block, me[0] * own, own, 0), 1, 2)
-    return latents_of(start, grams, stacked)
+    return latents_of(start, chains, grams, stacked, tokens, layers)
 
 
 def solution(mesh):

time: 87.5 us -> 85.8 us (0.981)
  starting transfers between devices: 24.9 us -> 22 us
  waiting for transfers between devices: 25.4 us -> 26.3 us
    ppermute x17 -> x19, starting transfers between devices: 24.9 us -> 22 us  [exchange(): return lax.ppermute(x, axis, [(j, j ^ bit) for j in range(size)])]
    ppermute x17 -> x19, waiting for transfers between devices: 25.4 us -> 26.3 us  [exchange(): return lax.ppermute(x, axis, [(j, j ^ bit) for j in range(size)])]
  transfers between devices with their start and end apart: 17 -> 19, of which waited for: 13 -> 15; matrix products, arithmetic and copies ran while one was open for 0% -> 1% of each run, Pallas kernels for 12% -> 15%
where the time goes in v4:
time: 85.8 us; the launch traced here: 85.5 us
  Pallas kernels  34.5 us (40%)
  waiting for transfers between devices  26.3 us (31%)
  starting transfers between devices  22 us (26%)
  local copies, waits for them, and re-layouts  1.75 us (2%)
    ppermute x19, waiting for transfers between devices, exchange(): return lax.ppermute(x, axis, [(j, j ^ bit) for j in range(size)])  26.3 us
    ppermute x19, starting transfers between devices, exchange(): return lax.ppermute(x, axis, [(j, j ^ bit) for j in range(size)])  22 us
    pallas_call x2, Pallas kernels, partial_products(): pl.pallas_call(functools.partial(partial_kernel, own, slot, cuts, with_sq...  18.1 us
    pallas_call x1, Pallas kernels, latents_of(): pl.pallas_call(functools.partial(basis_kernel, own, layers, chains), out_...  12.9 us
    pallas_call x2, Pallas kernels, stacked_and_gram(): pl.pallas_call(functools.partial(gram_kernel, spans, width), out_shape=ou...  2.87 us
  transfers between devices with their start and end apart: 19, of which 15 were waited for; matrix products, arithmetic and copies ran while one was open for 1% of the time, Pallas kernels for 15%

profile of v4, /device:TPU:0, one launch (start us, length us, event | category | flops | bytes accessed | tf_op | source)
XLA Modules:
  0.0 85.5 jit_solution(15812245467457472220)
XLA Ops:
  0.0 0.8 copy-done.1
  0.8 7.9 %partial_products.2 = (bf16[4,512,256]{2,1,0:T(8,128)(2,1)S(1)}, bf16[4,512,256]{2,1,0:T(8,128)(2,1)S(1)}) custom-call(s32[1]{0:T(128)} %bitcast.1.m_ref, bf16[4,2048]{1,0:T(4,128)(2,1)S(1)} %copy-done.1, bf16[4,512,2048]{2,1,0:T(8,128)(2,1)} %hid_ref.3, bf16[4,2048,1024]{2,1,0:T(8,128)(2,1)} %w_ref.3), custom_call_target="tpu_custom_call" | custom-call | flops 4294967296 | bytes 16777216 | tf_op jit(solution)/shard_map/partial_products/pallas_call | solution.py:86
  8.7 0.5 collective-permute-start
  9.2 2.3 %collective-permute-done.refs_1_ = bf16[4,512,256]{2,1,0:T(8,128)(2,1)S(1)} collective-permute-done((bf16[4,512,256]{2,1,0:T(8,128)(2,1)S(1)}, bf16[4,512,256]{2,1,0:T(8,128)(2,1)S(1)}, u32[]{:S(2)}, u32[]{:S(2)}) %collective-permute-start) | collective-permute-done | bytes 1048608 | tf_op jit(solution)/shard_map/ppermute | solution.py:26
  11.5 0.3 next_send.2
  11.7 2.9 %collective-permute-start.6 = (bf16[4,512,128]{2,1,0:T(8,128)(2,1)S(1)}, bf16[4,512,128]{2,1,0:T(8,128)(2,1)S(1)}, u32[]{:S(2)}, u32[]{:S(2)}) collective-permute-start(bf16[4,512,128]{2,1,0:T(8,128)(2,1)S(1)} %get-tuple-element.31), channel_id=1, source_target_pairs={{0,2},{1,3},{2,0},{3,1},{4,6},{5,7},{6,4},{7,5},{8,10},{9,11},{10,... | collective-permute-start | bytes 1572872 | tf_op jit(solution)/shard_map/ppermute | solution.py:26
  14.7 10.3 %partial_products.3 = (bf16[4,512,256]{2,1,0:T(8,128)(2,1)S(1)}, bf16[1,512,256]{2,1,0:T(8,128)(2,1)S(1)}, bf16[1,512,256]{2,1,0:T(8,128)(2,1)S(1)}, bf16[1,512,...) custom-call(s32[1]{0:T(128)} %bitcast.1.m_ref, bf16[4,2048]{1,0:T(4,128)(2,1)S(1)} %copy-done.1, ...), custom_call_target="tpu_custom_call" | custom-call | flops 4294967296 | bytes 16777216 | tf_op jit(solution)/shard_map/partial_products/pallas_call | solution.py:86
  25.0 0.1 collective-permute-start.1
  25.0 0.5 collective-permute-start.2
  25.5 0.1 collective-permute-start.3
  25.6 0.4 collective-permute-start.4
  26.0 0.2 collective-permute-done.1
  26.2 0.2 collective-permute-start.5
  26.4 0.3 collective-permute-done.2.refs_1_
  26.7 0.4 collective-permute-done.3.refs_2_
  27.1 0.4 collective-permute-done.4.refs_3_
  27.4 0.4 collective-permute-done.5.refs_4_
  27.8 0.0 collective-permute-done.6.refs_1_
  27.8 0.3 next_send.3
  28.1 0.0 copy-start.2
  28.1 0.7 copy-done.2
  28.8 0.8 collective-permute-start.7
  29.6 1.3 %collective-permute-start.13 = (bf16[2,512,128]{2,1,0:T(8,128)(2,1)}, bf16[2,512,128]{2,1,0:T(8,128)(2,1)S(1)}, u32[]{:S(2)}, u32[]{:S(2)}) collective-permute-start(bf16[2,512,128]{2,1,0:T(8,128)(2,1)} %copy-done.2), channel_id=1, source_target_pairs={{0,2},{1,3},{2,0},{3,1},{4,6},{5,7},{6,4},{7,5},{8,10},{9,11},{10,... | collective-permute-start | bytes 786440 | tf_op jit(solution)/shard_map/ppermute | solution.py:26
  30.9 7.6 %collective-permute-done.7.refs_1_ = bf16[2,560,128]{2,1,0:T(8,128)(2,1)S(1)} collective-permute-done((bf16[2,560,128]{2,1,0:T(8,128)(2,1)S(1)}, bf16[2,560,128]{2,1,0:T(8,128)(2,1)S(1)}, u32[]{:S(2)}, u32[]{:S(2)}) %collective-permute-start.7) | collective-permute-done | bytes 286752 | tf_op jit(solution)/shard_map/ppermute | solution.py:26
  38.6 1.5 %stacked_gram.2 = (bf16[512,512]{1,0:T(8,128)(2,1)}, bf16[128,1280]{1,0:T(8,128)(2,1)S(1)}) custom-call(f32[4,512]{1,0:T(4,128)S(1)} %add.43.squares_ref, bf16[4,512,128]{2,1,0:T(8,128)(2,1)S(1)} %get-tuple-element.45.refs_0_, bf16[4,512,128]{2,1,0:T(8,128)(2,1)S(1)} %collective-permute-done.6.refs_1_), custom_call_target="tpu_custom_call" | custom-call | tf_op jit(solution)/shard_map/stacked_gram/pallas_call | solution.py:203
  40.1 1.6 %collective-permute-start.8 = (bf16[64,1280]{1,0:T(8,128)(2,1)S(1)}, bf16[64,1280]{1,0:T(8,128)(2,1)S(1)}, u32[]{:S(2)}, u32[]{:S(2)}) collective-permute-start(bf16[64,1280]{1,0:T(8,128)(2,1)S(1)} %constant_dynamic-slice_fusion.1), channel_id=1, source_target_pairs={{0,4},{4,0},{8,12},{12,8},{16,20},{20,16},{24,28},{28,24},{1,5},{5... | collective-permute-start | bytes 491528 | tf_op jit(solution)/shard_map/ppermute | solution.py:26
  41.6 1.9 %collective-permute-done.13.refs_3_ = bf16[2,512,128]{2,1,0:T(8,128)(2,1)S(1)} collective-permute-done((bf16[2,512,128]{2,1,0:T(8,128)(2,1)}, bf16[2,512,128]{2,1,0:T(8,128)(2,1)S(1)}, u32[]{:S(2)}, u32[]{:S(2)}) %collective-permute-start.13) | collective-permute-done | bytes 262176 | tf_op jit(solution)/shard_map/ppermute | solution.py:26
  43.5 1.4 %stacked_gram.3 = (bf16[512,256]{1,0:T(8,128)(2,1)}, bf16[512,256]{1,0:T(8,128)(2,1)}, bf16[128,1280]{1,0:T(8,128)(2,1)S(1)}) custom-call(f32[4,512]{1,0:T(4,128)S(1)} %add.43.squares_ref, bf16[4,512,128]{2,1,0:T(8,128)(2,1)S(1)} %get-tuple-element.47.refs_0_.refs_2_, bf16[2,560,128]{2,1,0:T(8,128)(2,1)S(1)} %collective-permute-done.7.refs_1_, ...), custom_call_target="tpu_custom_call" | custom-call | tf_op jit(solution)/shard_map/stacked_gram/pallas_call | solution.py:203
  44.9 1.6 %collective-permute-start.14 = (bf16[64,1280]{1,0:T(8,128)(2,1)S(1)}, bf16[64,1280]{1,0:T(8,128)(2,1)S(1)}, u32[]{:S(2)}, u32[]{:S(2)}) collective-permute-start(bf16[64,1280]{1,0:T(8,128)(2,1)S(1)} %constant_dynamic-slice_fusion), channel_id=1, source_target_pairs={{0,4},{4,0},{8,12},{12,8},{16,20},{20,16},{24,28},{28,24},{1,5},{5... | collective-permute-start | bytes 491528 | tf_op jit(solution)/shard_map/ppermute | solution.py:26
  46.6 1.6 %collective-permute-start.9 = (bf16[32,1280]{1,0:T(8,128)(2,1)S(1)}, bf16[32,1280]{1,0:T(8,128)(2,1)S(1)}, u32[]{:S(2)}, u32[]{:S(2)}) collective-permute-start(bf16[32,1280]{1,0:T(8,128)(2,1)S(1)} %dynamic-slice_convert_fusion.1), channel_id=1, source_target_pairs={{0,8},{4,12},{8,0},{12,4},{16,24},{20,28},{24,16},{28,20},{1,9},{5... | collective-permute-start | bytes 245768 | tf_op jit(solution)/shard_map/ppermute | solution.py:26
  48.2 2.4 %collective-permute-done.14 = bf16[64,1280]{1,0:T(8,128)(2,1)S(1)} collective-permute-done((bf16[64,1280]{1,0:T(8,128)(2,1)S(1)}, bf16[64,1280]{1,0:T(8,128)(2,1)S(1)}, u32[]{:S(2)}, u32[]{:S(2)}) %collective-permute-start.14) | collective-permute-done | bytes 163872 | tf_op jit(solution)/shard_map/ppermute | solution.py:26
  50.7 1.7 %collective-permute-start.15 = (bf16[32,1280]{1,0:T(8,128)(2,1)S(1)}, bf16[32,1280]{1,0:T(8,128)(2,1)S(1)}, u32[]{:S(2)}, u32[]{:S(2)}) collective-permute-start(bf16[32,1280]{1,0:T(8,128)(2,1)S(1)} %dynamic-slice_convert_fusion), channel_id=1, source_target_pairs={{0,8},{4,12},{8,0},{12,4},{16,24},{20,28},{24,16},{28,20},{1,9},{5... | collective-permute-start | bytes 245768 | tf_op jit(solution)/shard_map/ppermute | solution.py:26
  52.4 2.7 %collective-permute-start.10 = (bf16[32,1280]{1,0:T(8,128)(2,1)S(1)}, bf16[32,1280]{1,0:T(8,128)(2,1)S(1)}, u32[]{:S(2)}, u32[]{:S(2)}) collective-permute-start(bf16[32,1280]{1,0:T(8,128)(2,1)S(1)} %add_convert_fusion.3), channel_id=1, source_target_pairs={{0,16},{4,20},{8,24},{12,28},{16,0},{20,4},{24,8},{28,12},{1,17},{... | collective-permute-start | bytes 245768 | tf_op jit(solution)/shard_map/ppermute | solution.py:26
  55.1 0.9 %collective-permute-done.15 = bf16[32,1280]{1,0:T(8,128)(2,1)S(1)} collective-permute-done((bf16[32,1280]{1,0:T(8,128)(2,1)S(1)}, bf16[32,1280]{1,0:T(8,128)(2,1)S(1)}, u32[]{:S(2)}, u32[]{:S(2)}) %collective-permute-start.15) | collective-permute-done | bytes 81952 | tf_op jit(solution)/shard_map/ppermute | solution.py:26
  55.9 2.0 %collective-permute-start.16 = (bf16[32,1280]{1,0:T(8,128)(2,1)S(1)}, bf16[32,1280]{1,0:T(8,128)(2,1)S(1)}, u32[]{:S(2)}, u32[]{:S(2)}) collective-permute-start(bf16[32,1280]{1,0:T(8,128)(2,1)S(1)} %add_convert_fusion.1), channel_id=1, source_target_pairs={{0,16},{4,20},{8,24},{12,28},{16,0},{20,4},{24,8},{28,12},{1,17},{... | collective-permute-start | bytes 245768 | tf_op jit(solution)/shard_map/ppermute | solution.py:26
  57.9 2.4 %collective-permute-done.10 = bf16[32,1280]{1,0:T(8,128)(2,1)S(1)} collective-permute-done((bf16[32,1280]{1,0:T(8,128)(2,1)S(1)}, bf16[32,1280]{1,0:T(8,128)(2,1)S(1)}, u32[]{:S(2)}, u32[]{:S(2)}) %collective-permute-start.10) | collective-permute-done | bytes 81952 | tf_op jit(solution)/shard_map/ppermute | solution.py:26
  60.4 0.1 collective-permute-start.11
  60.4 1.0 %collective-permute-done.16 = bf16[32,1280]{1,0:T(8,128)(2,1)S(1)} collective-permute-done((bf16[32,1280]{1,0:T(8,128)(2,1)S(1)}, bf16[32,1280]{1,0:T(8,128)(2,1)S(1)}, u32[]{:S(2)}, u32[]{:S(2)}) %collective-permute-start.16) | collective-permute-done | bytes 81952 | tf_op jit(solution)/shard_map/ppermute | solution.py:26
  61.4 1.7 %collective-permute-start.17 = (bf16[32,1280]{1,0:T(8,128)(2,1)S(1)}, bf16[32,1280]{1,0:T(8,128)(2,1)S(1)}, u32[]{:S(2)}, u32[]{:S(2)}) collective-permute-start(bf16[32,1280]{1,0:T(8,128)(2,1)S(1)} %add_convert_fusion), channel_id=1, source_target_pairs={{0,8},{4,12},{8,0},{12,4},{16,24},{20,28},{24,16},{28,20},{1,9},{5... | collective-permute-start | bytes 245768 | tf_op jit(solution)/shard_map/ppermute | solution.py:26
  63.1 1.7 %collective-permute-done.11 = bf16[32,1280]{1,0:T(8,128)(2,1)S(1)} collective-permute-done((bf16[32,1280]{1,0:T(8,128)(2,1)S(1)}, bf16[32,1280]{1,0:T(8,128)(2,1)S(1)}, u32[]{:S(2)}, u32[]{:S(2)}) %collective-permute-start.11) | collective-permute-done | bytes 81952 | tf_op jit(solution)/shard_map/ppermute | solution.py:26
  64.9 0.2 pad_maximum_fusion.2
  65.1 1.6 %collective-permute-start.12 = (bf16[64,1280]{1,0:T(8,128)(2,1)S(1)}, bf16[64,1280]{1,0:T(8,128)(2,1)S(1)}, u32[]{:S(2)}, u32[]{:S(2)}) collective-permute-start(bf16[64,1280]{1,0:T(8,128)(2,1)S(1)} %pad_maximum_fusion.2), channel_id=1, source_target_pairs={{0,4},{4,0},{8,12},{12,8},{16,20},{20,16},{24,28},{28,24},{1,5},{5... | collective-permute-start | bytes 491528 | tf_op jit(solution)/shard_map/ppermute | solution.py:26
  66.7 0.8 collective-permute-start.18
  67.6 0.1 copy.7
  67.7 2.7 %collective-permute-done.12 = bf16[64,1280]{1,0:T(8,128)(2,1)S(1)} collective-permute-done((bf16[64,1280]{1,0:T(8,128)(2,1)S(1)}, bf16[64,1280]{1,0:T(8,128)(2,1)S(1)}, u32[]{:S(2)}, u32[]{:S(2)}) %collective-permute-start.12) | collective-permute-done | bytes 163872 | tf_op jit(solution)/shard_map/ppermute | solution.py:26
  70.5 1.8 %collective-permute-done.18 = bf16[64,1280]{1,0:T(8,128)(2,1)S(1)} collective-permute-done((bf16[64,1280]{1,0:T(8,128)(2,1)S(1)}, bf16[64,1280]{1,0:T(8,128)(2,1)S(1)}, u32[]{:S(2)}, u32[]{:S(2)}) %collective-permute-start.18) | collective-permute-done | bytes 163872 | tf_op jit(solution)/shard_map/ppermute | solution.py:26
  72.2 0.1 broadcast_select_fusion.1
  72.4 12.9 %basis_latents.1 = bf16[512,2,128]{2,1,0:T(2,128)(2,1)} custom-call(bf16[2,128,512]{2,1,0:T(8,128)(2,1)S(1)} %bitcast.2, bf16[128,1280]{1,0:T(8,128)(2,1)S(1)} %pad_maximum_fusion.refs_0_, bf16[128,1280]{1,0:T(8,128)(2,1)S(1)} %pad_maximum_fusion.1.refs_1_, bf16[512,512]{1,0:T(8,128)(2,1)} %get-tuple-element.50.refs_2_, ...), custom_call_target="tpu_custom_call" | custom-call | tf_op jit(solution)/shard_map/basis_latents/pallas_call | solution.py:366
  (27 shorter events, 0.4 us)
Async XLA Ops:
  0.0 67.6 %copy-start = (bf16[8,512,128]{2,1,0:T(8,128)(2,1)S(1)}, bf16[8,512,128]{2,1,0:T(8,128)(2,1)}, u32[]{:S(2)}) copy-start(bf16[8,512,128]{2,1,0:T(8,128)(2,1)} %param.7) | copy-start | bytes 3145732
  0.0 0.8 copy-start.1
  8.7 2.8 %collective-permute-start = (bf16[4,512,256]{2,1,0:T(8,128)(2,1)S(1)}, bf16[4,512,256]{2,1,0:T(8,128)(2,1)S(1)}, u32[]{:S(2)}, u32[]{:S(2)}) collective-permute-start(bf16[4,512,256]{2,1,0:T(8,128)(2,1)S(1)} %get-tuple-element.30), channel_id=1, source_target_pairs={{0,1},{1,0},{2,3},{3,2},{4,5},{5,4},{6,7},{7,6},{8,9},{9,8},{10,11... | collective-permute-start | bytes 3145736 | tf_op jit(solution)/shard_map/ppermute | solution.py:26
  11.7 16.1 %collective-permute-start.6 = (bf16[4,512,128]{2,1,0:T(8,128)(2,1)S(1)}, bf16[4,512,128]{2,1,0:T(8,128)(2,1)S(1)}, u32[]{:S(2)}, u32[]{:S(2)}) collective-permute-start(bf16[4,512,128]{2,1,0:T(8,128)(2,1)S(1)} %get-tuple-element.31), channel_id=1, source_target_pairs={{0,2},{1,3},{2,0},{3,1},{4,6},{5,7},{6,4},{7,5},{8,10},{9,11},{10,... | collective-permute-start | bytes 1572872 | tf_op jit(solution)/shard_map/ppermute | solution.py:26
  25.0 1.2 %collective-permute-start.1 = (f32[4,512]{1,0:T(4,128)S(1)}, f32[4,512]{1,0:T(4,128)S(1)}, u32[]{:S(2)}, u32[]{:S(2)}) collective-permute-start(f32[4,512]{1,0:T(4,128)S(1)} %get-tuple-element.33), channel_id=1, source_target_pairs={{0,1},{1,0},{2,3},{3,2},{4,5},{5,4},{6,7},{7,6},{8,9},{9,8},{10,11... | collective-permute-start | bytes 24584 | tf_op jit(solution)/shard_map/ppermute | solution.py:26
  25.0 1.7 %collective-permute-start.2 = (bf16[1,512,256]{2,1,0:T(8,128)(2,1)S(1)}, bf16[1,512,256]{2,1,0:T(8,128)(2,1)S(1)}, u32[]{:S(2)}, u32[]{:S(2)}) collective-permute-start(bf16[1,512,256]{2,1,0:T(8,128)(2,1)S(1)} %get-tuple-element.35), channel_id=1, source_target_pairs={{0,1},{1,0},{2,3},{3,2},{4,5},{5,4},{6,7},{7,6},{8,9},{9,8},{10,11... | collective-permute-start | bytes 786440 | tf_op jit(solution)/shard_map/ppermute | solution.py:26
  25.5 1.5 %collective-permute-start.3 = (bf16[1,512,256]{2,1,0:T(8,128)(2,1)S(1)}, bf16[1,512,256]{2,1,0:T(8,128)(2,1)S(1)}, u32[]{:S(2)}, u32[]{:S(2)}) collective-permute-start(bf16[1,512,256]{2,1,0:T(8,128)(2,1)S(1)} %get-tuple-element.36), channel_id=1, source_target_pairs={{0,1},{1,0},{2,3},{3,2},{4,5},{5,4},{6,7},{7,6},{8,9},{9,8},{10,11... | collective-permute-start | bytes 786440 | tf_op jit(solution)/shard_map/ppermute | solution.py:26
  25.6 1.8 %collective-permute-start.4 = (bf16[1,512,256]{2,1,0:T(8,128)(2,1)S(1)}, bf16[1,512,256]{2,1,0:T(8,128)(2,1)S(1)}, u32[]{:S(2)}, u32[]{:S(2)}) collective-permute-start(bf16[1,512,256]{2,1,0:T(8,128)(2,1)S(1)} %get-tuple-element.37), channel_id=1, source_target_pairs={{0,1},{1,0},{2,3},{3,2},{4,5},{5,4},{6,7},{7,6},{8,9},{9,8},{10,11... | collective-permute-start | bytes 786440 | tf_op jit(solution)/shard_map/ppermute | solution.py:26
  26.2 1.6 %collective-permute-start.5 = (bf16[1,512,256]{2,1,0:T(8,128)(2,1)S(1)}, bf16[1,512,256]{2,1,0:T(8,128)(2,1)S(1)}, u32[]{:S(2)}, u32[]{:S(2)}) collective-permute-start(bf16[1,512,256]{2,1,0:T(8,128)(2,1)S(1)} %get-tuple-element.38), channel_id=1, source_target_pairs={{0,1},{1,0},{2,3},{3,2},{4,5},{5,4},{6,7},{7,6},{8,9},{9,8},{10,11... | collective-permute-start | bytes 786440 | tf_op jit(solution)/shard_map/ppermute | solution.py:26
  28.1 0.7 copy-start.2
  28.8 9.7 %collective-permute-start.7 = (bf16[2,560,128]{2,1,0:T(8,128)(2,1)S(1)}, bf16[2,560,128]{2,1,0:T(8,128)(2,1)S(1)}, u32[]{:S(2)}, u32[]{:S(2)}) collective-permute-start(bf16[2,560,128]{2,1,0:T(8,128)(2,1)S(1)} %get-tuple-element.44), channel_id=1, source_target_pairs={{0,2},{1,3},{2,0},{3,1},{4,6},{5,7},{6,4},{7,5},{8,10},{9,11},{10,... | collective-permute-start | bytes 860168 | tf_op jit(solution)/shard_map/ppermute | solution.py:26
  29.6 13.9 %collective-permute-start.13 = (bf16[2,512,128]{2,1,0:T(8,128)(2,1)}, bf16[2,512,128]{2,1,0:T(8,128)(2,1)S(1)}, u32[]{:S(2)}, u32[]{:S(2)}) collective-permute-start(bf16[2,512,128]{2,1,0:T(8,128)(2,1)} %copy-done.2), channel_id=1, source_target_pairs={{0,2},{1,3},{2,0},{3,1},{4,6},{5,7},{6,4},{7,5},{8,10},{9,11},{10,... | collective-permute-start | bytes 786440 | tf_op jit(solution)/shard_map/ppermute | solution.py:26
  40.1 6.4 %collective-permute-start.8 = (bf16[64,1280]{1,0:T(8,128)(2,1)S(1)}, bf16[64,1280]{1,0:T(8,128)(2,1)S(1)}, u32[]{:S(2)}, u32[]{:S(2)}) collective-permute-start(bf16[64,1280]{1,0:T(8,128)(2,1)S(1)} %constant_dynamic-slice_fusion.1), channel_id=1, source_target_pairs={{0,4},{4,0},{8,12},{12,8},{16,20},{20,16},{24,28},{28,24},{1,5},{5... | collective-permute-start | bytes 491528 | tf_op jit(solution)/shard_map/ppermute | solution.py:26
  44.9 5.7 %collective-permute-start.14 = (bf16[64,1280]{1,0:T(8,128)(2,1)S(1)}, bf16[64,1280]{1,0:T(8,128)(2,1)S(1)}, u32[]{:S(2)}, u32[]{:S(2)}) collective-permute-start(bf16[64,1280]{1,0:T(8,128)(2,1)S(1)} %constant_dynamic-slice_fusion), channel_id=1, source_target_pairs={{0,4},{4,0},{8,12},{12,8},{16,20},{20,16},{24,28},{28,24},{1,5},{5... | collective-permute-start | bytes 491528 | tf_op jit(solution)/shard_map/ppermute | solution.py:26
  46.6 5.8 %collective-permute-start.9 = (bf16[32,1280]{1,0:T(8,128)(2,1)S(1)}, bf16[32,1280]{1,0:T(8,128)(2,1)S(1)}, u32[]{:S(2)}, u32[]{:S(2)}) collective-permute-start(bf16[32,1280]{1,0:T(8,128)(2,1)S(1)} %dynamic-slice_convert_fusion.1), channel_id=1, source_target_pairs={{0,8},{4,12},{8,0},{12,4},{16,24},{20,28},{24,16},{28,20},{1,9},{5... | collective-permute-start | bytes 245768 | tf_op jit(solution)/shard_map/ppermute | solution.py:26
  50.7 5.2 %collective-permute-start.15 = (bf16[32,1280]{1,0:T(8,128)(2,1)S(1)}, bf16[32,1280]{1,0:T(8,128)(2,1)S(1)}, u32[]{:S(2)}, u32[]{:S(2)}) collective-permute-start(bf16[32,1280]{1,0:T(8,128)(2,1)S(1)} %dynamic-slice_convert_fusion), channel_id=1, source_target_pairs={{0,8},{4,12},{8,0},{12,4},{16,24},{20,28},{24,16},{28,20},{1,9},{5... | collective-permute-start | bytes 245768 | tf_op jit(solution)/shard_map/ppermute | solution.py:26
  52.4 7.9 %collective-permute-start.10 = (bf16[32,1280]{1,0:T(8,128)(2,1)S(1)}, bf16[32,1280]{1,0:T(8,128)(2,1)S(1)}, u32[]{:S(2)}, u32[]{:S(2)}) collective-permute-start(bf16[32,1280]{1,0:T(8,128)(2,1)S(1)} %add_convert_fusion.3), channel_id=1, source_target_pairs={{0,16},{4,20},{8,24},{12,28},{16,0},{20,4},{24,8},{28,12},{1,17},{... | collective-permute-start | bytes 245768 | tf_op jit(solution)/shard_map/ppermute | solution.py:26
  55.9 5.5 %collective-permute-start.16 = (bf16[32,1280]{1,0:T(8,128)(2,1)S(1)}, bf16[32,1280]{1,0:T(8,128)(2,1)S(1)}, u32[]{:S(2)}, u32[]{:S(2)}) collective-permute-start(bf16[32,1280]{1,0:T(8,128)(2,1)S(1)} %add_convert_fusion.1), channel_id=1, source_target_pairs={{0,16},{4,20},{8,24},{12,28},{16,0},{20,4},{24,8},{28,12},{1,17},{... | collective-permute-start | bytes 245768 | tf_op jit(solution)/shard_map/ppermute | solution.py:26
  60.4 4.5 %collective-permute-start.11 = (bf16[32,1280]{1,0:T(8,128)(2,1)S(1)}, bf16[32,1280]{1,0:T(8,128)(2,1)S(1)}, u32[]{:S(2)}, u32[]{:S(2)}) collective-permute-start(bf16[32,1280]{1,0:T(8,128)(2,1)S(1)} %add_convert_fusion.2), channel_id=1, source_target_pairs={{0,8},{4,12},{8,0},{12,4},{16,24},{20,28},{24,16},{28,20},{1,9},{5... | collective-permute-start | bytes 245768 | tf_op jit(solution)/shard_map/ppermute | solution.py:26
  61.4 5.3 %collective-permute-start.17 = (bf16[32,1280]{1,0:T(8,128)(2,1)S(1)}, bf16[32,1280]{1,0:T(8,128)(2,1)S(1)}, u32[]{:S(2)}, u32[]{:S(2)}) collective-permute-start(bf16[32,1280]{1,0:T(8,128)(2,1)S(1)} %add_convert_fusion), channel_id=1, source_target_pairs={{0,8},{4,12},{8,0},{12,4},{16,24},{20,28},{24,16},{28,20},{1,9},{5... | collective-permute-start | bytes 245768 | tf_op jit(solution)/shard_map/ppermute | solution.py:26
  65.1 5.4 %collective-permute-start.12 = (bf16[64,1280]{1,0:T(8,128)(2,1)S(1)}, bf16[64,1280]{1,0:T(8,128)(2,1)S(1)}, u32[]{:S(2)}, u32[]{:S(2)}) collective-permute-start(bf16[64,1280]{1,0:T(8,128)(2,1)S(1)} %pad_maximum_fusion.2), channel_id=1, source_target_pairs={{0,4},{4,0},{8,12},{12,8},{16,20},{20,16},{24,28},{28,24},{1,5},{5... | collective-permute-start | bytes 491528 | tf_op jit(solution)/shard_map/ppermute | solution.py:26
  66.7 5.5 %collective-permute-start.18 = (bf16[64,1280]{1,0:T(8,128)(2,1)S(1)}, bf16[64,1280]{1,0:T(8,128)(2,1)S(1)}, u32[]{:S(2)}, u32[]{:S(2)}) collective-permute-start(bf16[64,1280]{1,0:T(8,128)(2,1)S(1)} %pad_maximum_fusion.3), channel_id=1, source_target_pairs={{0,4},{4,0},{8,12},{12,8},{16,20},{20,16},{24,28},{28,24},{1,5},{5... | collective-permute-start | bytes 491528 | tf_op jit(solution)/shard_map/ppermute | solution.py:26

commit v5 on v4

--- a/solution.py
+++ b/solution.py
@@ -53,26 +53,25 @@
         copies[layer][0].wait()
         rows = rows_ref[layer]
         scaled = rows * gains[layer : layer + 1]
+        if with_squares:
+            wide = rows.astype(F32)
+            squares = None
+            for i in range(width // HD):
+                x = wide[:, i * HD : (i + 1) * HD]
+                squares = x * x if squares is None else squares + x * x
+            refs[1 + len(cuts)][layer : layer + 1, :] = lax.dot_general(
+                jnp.ones((8, HD), F32),
+                squares,
+                (((1,), (1,)), ((), ())),
+                precision=HIGHEST,
+                preferred_element_type=F32,
+            )[:1]
         for copy in copies[layer][1:]:
             copy.wait()
         total = jnp.dot(scaled, cols_ref[layer], preferred_element_type=F32)
         refs[0][layer] = total[:, :half].astype(BF16)
         ref, i = send[layer]
         ref[i] = total[:, half:].astype(BF16)
-        if not with_squares:
-            continue
-        wide = rows.astype(F32)
-        squares = None
-        for i in range(width // HD):
-            x = wide[:, i * HD : (i + 1) * HD]
-            squares = x * x if squares is None else squares + x * x
-        refs[1 + len(cuts)][layer : layer + 1, :] = lax.dot_general(
-            jnp.ones((8, HD), F32),
-            squares,
-            (((1,), (1,)), ((), ())),
-            precision=HIGHEST,
-            preferred_element_type=F32,
-        )[:1]
 
 
 def partial_products(hidden, gains, weights, me, own, slot, cuts, with_squares):

time: 85.8 us -> 85.4 us (level)
  no operation moved by 1% of the time
where the time goes in v5:
time: 85.4 us; the launch traced here: 85.1 us
  Pallas kernels  34.1 us (40%)
  waiting for transfers between devices  26.1 us (31%)
  starting transfers between devices  22.4 us (26%)
  local copies, waits for them, and re-layouts  1.75 us (2%)
    ppermute x19, waiting for transfers between devices, exchange(): return lax.ppermute(x, axis, [(j, j ^ bit) for j in range(size)])  26.1 us
    ppermute x19, starting transfers between devices, exchange(): return lax.ppermute(x, axis, [(j, j ^ bit) for j in range(size)])  22.4 us
    pallas_call x2, Pallas kernels, partial_products(): pl.pallas_call(functools.partial(partial_kernel, own, slot, cuts, with_sq...  17.8 us
    pallas_call x1, Pallas kernels, latents_of(): pl.pallas_call(functools.partial(basis_kernel, own, layers, chains), out_...  12.9 us
    pallas_call x2, Pallas kernels, stacked_and_gram(): pl.pallas_call(functools.partial(gram_kernel, spans, width), out_shape=ou...  2.87 us
  transfers between devices with their start and end apart: 19, of which 15 were waited for; matrix products, arithmetic and copies ran while one was open for 1% of the time, Pallas kernels for 15%

profile of v5, /device:TPU:0, one launch (start us, length us, event | category | flops | bytes accessed | tf_op | source)
XLA Modules:
  0.0 85.1 jit_solution(16161320825363141272)
XLA Ops:
  0.0 0.8 copy-done.1
  0.8 7.9 %partial_products.2 = (bf16[4,512,256]{2,1,0:T(8,128)(2,1)S(1)}, bf16[4,512,256]{2,1,0:T(8,128)(2,1)S(1)}) custom-call(s32[1]{0:T(128)} %bitcast.1.m_ref, bf16[4,2048]{1,0:T(4,128)(2,1)S(1)} %copy-done.1, bf16[4,512,2048]{2,1,0:T(8,128)(2,1)} %hid_ref.3, bf16[4,2048,1024]{2,1,0:T(8,128)(2,1)} %w_ref.3), custom_call_target="tpu_custom_call" | custom-call | flops 4294967296 | bytes 16777216 | tf_op jit(solution)/shard_map/partial_products/pallas_call | solution.py:85
  8.7 0.5 collective-permute-start
  9.2 2.3 %collective-permute-done.refs_1_ = bf16[4,512,256]{2,1,0:T(8,128)(2,1)S(1)} collective-permute-done((bf16[4,512,256]{2,1,0:T(8,128)(2,1)S(1)}, bf16[4,512,256]{2,1,0:T(8,128)(2,1)S(1)}, u32[]{:S(2)}, u32[]{:S(2)}) %collective-permute-start) | collective-permute-done | bytes 1048608 | tf_op jit(solution)/shard_map/ppermute | solution.py:26
  11.5 0.3 next_send.2
  11.7 2.9 %collective-permute-start.6 = (bf16[4,512,128]{2,1,0:T(8,128)(2,1)S(1)}, bf16[4,512,128]{2,1,0:T(8,128)(2,1)S(1)}, u32[]{:S(2)}, u32[]{:S(2)}) collective-permute-start(bf16[4,512,128]{2,1,0:T(8,128)(2,1)S(1)} %get-tuple-element.31), channel_id=1, source_target_pairs={{0,2},{1,3},{2,0},{3,1},{4,6},{5,7},{6,4},{7,5},{8,10},{9,11},{10,... | collective-permute-start | bytes 1572872 | tf_op jit(solution)/shard_map/ppermute | solution.py:26
  14.7 9.9 %partial_products.3 = (bf16[4,512,256]{2,1,0:T(8,128)(2,1)S(1)}, bf16[1,512,256]{2,1,0:T(8,128)(2,1)S(1)}, bf16[1,512,256]{2,1,0:T(8,128)(2,1)S(1)}, bf16[1,512,...) custom-call(s32[1]{0:T(128)} %bitcast.1.m_ref, bf16[4,2048]{1,0:T(4,128)(2,1)S(1)} %copy-done.1, ...), custom_call_target="tpu_custom_call" | custom-call | flops 4294967296 | bytes 16777216 | tf_op jit(solution)/shard_map/partial_products/pallas_call | solution.py:85
  24.6 0.1 collective-permute-start.1
  24.7 0.5 collective-permute-start.2
  25.2 0.1 collective-permute-start.3
  25.2 0.4 collective-permute-start.4
  25.7 0.2 collective-permute-done.1
  25.8 0.2 collective-permute-start.5
  26.0 0.3 collective-permute-done.2.refs_1_
  26.3 0.4 collective-permute-done.3.refs_2_
  26.7 0.4 collective-permute-done.4.refs_3_
  27.1 0.4 collective-permute-done.5.refs_4_
  27.5 0.0 collective-permute-done.6.refs_1_
  27.5 0.3 next_send.3
  27.7 0.0 copy-start.2
  27.8 0.7 copy-done.2
  28.4 1.2 %collective-permute-start.7 = (bf16[2,560,128]{2,1,0:T(8,128)(2,1)S(1)}, bf16[2,560,128]{2,1,0:T(8,128)(2,1)S(1)}, u32[]{:S(2)}, u32[]{:S(2)}) collective-permute-start(bf16[2,560,128]{2,1,0:T(8,128)(2,1)S(1)} %get-tuple-element.44), channel_id=1, source_target_pairs={{0,2},{1,3},{2,0},{3,1},{4,6},{5,7},{6,4},{7,5},{8,10},{9,11},{10,... | collective-permute-start | bytes 860168 | tf_op jit(solution)/shard_map/ppermute | solution.py:26
  29.6 0.9 %collective-permute-start.13 = (bf16[2,512,128]{2,1,0:T(8,128)(2,1)}, bf16[2,512,128]{2,1,0:T(8,128)(2,1)S(1)}, u32[]{:S(2)}, u32[]{:S(2)}) collective-permute-start(bf16[2,512,128]{2,1,0:T(8,128)(2,1)} %copy-done.2), channel_id=1, source_target_pairs={{0,2},{1,3},{2,0},{3,1},{4,6},{5,7},{6,4},{7,5},{8,10},{9,11},{10,... | collective-permute-start | bytes 786440 | tf_op jit(solution)/shard_map/ppermute | solution.py:26
  30.5 7.6 %collective-permute-done.7.refs_1_ = bf16[2,560,128]{2,1,0:T(8,128)(2,1)S(1)} collective-permute-done((bf16[2,560,128]{2,1,0:T(8,128)(2,1)S(1)}, bf16[2,560,128]{2,1,0:T(8,128)(2,1)S(1)}, u32[]{:S(2)}, u32[]{:S(2)}) %collective-permute-start.7) | collective-permute-done | bytes 286752 | tf_op jit(solution)/shard_map/ppermute | solution.py:26
  38.2 1.5 %stacked_gram.2 = (bf16[512,512]{1,0:T(8,128)(2,1)}, bf16[128,1280]{1,0:T(8,128)(2,1)S(1)}) custom-call(f32[4,512]{1,0:T(4,128)S(1)} %add.43.squares_ref, bf16[4,512,128]{2,1,0:T(8,128)(2,1)S(1)} %get-tuple-element.45.refs_0_, bf16[4,512,128]{2,1,0:T(8,128)(2,1)S(1)} %collective-permute-done.6.refs_1_), custom_call_target="tpu_custom_call" | custom-call | tf_op jit(solution)/shard_map/stacked_gram/pallas_call | solution.py:202
  39.7 1.6 %collective-permute-start.8 = (bf16[64,1280]{1,0:T(8,128)(2,1)S(1)}, bf16[64,1280]{1,0:T(8,128)(2,1)S(1)}, u32[]{:S(2)}, u32[]{:S(2)}) collective-permute-start(bf16[64,1280]{1,0:T(8,128)(2,1)S(1)} %constant_dynamic-slice_fusion.1), channel_id=1, source_target_pairs={{0,4},{4,0},{8,12},{12,8},{16,20},{20,16},{24,28},{28,24},{1,5},{5... | collective-permute-start | bytes 491528 | tf_op jit(solution)/shard_map/ppermute | solution.py:26
  41.3 1.9 %collective-permute-done.13.refs_3_ = bf16[2,512,128]{2,1,0:T(8,128)(2,1)S(1)} collective-permute-done((bf16[2,512,128]{2,1,0:T(8,128)(2,1)}, bf16[2,512,128]{2,1,0:T(8,128)(2,1)S(1)}, u32[]{:S(2)}, u32[]{:S(2)}) %collective-permute-start.13) | collective-permute-done | bytes 262176 | tf_op jit(solution)/shard_map/ppermute | solution.py:26
  43.2 1.4 %stacked_gram.3 = (bf16[512,256]{1,0:T(8,128)(2,1)}, bf16[512,256]{1,0:T(8,128)(2,1)}, bf16[128,1280]{1,0:T(8,128)(2,1)S(1)}) custom-call(f32[4,512]{1,0:T(4,128)S(1)} %add.43.squares_ref, bf16[4,512,128]{2,1,0:T(8,128)(2,1)S(1)} %get-tuple-element.47.refs_0_.refs_2_, bf16[2,560,128]{2,1,0:T(8,128)(2,1)S(1)} %collective-permute-done.7.refs_1_, ...), custom_call_target="tpu_custom_call" | custom-call | tf_op jit(solution)/shard_map/stacked_gram/pallas_call | solution.py:202
  44.6 1.6 %collective-permute-start.14 = (bf16[64,1280]{1,0:T(8,128)(2,1)S(1)}, bf16[64,1280]{1,0:T(8,128)(2,1)S(1)}, u32[]{:S(2)}, u32[]{:S(2)}) collective-permute-start(bf16[64,1280]{1,0:T(8,128)(2,1)S(1)} %constant_dynamic-slice_fusion), channel_id=1, source_target_pairs={{0,4},{4,0},{8,12},{12,8},{16,20},{20,16},{24,28},{28,24},{1,5},{5... | collective-permute-start | bytes 491528 | tf_op jit(solution)/shard_map/ppermute | solution.py:26
  46.2 0.0 collective-permute-done.8
  46.2 1.6 %collective-permute-start.9 = (bf16[32,1280]{1,0:T(8,128)(2,1)S(1)}, bf16[32,1280]{1,0:T(8,128)(2,1)S(1)}, u32[]{:S(2)}, u32[]{:S(2)}) collective-permute-start(bf16[32,1280]{1,0:T(8,128)(2,1)S(1)} %dynamic-slice_convert_fusion.1), channel_id=1, source_target_pairs={{0,8},{4,12},{8,0},{12,4},{16,24},{20,28},{24,16},{28,20},{1,9},{5... | collective-permute-start | bytes 245768 | tf_op jit(solution)/shard_map/ppermute | solution.py:26
  47.9 2.4 %collective-permute-done.14 = bf16[64,1280]{1,0:T(8,128)(2,1)S(1)} collective-permute-done((bf16[64,1280]{1,0:T(8,128)(2,1)S(1)}, bf16[64,1280]{1,0:T(8,128)(2,1)S(1)}, u32[]{:S(2)}, u32[]{:S(2)}) %collective-permute-start.14) | collective-permute-done | bytes 163872 | tf_op jit(solution)/shard_map/ppermute | solution.py:26
  50.3 1.7 %collective-permute-start.15 = (bf16[32,1280]{1,0:T(8,128)(2,1)S(1)}, bf16[32,1280]{1,0:T(8,128)(2,1)S(1)}, u32[]{:S(2)}, u32[]{:S(2)}) collective-permute-start(bf16[32,1280]{1,0:T(8,128)(2,1)S(1)} %dynamic-slice_convert_fusion), channel_id=1, source_target_pairs={{0,8},{4,12},{8,0},{12,4},{16,24},{20,28},{24,16},{28,20},{1,9},{5... | collective-permute-start | bytes 245768 | tf_op jit(solution)/shard_map/ppermute | solution.py:26
  52.0 2.7 %collective-permute-start.10 = (bf16[32,1280]{1,0:T(8,128)(2,1)S(1)}, bf16[32,1280]{1,0:T(8,128)(2,1)S(1)}, u32[]{:S(2)}, u32[]{:S(2)}) collective-permute-start(bf16[32,1280]{1,0:T(8,128)(2,1)S(1)} %add_convert_fusion.3), channel_id=1, source_target_pairs={{0,16},{4,20},{8,24},{12,28},{16,0},{20,4},{24,8},{28,12},{1,17},{... | collective-permute-start | bytes 245768 | tf_op jit(solution)/shard_map/ppermute | solution.py:26
  54.7 0.9 %collective-permute-done.15 = bf16[32,1280]{1,0:T(8,128)(2,1)S(1)} collective-permute-done((bf16[32,1280]{1,0:T(8,128)(2,1)S(1)}, bf16[32,1280]{1,0:T(8,128)(2,1)S(1)}, u32[]{:S(2)}, u32[]{:S(2)}) %collective-permute-start.15) | collective-permute-done | bytes 81952 | tf_op jit(solution)/shard_map/ppermute | solution.py:26
  55.6 2.2 %collective-permute-start.16 = (bf16[32,1280]{1,0:T(8,128)(2,1)S(1)}, bf16[32,1280]{1,0:T(8,128)(2,1)S(1)}, u32[]{:S(2)}, u32[]{:S(2)}) collective-permute-start(bf16[32,1280]{1,0:T(8,128)(2,1)S(1)} %add_convert_fusion.1), channel_id=1, source_target_pairs={{0,16},{4,20},{8,24},{12,28},{16,0},{20,4},{24,8},{28,12},{1,17},{... | collective-permute-start | bytes 245768 | tf_op jit(solution)/shard_map/ppermute | solution.py:26
  57.7 2.4 %collective-permute-done.10 = bf16[32,1280]{1,0:T(8,128)(2,1)S(1)} collective-permute-done((bf16[32,1280]{1,0:T(8,128)(2,1)S(1)}, bf16[32,1280]{1,0:T(8,128)(2,1)S(1)}, u32[]{:S(2)}, u32[]{:S(2)}) %collective-permute-start.10) | collective-permute-done | bytes 81952 | tf_op jit(solution)/shard_map/ppermute | solution.py:26
  60.2 0.1 collective-permute-start.11
  60.3 1.0 %collective-permute-done.16 = bf16[32,1280]{1,0:T(8,128)(2,1)S(1)} collective-permute-done((bf16[32,1280]{1,0:T(8,128)(2,1)S(1)}, bf16[32,1280]{1,0:T(8,128)(2,1)S(1)}, u32[]{:S(2)}, u32[]{:S(2)}) %collective-permute-start.16) | collective-permute-done | bytes 81952 | tf_op jit(solution)/shard_map/ppermute | solution.py:26
  61.3 1.7 %collective-permute-start.17 = (bf16[32,1280]{1,0:T(8,128)(2,1)S(1)}, bf16[32,1280]{1,0:T(8,128)(2,1)S(1)}, u32[]{:S(2)}, u32[]{:S(2)}) collective-permute-start(bf16[32,1280]{1,0:T(8,128)(2,1)S(1)} %add_convert_fusion), channel_id=1, source_target_pairs={{0,8},{4,12},{8,0},{12,4},{16,24},{20,28},{24,16},{28,20},{1,9},{5... | collective-permute-start | bytes 245768 | tf_op jit(solution)/shard_map/ppermute | solution.py:26
  62.9 1.7 %collective-permute-done.11 = bf16[32,1280]{1,0:T(8,128)(2,1)S(1)} collective-permute-done((bf16[32,1280]{1,0:T(8,128)(2,1)S(1)}, bf16[32,1280]{1,0:T(8,128)(2,1)S(1)}, u32[]{:S(2)}, u32[]{:S(2)}) %collective-permute-start.11) | collective-permute-done | bytes 81952 | tf_op jit(solution)/shard_map/ppermute | solution.py:26
  64.7 1.6 %collective-permute-start.12 = (bf16[64,1280]{1,0:T(8,128)(2,1)S(1)}, bf16[64,1280]{1,0:T(8,128)(2,1)S(1)}, u32[]{:S(2)}, u32[]{:S(2)}) collective-permute-start(bf16[64,1280]{1,0:T(8,128)(2,1)S(1)} %pad_maximum_fusion.2), channel_id=1, source_target_pairs={{0,4},{4,0},{8,12},{12,8},{16,20},{20,16},{24,28},{28,24},{1,5},{5... | collective-permute-start | bytes 491528 | tf_op jit(solution)/shard_map/ppermute | solution.py:26
  66.4 1.0 %collective-permute-start.18 = (bf16[64,1280]{1,0:T(8,128)(2,1)S(1)}, bf16[64,1280]{1,0:T(8,128)(2,1)S(1)}, u32[]{:S(2)}, u32[]{:S(2)}) collective-permute-start(bf16[64,1280]{1,0:T(8,128)(2,1)S(1)} %pad_maximum_fusion.3), channel_id=1, source_target_pairs={{0,4},{4,0},{8,12},{12,8},{16,20},{20,16},{24,28},{28,24},{1,5},{5... | collective-permute-start | bytes 491528 | tf_op jit(solution)/shard_map/ppermute | solution.py:26
  67.4 0.1 copy.7
  67.6 2.6 %collective-permute-done.12 = bf16[64,1280]{1,0:T(8,128)(2,1)S(1)} collective-permute-done((bf16[64,1280]{1,0:T(8,128)(2,1)S(1)}, bf16[64,1280]{1,0:T(8,128)(2,1)S(1)}, u32[]{:S(2)}, u32[]{:S(2)}) %collective-permute-start.12) | collective-permute-done | bytes 163872 | tf_op jit(solution)/shard_map/ppermute | solution.py:26
  70.1 1.8 %collective-permute-done.18 = bf16[64,1280]{1,0:T(8,128)(2,1)S(1)} collective-permute-done((bf16[64,1280]{1,0:T(8,128)(2,1)S(1)}, bf16[64,1280]{1,0:T(8,128)(2,1)S(1)}, u32[]{:S(2)}, u32[]{:S(2)}) %collective-permute-start.18) | collective-permute-done | bytes 163872 | tf_op jit(solution)/shard_map/ppermute | solution.py:26
  71.9 0.1 broadcast_select_fusion.1
  72.0 12.9 %basis_latents.1 = bf16[512,2,128]{2,1,0:T(2,128)(2,1)} custom-call(bf16[2,128,512]{2,1,0:T(8,128)(2,1)S(1)} %bitcast.2, bf16[128,1280]{1,0:T(8,128)(2,1)S(1)} %pad_maximum_fusion.refs_0_, bf16[128,1280]{1,0:T(8,128)(2,1)S(1)} %pad_maximum_fusion.1.refs_1_, bf16[512,512]{1,0:T(8,128)(2,1)} %get-tuple-element.50.refs_2_, ...), custom_call_target="tpu_custom_call" | custom-call | tf_op jit(solution)/shard_map/basis_latents/pallas_call | solution.py:365
  (27 shorter events, 0.4 us)
Async XLA Ops:
  0.0 67.4 %copy-start = (bf16[8,512,128]{2,1,0:T(8,128)(2,1)S(1)}, bf16[8,512,128]{2,1,0:T(8,128)(2,1)}, u32[]{:S(2)}) copy-start(bf16[8,512,128]{2,1,0:T(8,128)(2,1)} %param.7) | copy-start | bytes 3145732
  0.0 0.8 copy-start.1
  8.7 2.8 %collective-permute-start = (bf16[4,512,256]{2,1,0:T(8,128)(2,1)S(1)}, bf16[4,512,256]{2,1,0:T(8,128)(2,1)S(1)}, u32[]{:S(2)}, u32[]{:S(2)}) collective-permute-start(bf16[4,512,256]{2,1,0:T(8,128)(2,1)S(1)} %get-tuple-element.30), channel_id=1, source_target_pairs={{0,1},{1,0},{2,3},{3,2},{4,5},{5,4},{6,7},{7,6},{8,9},{9,8},{10,11... | collective-permute-start | bytes 3145736 | tf_op jit(solution)/shard_map/ppermute | solution.py:26
  11.7 15.7 %collective-permute-start.6 = (bf16[4,512,128]{2,1,0:T(8,128)(2,1)S(1)}, bf16[4,512,128]{2,1,0:T(8,128)(2,1)S(1)}, u32[]{:S(2)}, u32[]{:S(2)}) collective-permute-start(bf16[4,512,128]{2,1,0:T(8,128)(2,1)S(1)} %get-tuple-element.31), channel_id=1, source_target_pairs={{0,2},{1,3},{2,0},{3,1},{4,6},{5,7},{6,4},{7,5},{8,10},{9,11},{10,... | collective-permute-start | bytes 1572872 | tf_op jit(solution)/shard_map/ppermute | solution.py:26
  24.6 1.2 %collective-permute-start.1 = (f32[4,512]{1,0:T(4,128)S(1)}, f32[4,512]{1,0:T(4,128)S(1)}, u32[]{:S(2)}, u32[]{:S(2)}) collective-permute-start(f32[4,512]{1,0:T(4,128)S(1)} %get-tuple-element.33), channel_id=1, source_target_pairs={{0,1},{1,0},{2,3},{3,2},{4,5},{5,4},{6,7},{7,6},{8,9},{9,8},{10,11... | collective-permute-start | bytes 24584 | tf_op jit(solution)/shard_map/ppermute | solution.py:26
  24.7 1.7 %collective-permute-start.2 = (bf16[1,512,256]{2,1,0:T(8,128)(2,1)S(1)}, bf16[1,512,256]{2,1,0:T(8,128)(2,1)S(1)}, u32[]{:S(2)}, u32[]{:S(2)}) collective-permute-start(bf16[1,512,256]{2,1,0:T(8,128)(2,1)S(1)} %get-tuple-element.35), channel_id=1, source_target_pairs={{0,1},{1,0},{2,3},{3,2},{4,5},{5,4},{6,7},{7,6},{8,9},{9,8},{10,11... | collective-permute-start | bytes 786440 | tf_op jit(solution)/shard_map/ppermute | solution.py:26
  25.2 1.5 %collective-permute-start.3 = (bf16[1,512,256]{2,1,0:T(8,128)(2,1)S(1)}, bf16[1,512,256]{2,1,0:T(8,128)(2,1)S(1)}, u32[]{:S(2)}, u32[]{:S(2)}) collective-permute-start(bf16[1,512,256]{2,1,0:T(8,128)(2,1)S(1)} %get-tuple-element.36), channel_id=1, source_target_pairs={{0,1},{1,0},{2,3},{3,2},{4,5},{5,4},{6,7},{7,6},{8,9},{9,8},{10,11... | collective-permute-start | bytes 786440 | tf_op jit(solution)/shard_map/ppermute | solution.py:26
  25.2 1.8 %collective-permute-start.4 = (bf16[1,512,256]{2,1,0:T(8,128)(2,1)S(1)}, bf16[1,512,256]{2,1,0:T(8,128)(2,1)S(1)}, u32[]{:S(2)}, u32[]{:S(2)}) collective-permute-start(bf16[1,512,256]{2,1,0:T(8,128)(2,1)S(1)} %get-tuple-element.37), channel_id=1, source_target_pairs={{0,1},{1,0},{2,3},{3,2},{4,5},{5,4},{6,7},{7,6},{8,9},{9,8},{10,11... | collective-permute-start | bytes 786440 | tf_op jit(solution)/shard_map/ppermute | solution.py:26
  25.8 1.6 %collective-permute-start.5 = (bf16[1,512,256]{2,1,0:T(8,128)(2,1)S(1)}, bf16[1,512,256]{2,1,0:T(8,128)(2,1)S(1)}, u32[]{:S(2)}, u32[]{:S(2)}) collective-permute-start(bf16[1,512,256]{2,1,0:T(8,128)(2,1)S(1)} %get-tuple-element.38), channel_id=1, source_target_pairs={{0,1},{1,0},{2,3},{3,2},{4,5},{5,4},{6,7},{7,6},{8,9},{9,8},{10,11... | collective-permute-start | bytes 786440 | tf_op jit(solution)/shard_map/ppermute | solution.py:26
  27.7 0.7 copy-start.2
  28.4 9.7 %collective-permute-start.7 = (bf16[2,560,128]{2,1,0:T(8,128)(2,1)S(1)}, bf16[2,560,128]{2,1,0:T(8,128)(2,1)S(1)}, u32[]{:S(2)}, u32[]{:S(2)}) collective-permute-start(bf16[2,560,128]{2,1,0:T(8,128)(2,1)S(1)} %get-tuple-element.44), channel_id=1, source_target_pairs={{0,2},{1,3},{2,0},{3,1},{4,6},{5,7},{6,4},{7,5},{8,10},{9,11},{10,... | collective-permute-start | bytes 860168 | tf_op jit(solution)/shard_map/ppermute | solution.py:26
  29.6 13.6 %collective-permute-start.13 = (bf16[2,512,128]{2,1,0:T(8,128)(2,1)}, bf16[2,512,128]{2,1,0:T(8,128)(2,1)S(1)}, u32[]{:S(2)}, u32[]{:S(2)}) collective-permute-start(bf16[2,512,128]{2,1,0:T(8,128)(2,1)} %copy-done.2), channel_id=1, source_target_pairs={{0,2},{1,3},{2,0},{3,1},{4,6},{5,7},{6,4},{7,5},{8,10},{9,11},{10,... | collective-permute-start | bytes 786440 | tf_op jit(solution)/shard_map/ppermute | solution.py:26
  39.7 6.4 %collective-permute-start.8 = (bf16[64,1280]{1,0:T(8,128)(2,1)S(1)}, bf16[64,1280]{1,0:T(8,128)(2,1)S(1)}, u32[]{:S(2)}, u32[]{:S(2)}) collective-permute-start(bf16[64,1280]{1,0:T(8,128)(2,1)S(1)} %constant_dynamic-slice_fusion.1), channel_id=1, source_target_pairs={{0,4},{4,0},{8,12},{12,8},{16,20},{20,16},{24,28},{28,24},{1,5},{5... | collective-permute-start | bytes 491528 | tf_op jit(solution)/shard_map/ppermute | solution.py:26
  44.6 5.7 %collective-permute-start.14 = (bf16[64,1280]{1,0:T(8,128)(2,1)S(1)}, bf16[64,1280]{1,0:T(8,128)(2,1)S(1)}, u32[]{:S(2)}, u32[]{:S(2)}) collective-permute-start(bf16[64,1280]{1,0:T(8,128)(2,1)S(1)} %constant_dynamic-slice_fusion), channel_id=1, source_target_pairs={{0,4},{4,0},{8,12},{12,8},{16,20},{20,16},{24,28},{28,24},{1,5},{5... | collective-permute-start | bytes 491528 | tf_op jit(solution)/shard_map/ppermute | solution.py:26
  46.2 5.8 %collective-permute-start.9 = (bf16[32,1280]{1,0:T(8,128)(2,1)S(1)}, bf16[32,1280]{1,0:T(8,128)(2,1)S(1)}, u32[]{:S(2)}, u32[]{:S(2)}) collective-permute-start(bf16[32,1280]{1,0:T(8,128)(2,1)S(1)} %dynamic-slice_convert_fusion.1), channel_id=1, source_target_pairs={{0,8},{4,12},{8,0},{12,4},{16,24},{20,28},{24,16},{28,20},{1,9},{5... | collective-permute-start | bytes 245768 | tf_op jit(solution)/shard_map/ppermute | solution.py:26
  50.3 5.2 %collective-permute-start.15 = (bf16[32,1280]{1,0:T(8,128)(2,1)S(1)}, bf16[32,1280]{1,0:T(8,128)(2,1)S(1)}, u32[]{:S(2)}, u32[]{:S(2)}) collective-permute-start(bf16[32,1280]{1,0:T(8,128)(2,1)S(1)} %dynamic-slice_convert_fusion), channel_id=1, source_target_pairs={{0,8},{4,12},{8,0},{12,4},{16,24},{20,28},{24,16},{28,20},{1,9},{5... | collective-permute-start | bytes 245768 | tf_op jit(solution)/shard_map/ppermute | solution.py:26
  52.0 8.1 %collective-permute-start.10 = (bf16[32,1280]{1,0:T(8,128)(2,1)S(1)}, bf16[32,1280]{1,0:T(8,128)(2,1)S(1)}, u32[]{:S(2)}, u32[]{:S(2)}) collective-permute-start(bf16[32,1280]{1,0:T(8,128)(2,1)S(1)} %add_convert_fusion.3), channel_id=1, source_target_pairs={{0,16},{4,20},{8,24},{12,28},{16,0},{20,4},{24,8},{28,12},{1,17},{... | collective-permute-start | bytes 245768 | tf_op jit(solution)/shard_map/ppermute | solution.py:26
  55.6 5.6 %collective-permute-start.16 = (bf16[32,1280]{1,0:T(8,128)(2,1)S(1)}, bf16[32,1280]{1,0:T(8,128)(2,1)S(1)}, u32[]{:S(2)}, u32[]{:S(2)}) collective-permute-start(bf16[32,1280]{1,0:T(8,128)(2,1)S(1)} %add_convert_fusion.1), channel_id=1, source_target_pairs={{0,16},{4,20},{8,24},{12,28},{16,0},{20,4},{24,8},{28,12},{1,17},{... | collective-permute-start | bytes 245768 | tf_op jit(solution)/shard_map/ppermute | solution.py:26
  60.2 4.5 %collective-permute-start.11 = (bf16[32,1280]{1,0:T(8,128)(2,1)S(1)}, bf16[32,1280]{1,0:T(8,128)(2,1)S(1)}, u32[]{:S(2)}, u32[]{:S(2)}) collective-permute-start(bf16[32,1280]{1,0:T(8,128)(2,1)S(1)} %add_convert_fusion.2), channel_id=1, source_target_pairs={{0,8},{4,12},{8,0},{12,4},{16,24},{20,28},{24,16},{28,20},{1,9},{5... | collective-permute-start | bytes 245768 | tf_op jit(solution)/shard_map/ppermute | solution.py:26
  61.3 5.1 %collective-permute-start.17 = (bf16[32,1280]{1,0:T(8,128)(2,1)S(1)}, bf16[32,1280]{1,0:T(8,128)(2,1)S(1)}, u32[]{:S(2)}, u32[]{:S(2)}) collective-permute-start(bf16[32,1280]{1,0:T(8,128)(2,1)S(1)} %add_convert_fusion), channel_id=1, source_target_pairs={{0,8},{4,12},{8,0},{12,4},{16,24},{20,28},{24,16},{28,20},{1,9},{5... | collective-permute-start | bytes 245768 | tf_op jit(solution)/shard_map/ppermute | solution.py:26
  64.7 5.4 %collective-permute-start.12 = (bf16[64,1280]{1,0:T(8,128)(2,1)S(1)}, bf16[64,1280]{1,0:T(8,128)(2,1)S(1)}, u32[]{:S(2)}, u32[]{:S(2)}) collective-permute-start(bf16[64,1280]{1,0:T(8,128)(2,1)S(1)} %pad_maximum_fusion.2), channel_id=1, source_target_pairs={{0,4},{4,0},{8,12},{12,8},{16,20},{20,16},{24,28},{28,24},{1,5},{5... | collective-permute-start | bytes 491528 | tf_op jit(solution)/shard_map/ppermute | solution.py:26
  66.4 5.5 %collective-permute-start.18 = (bf16[64,1280]{1,0:T(8,128)(2,1)S(1)}, bf16[64,1280]{1,0:T(8,128)(2,1)S(1)}, u32[]{:S(2)}, u32[]{:S(2)}) collective-permute-start(bf16[64,1280]{1,0:T(8,128)(2,1)S(1)} %pad_maximum_fusion.3), channel_id=1, source_target_pairs={{0,4},{4,0},{8,12},{12,8},{16,20},{20,16},{24,28},{28,24},{1,5},{5... | collective-permute-start | bytes 491528 | tf_op jit(solution)/shard_map/ppermute | solution.py:26
